TPU v7x, 32 devices: a whole 2x2x4 slice. The times are simulated.
32 devices in a mesh: segment: 4 (over x, core), vert: 8 (over z, y).
Axes of the slice: x: 2, y: 2, z: 4, core: 2. Of those that a mesh axis runs over, the one named last changes fastest.
Arguments:
- init_feats: bfloat16 [4, 2048, 1024], P(None, 'vert'), may hold values from -6 to 6
- layer_weight: bfloat16 [4, 1024, 1024], P('segment'), may hold values from -0.1875 to 0.1875
- tile_cols: int32 [4, 16], P(None, 'vert'), may hold values from 0 to 1
- tile_vals: bfloat16 [4, 16, 128, 128], P(None, 'vert'), may hold values from -0.5 to 0.5
- send_rows: int32 [4, 64, 8], P(None, 'vert'), may hold values from 0 to 255
- send_count: int32 [4, 64], P(None, 'vert'), may hold values from 1 to 8, as said below
- recv_rows: int32 [4, 64, 8], P(None, 'vert'), may hold values from 0 to 255
- recv_weight: bfloat16 [4, 64, 8], P(None, 'vert'), may hold values from 0.25 to 1
- pair_owner: int32 [4, 2048, 1], P(None, 'vert'), may hold values from 0 to 7; in each aligned block of 256 rows (0 to 255, 256 to 511, ..., all dimensions but the last counted through in order) at most 48 rows name the same one
Outputs:
- losses: float32 [4, 4, 3072], P('segment', None, 'vert')
Inputs may be any that keep to these rules, and one draw needn't show every extreme that they name: `send_count`: for every span and sender, each peer gets 1 to 8 used slots and some peer gets exactly 8. `pair_owner`: in each span no device's rows name one owner more than 48 times; some reach 48.
All inputs are finite; a program needn't handle non-finite values.
Results may differ from a plain program's by a relative error of at most 0.0025.
Values may be sent and summed in bfloat16 or wider, within the bound.
No kernel may reach another device: no remote copies, remote signals or barrier semaphores. Data moves between devices by JAX's collectives and lax.ppermute only.
A program may use at most 192 MiB of HBM per device.

v0:
```python
import jax
import jax.numpy as jnp
from jax import lax
from jax.sharding import PartitionSpec as P

ALPHA_MIX = 0.5
LAMBDA_DECAY = 0.5
SOFTMAX_TEMP = 0.1


def from_behind(block, axis, distance):
    devices = range(lax.axis_size(axis))
    route = [(i - distance, i) for i in devices if i - distance in devices]
    return lax.ppermute(block, axis, route)


def rms_unit(vectors):
    vectors = vectors.astype(jnp.float32)
    return (
        vectors * lax.rsqrt(jnp.mean(vectors * vectors, axis=-1, keepdims=True) + 1e-06)
    ).astype(jnp.bfloat16)


def pack_pairs(owners, embed, init_span, capacity, vert_count):
    row_count = embed.shape[0]
    target_dev = owners[:, 0]
    onehot = (target_dev[:, None] == jnp.arange(vert_count)[None, :]).astype(jnp.int32)
    before = jnp.cumsum(onehot, axis=0) - onehot
    place = jnp.sum(before * onehot, axis=1)
    lookup = (
        jnp.full((vert_count * capacity,), row_count, jnp.int32)
        .at[target_dev * capacity + place]
        .set(jnp.arange(row_count, dtype=jnp.int32))
    )
    blank = jnp.zeros((1, embed.shape[1]), jnp.bfloat16)
    padded_embed = jnp.concatenate([embed, blank], axis=0)
    padded_init = jnp.concatenate([init_span, blank], axis=0)
    anchors = padded_embed[lookup].reshape(vert_count, capacity, -1)
    keys_all = padded_init[lookup].reshape(vert_count, capacity, -1)
    flags = (lookup < row_count).astype(jnp.bfloat16).reshape(vert_count, capacity)
    return (anchors, keys_all, flags)


def score_pairs(anchors, keys_all, flags):
    feature_columns = anchors.shape[-1]
    query_rows = rms_unit(anchors.reshape(-1, feature_columns))
    normalized_keys = rms_unit(keys_all.reshape(-1, feature_columns))
    similarity_scores = jnp.dot(
        query_rows, normalized_keys.T, preferred_element_type=jnp.float32
    ) / (feature_columns * SOFTMAX_TEMP)
    live_mask = flags.reshape(-1).astype(jnp.float32)
    totals = jnp.sum(jnp.exp(similarity_scores) * live_mask[None, :], axis=1)
    diagonal = jnp.diagonal(similarity_scores)
    return (jnp.log(totals + 1.0 - live_mask) - diagonal) * live_mask


def local(
    init_feats,
    layer_weight,
    tile_cols,
    tile_vals,
    send_rows,
    send_count,
    recv_rows,
    recv_weight,
    pair_owner,
):
    segment_count = lax.axis_size("segment")
    vert_count = lax.axis_size("vert")
    position = lax.axis_index("segment")
    span_count, row_count, feature_columns = init_feats.shape
    capacity = 3 * row_count // (2 * vert_count)
    tile_size = tile_vals.shape[-1]
    tile_rows = row_count // tile_size
    slot_count = send_rows.shape[-1]
    weight = layer_weight[0]
    mixing = jnp.log(LAMBDA_DECAY / (position.astype(jnp.float32) + 1.0) + 1.0)
    row_ids = jnp.arange(row_count, dtype=jnp.int32)

    def section(span_id, hidden, init_span):
        columns = tile_cols[span_id]
        values = tile_vals[span_id]
        picked = hidden.reshape(tile_rows, tile_size, feature_columns)[columns]
        local_sum = jnp.einsum(
            "tij,tjd->tid", values, picked, preferred_element_type=jnp.float32
        ).reshape(row_count, feature_columns)
        retain = jnp.arange(slot_count)[None, :] < send_count[span_id][:, None]
        outgoing = jnp.where(
            retain[..., None], hidden[send_rows[span_id]], jnp.zeros((), jnp.bfloat16)
        )
        incoming = lax.all_to_all(outgoing, "vert", split_axis=0, concat_axis=0, tiled=True)
        targets = recv_rows[span_id].reshape(-1)
        edge_weights = recv_weight[span_id].reshape(-1)
        placing = jnp.where(
            targets[None, :] == row_ids[:, None], edge_weights[None, :], jnp.zeros((), jnp.bfloat16)
        )
        border = jnp.dot(
            placing, incoming.reshape(-1, feature_columns), preferred_element_type=jnp.float32
        )
        mixed = (1.0 - ALPHA_MIX) * (local_sum + border) + ALPHA_MIX * init_span.astype(jnp.float32)
        support = mixed.astype(jnp.bfloat16)
        product = jnp.dot(support, weight, preferred_element_type=jnp.float32)
        return jax.nn.relu((1.0 - mixing) * support.astype(jnp.float32) + mixing * product).astype(
            jnp.bfloat16
        )

    stored = jnp.zeros((span_count, row_count, feature_columns), jnp.bfloat16)

    def advance(moment, carry):
        arrived, stored_now = carry
        span_raw = moment - position
        active = (span_raw >= 0) & (span_raw < span_count)
        span_id = jnp.clip(span_raw, 0, span_count - 1)
        init_span = init_feats[span_id]
        hidden = jnp.where(position == 0, init_span, arrived)
        result = section(span_id, hidden, init_span)
        passed = from_behind(result, "segment", 1)
        stored_now = jnp.where(active, stored_now.at[span_id].set(result), stored_now)
        return (passed, stored_now)

    start_carry = (jnp.zeros((row_count, feature_columns), jnp.bfloat16), stored)
    final_carry = lax.fori_loop(0, span_count + segment_count - 1, advance, start_carry)
    stored = final_carry[1]

    def pack_one(owners, embed, init_span):
        return pack_pairs(owners, embed, init_span, capacity, vert_count)

    anchors, keys_all, flags = jax.vmap(pack_one)(pair_owner, stored, init_feats)
    got_anchors, got_keys, got_flags = (
        lax.all_to_all(anchors, "vert", split_axis=1, concat_axis=1, tiled=True),
        lax.all_to_all(keys_all, "vert", split_axis=1, concat_axis=1, tiled=True),
        lax.all_to_all(flags, "vert", split_axis=1, concat_axis=1, tiled=True),
    )
    losses = jax.vmap(score_pairs)(got_anchors, got_keys, got_flags)
    return losses[None]


def solution(mesh):
    return jax.shard_map(
        local,
        mesh=mesh,
        in_specs=(
            P(None, "vert", None),
            P("segment", None, None),
            P(None, "vert"),
            P(None, "vert", None, None),
            P(None, "vert", None),
            P(None, "vert"),
            P(None, "vert", None),
            P(None, "vert", None),
            P(None, "vert", None),
        ),
        out_specs=P("segment", None, "vert"),
        check_vma=False,
    )
```

profile of v0, /device:TPU:0, one launch (start us, length us, event | category | flops | bytes accessed | tf_op | source)
XLA Modules:
  0.0 462.6 jit_solution(10438071151026570301)
XLA Ops:
  2.2 2.3 reduce-window.6
  7.1 4.3 scatter_custom_fusion
  12.1 1.6 broadcast_in_dim.102
  13.8 208.7 %while.18 = (s32[]{:T(128)}, bf16[256,1024]{1,0:T(8,128)(2,1)S(1)}, bf16[4,256,1024]{2,1,0:T(8,128)(2,1)}, f32[]{:T(128)}, s32[]{:T(128)}, /*index=5*/bf16[4,2,1...) while((s32[]{:T(128)}, bf16[256,1024]{1,0:T(8,128)(2,1)S(1)}, ...), condition=%wide.region_2.3_spmd.clone, body=%wide.region_0.2_spmd.clone.sunk | while | flops 641304832 | bytes 14236221 | solution.py:122
  17.9 7.3 %all-to-all-start = ((bf16[8,8,1024]{2,1,0:T(8,128)(2,1)}), bf16[8,8,1024]{2,1,0:T(8,128)(2,1)S(1)}, u32[]{:S(2)}, u32[]{:S(2)}) async-start(bf16[8,8,1024]{2,1,0:T(8,128)(2,1)} %bitcast_select_fusion.5), calls=%async_computation | async-start | bytes 262144 | tf_op jit(solution)/shard_map/while/body/eval_jaxpr/all_to_all | solution.py:91
  29.2 3.4 all-to-all-done
  33.9 3.9 fusion.64
  44.7 3.4 all-to-all-start
  52.1 3.3 all-to-all-done
  56.7 4.0 fusion.64
  60.7 7.6 %collective-permute-start = (bf16[256,1024]{1,0:T(8,128)(2,1)S(1)}, bf16[256,1024]{1,0:T(8,128)(2,1)S(1)}, u32[]{:S(2)}, u32[]{:S(2)}) collective-permute-start(bf16[256,1024]{1,0:T(8,128)(2,1)S(1)} %get-tuple-element.556), channel_id=1, source_target_pairs={{0,8},{8,16},{16,24},{1,9},{9,17},{17,25},{2,10},{10,18},{18,26},{... | collective-permute-start | bytes 1572872 | tf_op jit(solution)/shard_map/while/body/eval_jaxpr/ppermute | solution.py:14
  68.2 1.5 collective-permute-done
  73.8 3.5 all-to-all-start
  81.4 3.4 all-to-all-done
  86.1 4.0 fusion.64
  90.0 8.8 %collective-permute-start = (bf16[256,1024]{1,0:T(8,128)(2,1)S(1)}, bf16[256,1024]{1,0:T(8,128)(2,1)S(1)}, u32[]{:S(2)}, u32[]{:S(2)}) collective-permute-start(bf16[256,1024]{1,0:T(8,128)(2,1)S(1)} %get-tuple-element.556), channel_id=1, source_target_pairs={{0,8},{8,16},{16,24},{1,9},{9,17},{17,25},{2,10},{10,18},{18,26},{... | collective-permute-start | bytes 1572872 | tf_op jit(solution)/shard_map/while/body/eval_jaxpr/ppermute | solution.py:14
  104.4 3.5 all-to-all-start
  111.9 3.4 all-to-all-done
  116.6 4.0 fusion.64
  120.6 8.8 %collective-permute-start = (bf16[256,1024]{1,0:T(8,128)(2,1)S(1)}, bf16[256,1024]{1,0:T(8,128)(2,1)S(1)}, u32[]{:S(2)}, u32[]{:S(2)}) collective-permute-start(bf16[256,1024]{1,0:T(8,128)(2,1)S(1)} %get-tuple-element.556), channel_id=1, source_target_pairs={{0,8},{8,16},{16,24},{1,9},{9,17},{17,25},{2,10},{10,18},{18,26},{... | collective-permute-start | bytes 1572872 | tf_op jit(solution)/shard_map/while/body/eval_jaxpr/ppermute | solution.py:14
  134.9 3.5 all-to-all-start
  142.4 3.4 all-to-all-done
  147.1 4.0 fusion.64
  151.1 8.8 %collective-permute-start = (bf16[256,1024]{1,0:T(8,128)(2,1)S(1)}, bf16[256,1024]{1,0:T(8,128)(2,1)S(1)}, u32[]{:S(2)}, u32[]{:S(2)}) collective-permute-start(bf16[256,1024]{1,0:T(8,128)(2,1)S(1)} %get-tuple-element.556), channel_id=1, source_target_pairs={{0,8},{8,16},{16,24},{1,9},{9,17},{17,25},{2,10},{10,18},{18,26},{... | collective-permute-start | bytes 1572872 | tf_op jit(solution)/shard_map/while/body/eval_jaxpr/ppermute | solution.py:14
  165.5 3.5 all-to-all-start
  173.0 3.4 all-to-all-done
  177.7 4.0 fusion.64
  181.6 8.8 %collective-permute-start = (bf16[256,1024]{1,0:T(8,128)(2,1)S(1)}, bf16[256,1024]{1,0:T(8,128)(2,1)S(1)}, u32[]{:S(2)}, u32[]{:S(2)}) collective-permute-start(bf16[256,1024]{1,0:T(8,128)(2,1)S(1)} %get-tuple-element.556), channel_id=1, source_target_pairs={{0,8},{8,16},{16,24},{1,9},{9,17},{17,25},{2,10},{10,18},{18,26},{... | collective-permute-start | bytes 1572872 | tf_op jit(solution)/shard_map/while/body/eval_jaxpr/ppermute | solution.py:14
  196.0 3.5 all-to-all-start
  203.5 3.4 all-to-all-done
  208.2 4.0 fusion.64
  212.2 8.8 %collective-permute-start = (bf16[256,1024]{1,0:T(8,128)(2,1)S(1)}, bf16[256,1024]{1,0:T(8,128)(2,1)S(1)}, u32[]{:S(2)}, u32[]{:S(2)}) collective-permute-start(bf16[256,1024]{1,0:T(8,128)(2,1)S(1)} %get-tuple-element.556), channel_id=1, source_target_pairs={{0,8},{8,16},{16,24},{1,9},{9,17},{17,25},{2,10},{10,18},{18,26},{... | collective-permute-start | bytes 1572872 | tf_op jit(solution)/shard_map/while/body/eval_jaxpr/ppermute | solution.py:14
  222.5 3.5 all-to-all-start.3
  226.0 3.2 copy.55
  230.1 22.6 %gather_fusion.3 = bf16[1536,1024]{1,0:T(8,128)(2,1)} fusion(bf16[4,257,1024]{2,0,1:T(4,128)(2,1)S(1)} %concatenate.19, s32[1536]{0:T(1024)S(1)} %reshape.324), kind=kCustom, calls=%fused_computation.3 | custom fusion | bytes 6303744 | tf_op jit(solution)/shard_map/vmap()/gather | solution.py:38
  252.6 4.0 copy.58
  256.7 6.1 %all-to-all-start.1 = ((bf16[4,8,48,1024]{3,2,0,1:T(8,128)(2,1)}), bf16[4,8,48,1024]{3,2,0,1:T(8,128)(2,1)}, u32[]{:S(2)}, u32[]{:S(2)}) async-start(bf16[4,8,48,1024]{3,2,0,1:T(8,128)(2,1)} %copy.58), calls=%async_computation.1 | async-start | bytes 6291456 | tf_op jit(solution)/shard_map/all_to_all | solution.py:130
  262.8 1.6 copy.60
  265.3 22.6 %gather_fusion.4 = bf16[1536,1024]{1,0:T(8,128)(2,1)} fusion(bf16[4,257,1024]{2,0,1:T(4,128)(2,1)S(1)} %concatenate.20, s32[1536]{0:T(1024)S(1)} %reshape.324), kind=kCustom, calls=%fused_computation.4 | custom fusion | bytes 6303744 | tf_op jit(solution)/shard_map/vmap()/gather | solution.py:39
  287.9 4.1 copy.61
  292.0 38.4 %all-to-all-done.1 = bf16[4,8,48,1024]{3,2,0,1:T(8,128)(2,1)} async-done(((bf16[4,8,48,1024]{3,2,0,1:T(8,128)(2,1)}), bf16[4,8,48,1024]{3,2,0,1:T(8,128)(2,1)}, u32[]{:S(2)}, u32[]{:S(2)}) %all-to-all-start.1) | async-done | bytes 3145760 | tf_op jit(solution)/shard_map/all_to_all | solution.py:130
  330.3 8.3 %all-to-all-start.2 = ((bf16[4,8,48,1024]{3,2,0,1:T(8,128)(2,1)}), bf16[4,8,48,1024]{3,2,0,1:T(8,128)(2,1)S(1)}, u32[]{:S(2)}, u32[]{:S(2)}) async-start(bf16[4,8,48,1024]{3,2,0,1:T(8,128)(2,1)} %copy.61), calls=%async_computation.2 | async-start | bytes 6291456 | tf_op jit(solution)/shard_map/all_to_all | solution.py:131
  338.9 2.6 multiply_reduce_fusion.1
  341.5 68.6 %all-to-all-done.2 = bf16[4,8,48,1024]{3,2,0,1:T(8,128)(2,1)S(1)} async-done(((bf16[4,8,48,1024]{3,2,0,1:T(8,128)(2,1)}), bf16[4,8,48,1024]{3,2,0,1:T(8,128)(2,1)S(1)}, u32[]{:S(2)}, u32[]{:S(2)}) %all-to-all-start.2) | async-done | bytes 3145760 | tf_op jit(solution)/shard_map/all_to_all | solution.py:131
  410.9 2.6 copy_convert_fusion.1
  415.1 1.9 multiply_reduce_fusion.2
  417.0 36.5 %copy.67 = f32[4,384,384]{0,2,1:T(8,128)} copy(f32[4,384,384]{1,2,0:T(8,128)S(1)} %get-tuple-element.462) | data formatting | bytes 4718592 | tf_op jit(solution)/shard_map/vmap()/div | solution.py:48
  453.6 8.3 %gather_fusion.2 = f32[384,4]{1,0:T(8,128)S(1)} fusion(f32[4,384,384]{0,2,1:T(8,128)} %copy.67, s32[384]{0:T(512)S(1)} %or_reduce_fusion), kind=kCustom, calls=%fused_computation.2 | custom fusion | bytes 15360 | tf_op jit(solution)/shard_map/vmap(jit(diagonal))/cond/branch_0_fun/gather | solution.py:53
  (191 shorter events, 86.5 us)
Async XLA Ops:
  13.8 13.6 %copy-start.1 = (s32[3]{0:T(128)S(1)}, s32[3]{0:T(128)}, u32[]{:S(2)}) copy-start(s32[3]{0:T(128)} %get-tuple-element.618) | copy-start | bytes 40 | tf_op jit(solution)/shard_map/while
  17.9 14.6 %all-to-all-start = ((bf16[8,8,1024]{2,1,0:T(8,128)(2,1)}), bf16[8,8,1024]{2,1,0:T(8,128)(2,1)S(1)}, u32[]{:S(2)}, u32[]{:S(2)}) async-start(bf16[8,8,1024]{2,1,0:T(8,128)(2,1)} %bitcast_select_fusion.5), calls=%async_computation | async-start | bytes 262144 | tf_op jit(solution)/shard_map/while/body/eval_jaxpr/all_to_all | solution.py:91
  37.8 2.8 collective-permute-start
  40.6 9.7 %copy-start.1 = (s32[3]{0:T(128)S(1)}, s32[3]{0:T(128)}, u32[]{:S(2)}) copy-start(s32[3]{0:T(128)} %get-tuple-element.618) | copy-start | bytes 40 | tf_op jit(solution)/shard_map/while
  44.7 10.7 %all-to-all-start = ((bf16[8,8,1024]{2,1,0:T(8,128)(2,1)}), bf16[8,8,1024]{2,1,0:T(8,128)(2,1)S(1)}, u32[]{:S(2)}, u32[]{:S(2)}) async-start(bf16[8,8,1024]{2,1,0:T(8,128)(2,1)} %bitcast_select_fusion.5), calls=%async_computation | async-start | bytes 262144 | tf_op jit(solution)/shard_map/while/body/eval_jaxpr/all_to_all | solution.py:91
  60.7 9.1 %collective-permute-start = (bf16[256,1024]{1,0:T(8,128)(2,1)S(1)}, bf16[256,1024]{1,0:T(8,128)(2,1)S(1)}, u32[]{:S(2)}, u32[]{:S(2)}) collective-permute-start(bf16[256,1024]{1,0:T(8,128)(2,1)S(1)} %get-tuple-element.556), channel_id=1, source_target_pairs={{0,8},{8,16},{16,24},{1,9},{9,17},{17,25},{2,10},{10,18},{18,26},{... | collective-permute-start | bytes 1572872 | tf_op jit(solution)/shard_map/while/body/eval_jaxpr/ppermute | solution.py:14
  69.7 9.8 %copy-start.1 = (s32[3]{0:T(128)S(1)}, s32[3]{0:T(128)}, u32[]{:S(2)}) copy-start(s32[3]{0:T(128)} %get-tuple-element.618) | copy-start | bytes 40 | tf_op jit(solution)/shard_map/while
  73.8 10.9 %all-to-all-start = ((bf16[8,8,1024]{2,1,0:T(8,128)(2,1)}), bf16[8,8,1024]{2,1,0:T(8,128)(2,1)S(1)}, u32[]{:S(2)}, u32[]{:S(2)}) async-start(bf16[8,8,1024]{2,1,0:T(8,128)(2,1)} %bitcast_select_fusion.5), calls=%async_computation | async-start | bytes 262144 | tf_op jit(solution)/shard_map/while/body/eval_jaxpr/all_to_all | solution.py:91
  90.0 10.3 %collective-permute-start = (bf16[256,1024]{1,0:T(8,128)(2,1)S(1)}, bf16[256,1024]{1,0:T(8,128)(2,1)S(1)}, u32[]{:S(2)}, u32[]{:S(2)}) collective-permute-start(bf16[256,1024]{1,0:T(8,128)(2,1)S(1)} %get-tuple-element.556), channel_id=1, source_target_pairs={{0,8},{8,16},{16,24},{1,9},{9,17},{17,25},{2,10},{10,18},{18,26},{... | collective-permute-start | bytes 1572872 | tf_op jit(solution)/shard_map/while/body/eval_jaxpr/ppermute | solution.py:14
  100.3 9.8 %copy-start.1 = (s32[3]{0:T(128)S(1)}, s32[3]{0:T(128)}, u32[]{:S(2)}) copy-start(s32[3]{0:T(128)} %get-tuple-element.618) | copy-start | bytes 40 | tf_op jit(solution)/shard_map/while
  104.4 10.9 %all-to-all-start = ((bf16[8,8,1024]{2,1,0:T(8,128)(2,1)}), bf16[8,8,1024]{2,1,0:T(8,128)(2,1)S(1)}, u32[]{:S(2)}, u32[]{:S(2)}) async-start(bf16[8,8,1024]{2,1,0:T(8,128)(2,1)} %bitcast_select_fusion.5), calls=%async_computation | async-start | bytes 262144 | tf_op jit(solution)/shard_map/while/body/eval_jaxpr/all_to_all | solution.py:91
  120.6 10.3 %collective-permute-start = (bf16[256,1024]{1,0:T(8,128)(2,1)S(1)}, bf16[256,1024]{1,0:T(8,128)(2,1)S(1)}, u32[]{:S(2)}, u32[]{:S(2)}) collective-permute-start(bf16[256,1024]{1,0:T(8,128)(2,1)S(1)} %get-tuple-element.556), channel_id=1, source_target_pairs={{0,8},{8,16},{16,24},{1,9},{9,17},{17,25},{2,10},{10,18},{18,26},{... | collective-permute-start | bytes 1572872 | tf_op jit(solution)/shard_map/while/body/eval_jaxpr/ppermute | solution.py:14
  130.8 9.8 %copy-start.1 = (s32[3]{0:T(128)S(1)}, s32[3]{0:T(128)}, u32[]{:S(2)}) copy-start(s32[3]{0:T(128)} %get-tuple-element.618) | copy-start | bytes 40 | tf_op jit(solution)/shard_map/while
  134.9 10.9 %all-to-all-start = ((bf16[8,8,1024]{2,1,0:T(8,128)(2,1)}), bf16[8,8,1024]{2,1,0:T(8,128)(2,1)S(1)}, u32[]{:S(2)}, u32[]{:S(2)}) async-start(bf16[8,8,1024]{2,1,0:T(8,128)(2,1)} %bitcast_select_fusion.5), calls=%async_computation | async-start | bytes 262144 | tf_op jit(solution)/shard_map/while/body/eval_jaxpr/all_to_all | solution.py:91
  151.1 10.3 %collective-permute-start = (bf16[256,1024]{1,0:T(8,128)(2,1)S(1)}, bf16[256,1024]{1,0:T(8,128)(2,1)S(1)}, u32[]{:S(2)}, u32[]{:S(2)}) collective-permute-start(bf16[256,1024]{1,0:T(8,128)(2,1)S(1)} %get-tuple-element.556), channel_id=1, source_target_pairs={{0,8},{8,16},{16,24},{1,9},{9,17},{17,25},{2,10},{10,18},{18,26},{... | collective-permute-start | bytes 1572872 | tf_op jit(solution)/shard_map/while/body/eval_jaxpr/ppermute | solution.py:14
  161.4 9.8 %copy-start.1 = (s32[3]{0:T(128)S(1)}, s32[3]{0:T(128)}, u32[]{:S(2)}) copy-start(s32[3]{0:T(128)} %get-tuple-element.618) | copy-start | bytes 40 | tf_op jit(solution)/shard_map/while
  165.5 10.9 %all-to-all-start = ((bf16[8,8,1024]{2,1,0:T(8,128)(2,1)}), bf16[8,8,1024]{2,1,0:T(8,128)(2,1)S(1)}, u32[]{:S(2)}, u32[]{:S(2)}) async-start(bf16[8,8,1024]{2,1,0:T(8,128)(2,1)} %bitcast_select_fusion.5), calls=%async_computation | async-start | bytes 262144 | tf_op jit(solution)/shard_map/while/body/eval_jaxpr/all_to_all | solution.py:91
  181.6 10.3 %collective-permute-start = (bf16[256,1024]{1,0:T(8,128)(2,1)S(1)}, bf16[256,1024]{1,0:T(8,128)(2,1)S(1)}, u32[]{:S(2)}, u32[]{:S(2)}) collective-permute-start(bf16[256,1024]{1,0:T(8,128)(2,1)S(1)} %get-tuple-element.556), channel_id=1, source_target_pairs={{0,8},{8,16},{16,24},{1,9},{9,17},{17,25},{2,10},{10,18},{18,26},{... | collective-permute-start | bytes 1572872 | tf_op jit(solution)/shard_map/while/body/eval_jaxpr/ppermute | solution.py:14
  191.9 9.8 %copy-start.1 = (s32[3]{0:T(128)S(1)}, s32[3]{0:T(128)}, u32[]{:S(2)}) copy-start(s32[3]{0:T(128)} %get-tuple-element.618) | copy-start | bytes 40 | tf_op jit(solution)/shard_map/while
  196.0 10.9 %all-to-all-start = ((bf16[8,8,1024]{2,1,0:T(8,128)(2,1)}), bf16[8,8,1024]{2,1,0:T(8,128)(2,1)S(1)}, u32[]{:S(2)}, u32[]{:S(2)}) async-start(bf16[8,8,1024]{2,1,0:T(8,128)(2,1)} %bitcast_select_fusion.5), calls=%async_computation | async-start | bytes 262144 | tf_op jit(solution)/shard_map/while/body/eval_jaxpr/all_to_all | solution.py:91
  212.2 10.3 %collective-permute-start = (bf16[256,1024]{1,0:T(8,128)(2,1)S(1)}, bf16[256,1024]{1,0:T(8,128)(2,1)S(1)}, u32[]{:S(2)}, u32[]{:S(2)}) collective-permute-start(bf16[256,1024]{1,0:T(8,128)(2,1)S(1)} %get-tuple-element.556), channel_id=1, source_target_pairs={{0,8},{8,16},{16,24},{1,9},{9,17},{17,25},{2,10},{10,18},{18,26},{... | collective-permute-start | bytes 1572872 | tf_op jit(solution)/shard_map/while/body/eval_jaxpr/ppermute | solution.py:14
  222.5 34.2 %all-to-all-start.3 = ((bf16[4,8,48]{2,0,1:T(4,128)(2,1)}), bf16[4,8,48]{2,0,1:T(4,128)(2,1)S(1)}, u32[]{:S(2)}, u32[]{:S(2)}) async-start(bf16[4,8,48]{2,0,1:T(4,128)(2,1)} %copy.63), calls=%async_computation.3 | async-start | bytes 16384 | tf_op jit(solution)/shard_map/all_to_all | solution.py:132
  256.7 6.1 %copy-start = (bf16[4,256,1024]{2,1,0:T(8,128)(2,1)S(1)}, bf16[4,256,1024]{2,1,0:T(8,128)(2,1)}, u32[]{:S(2)}) copy-start(bf16[4,256,1024]{2,1,0:T(8,128)(2,1)} %get-tuple-element.622) | copy-start | bytes 6291460
  256.7 73.6 %all-to-all-start.1 = ((bf16[4,8,48,1024]{3,2,0,1:T(8,128)(2,1)}), bf16[4,8,48,1024]{3,2,0,1:T(8,128)(2,1)}, u32[]{:S(2)}, u32[]{:S(2)}) async-start(bf16[4,8,48,1024]{3,2,0,1:T(8,128)(2,1)} %copy.58), calls=%async_computation.1 | async-start | bytes 6291456 | tf_op jit(solution)/shard_map/all_to_all | solution.py:130
  330.3 79.8 %all-to-all-start.2 = ((bf16[4,8,48,1024]{3,2,0,1:T(8,128)(2,1)}), bf16[4,8,48,1024]{3,2,0,1:T(8,128)(2,1)S(1)}, u32[]{:S(2)}, u32[]{:S(2)}) async-start(bf16[4,8,48,1024]{3,2,0,1:T(8,128)(2,1)} %copy.61), calls=%async_computation.2 | async-start | bytes 6291456 | tf_op jit(solution)/shard_map/all_to_all | solution.py:131
where the time goes:
time: 466 us; the launch traced here: 463 us
  waiting for transfers between devices  141 us (30%)
  local copies, waits for them, and re-layouts  139 us (30%)
  starting transfers between devices  99 us (21%)
  matrix products  46.7 us (10%)
  other arithmetic  36 us (8%)
    all_to_all x1, waiting for transfers between devices, local(): lax.all_to_all(keys_all, 'vert', split_axis=1, concat_axis=1, tiled=True)  68.6 us
    ppermute x7, starting transfers between devices, from_behind(): return lax.ppermute(block, axis, route)  52.8 us
    all_to_all x1, waiting for transfers between devices, local(): lax.all_to_all(anchors, 'vert', split_axis=1, concat_axis=1, tiled=True)  38.4 us
    div x1, local copies, waits for them, and re-layouts, score_pairs(): jnp.dot(query_rows, normalized_keys.T, preferred_element_type=jnp.float32)  36.5 us
    all_to_all x7, starting transfers between devices, section(): lax.all_to_all(outgoing, 'vert', split_axis=0, concat_axis=0, tiled=True)  28.3 us
    dot_general x7, matrix products, section(): product = jnp.dot(support, weight, preferred_element_type=jnp.float32)  27.7 us
    all_to_all x7, waiting for transfers between devices, section(): lax.all_to_all(outgoing, 'vert', split_axis=0, concat_axis=0, tiled=True)  23.4 us
    gather x2, local copies, waits for them, and re-layouts, pack_pairs(): anchors = padded_embed[lookup].reshape(vert_count, capacity, -1)  22.6 us
  transfers between devices with their start and end apart: 17, of which 16 were waited for; matrix products, arithmetic and copies ran while one was open for 20% of the time, Pallas kernels for 0%

commit v1 on v0

--- a/solution.py
+++ b/solution.py
@@ -1,11 +1,282 @@
+import functools
+
 import jax
 import jax.numpy as jnp
+import numpy as np
 from jax import lax
+from jax.experimental import pallas as pl
+from jax.experimental.pallas import tpu as pltpu
 from jax.sharding import PartitionSpec as P
 
 ALPHA_MIX = 0.5
 LAMBDA_DECAY = 0.5
 SOFTMAX_TEMP = 0.1
+NORM_EPS = 1e-06
+SPAN_BYTES = 4 * 1024 * 1024
+
+
+def up_to(count, multiple):
+    return -(-count // multiple) * multiple
+
+
+def swap(block, axis, bit):
+    return lax.ppermute(block, axis, [(i, i ^ bit) for i in range(lax.axis_size(axis))])
+
+
+def rms_unit(vectors):
+    scale = lax.rsqrt(jnp.mean(vectors * vectors, axis=-1, keepdims=True) + NORM_EPS)
+    return (vectors * scale).astype(jnp.bfloat16)
+
+
+def encoder_kernel(
+    dims, cols_ref, where_ref, pack_ref, spread_ref, pick_ref, live_row_ref, live_col_ref, *rest
+):
+    layers, blocks, rows, tile, border, slots = dims
+    weight_refs = rest[:layers]
+    loss_ref, hidden, boundary, anchors, keys, last, weight, weight_sem = rest[layers:]
+    width = hidden.shape[-1]
+    step = pl.program_id(0)
+    phase, block = step // blocks, step % blocks
+    row_start = pl.multiple_of(block * rows, rows)
+    slot_start = pl.multiple_of(block * slots, slots)
+    border_start = pl.multiple_of(block * (border // blocks), border // blocks)
+
+    def fetch(layer, slot):
+        for place in range(layers):
+            @pl.when(where_ref[layer] == place)
+            def _():
+                pltpu.make_async_copy(
+                    weight_refs[place], weight.at[slot], weight_sem.at[slot]
+                ).start()
+
+    def arrive(slot):
+        pltpu.make_async_copy(weight_refs[0], weight.at[slot], weight_sem.at[slot]).wait()
+
+    @pl.when(step == 0)
+    def _():
+        fetch(0, 0)
+
+    init_block = pack_ref[block, pl.ds(0, rows), :]
+
+    def publish(block_out, side, target):
+        picked = jnp.dot(pick_ref[0], block_out, preferred_element_type=jnp.float32)
+        each = border // blocks
+        for receiver in range(blocks):
+            boundary[side, receiver, pl.ds(border_start, each), :] = picked[
+                receiver * each : (receiver + 1) * each
+            ]
+        target[pl.ds(slot_start, slots), :] = rms_unit(picked[border:])
+
+    def support_of(side):
+        incoming = boundary[side, block].astype(jnp.bfloat16)
+        parts = []
+        for t in range(rows // tile):
+            column = cols_ref[block * (rows // tile) + t]
+            start = pl.multiple_of(row_start + column * tile, tile)
+            source = jnp.concatenate([hidden[side, pl.ds(start, tile), :], incoming], axis=0)
+            parts.append(jnp.dot(spread_ref[t], source, preferred_element_type=jnp.float32))
+        gathered = jnp.concatenate(parts, axis=0)
+        mixed = (1.0 - ALPHA_MIX) * gathered + ALPHA_MIX * init_block.astype(jnp.float32)
+        return mixed.astype(jnp.bfloat16)
+
+    def transform(support, slot, mixing):
+        product = jnp.dot(support, weight[slot], preferred_element_type=jnp.float32)
+        blended = (1.0 - mixing) * support.astype(jnp.float32) + mixing * product
+        return jnp.maximum(blended, 0.0).astype(jnp.bfloat16)
+
+    def score(layer):
+        total_slots = blocks * slots
+        logits = lax.dot_general(
+            keys[...], anchors[...], (((1,), (1,)), ((), ())), preferred_element_type=jnp.float32
+        ) / (width * SOFTMAX_TEMP)
+        live_row = live_row_ref[...]
+        totals = jnp.sum(jnp.exp(logits) * live_col_ref[...], axis=0, keepdims=True)
+        key_ids = lax.broadcasted_iota(jnp.int32, (total_slots, total_slots), 0)
+        anchor_ids = lax.broadcasted_iota(jnp.int32, (total_slots, total_slots), 1)
+        diagonal = jnp.sum(
+            jnp.where(key_ids == anchor_ids, logits, 0.0), axis=0, keepdims=True
+        )
+        loss_ref[pl.ds(layer, 1), :] = (
+            jnp.log(totals + 1.0 - live_row) - diagonal
+        ) * live_row
+
+    @pl.when(phase == 0)
+    def _():
+        hidden[0, pl.ds(row_start, rows), :] = init_block
+        publish(init_block, 0, keys)
+
+    for layer in range(layers):
+        mixing = float(np.log(np.float32(LAMBDA_DECAY) / np.float32(layer + 1) + np.float32(1.0)))
+        side, slot = layer % 2, layer % 2
+
+        @pl.when((phase == layer + 1) & (block == 0))
+        def _():
+            arrive(slot)
+            if layer + 1 < layers:
+                fetch(layer + 1, 1 - slot)
+
+    mixings = [
+        float(np.log(np.float32(LAMBDA_DECAY) / np.float32(layer + 1) + np.float32(1.0)))
+        for layer in range(layers)
+    ]
+
+    @pl.when((phase > 0) & (phase < layers))
+    def _():
+        layer = phase - 1
+        side = layer % 2
+        mixing = jnp.float32(mixings[0])
+        for index in range(1, layers):
+            mixing = jnp.where(layer == index, jnp.float32(mixings[index]), mixing)
+        support = support_of(side)
+        block_out = transform(support, side, mixing)
+        hidden[1 - side, pl.ds(row_start, rows), :] = block_out
+        publish(block_out, 1 - side, anchors)
+
+        @pl.when(block == blocks - 1)
+        def _():
+            score(layer)
+
+    @pl.when(phase == layers)
+    def _():
+        side = (layers - 1) % 2
+        support = support_of(side)
+        chosen = jnp.dot(pick_ref[0, border:, :], support, preferred_element_type=jnp.float32)
+        last[pl.ds(slot_start, slots), :] = chosen.astype(jnp.bfloat16)
+
+        @pl.when(block == blocks - 1)
+        def _():
+            final = transform(last[...], side, mixings[layers - 1])
+            anchors[...] = rms_unit(final.astype(jnp.float32))
+            score(layers - 1)
+
+
+def encode(pack, weights, where, cols, spread, pick, live, rows, tile, border, slots):
+    layers = len(weights)
+    blocks, _, width = pack.shape
+    tiles = rows // tile
+    total = blocks * slots
+    dims = (layers, blocks, rows, tile, border, slots)
+    block_of = lambda i, *_: (i % blocks, 0, 0)
+    whole = lambda *shape: pl.BlockSpec(
+        shape, lambda i, *_: (0,) * len(shape), pipeline_mode=pl.Buffered(1)
+    )
+    return pl.pallas_call(
+        functools.partial(encoder_kernel, dims),
+        out_shape=jax.ShapeDtypeStruct((layers, total), jnp.float32),
+        grid_spec=pltpu.PrefetchScalarGridSpec(
+            num_scalar_prefetch=2,
+            grid=((layers + 1) * blocks,),
+            in_specs=[
+                whole(*pack.shape),
+                pl.BlockSpec((tiles, tile, spread.shape[-1]), block_of),
+                pl.BlockSpec((1, border + slots, rows), block_of),
+                whole(1, total),
+                whole(total, 1),
+            ]
+            + [pl.BlockSpec(memory_space=pl.ANY)] * layers,
+            out_specs=pl.BlockSpec((layers, total), lambda i, *_: (0, 0)),
+            scratch_shapes=[
+                pltpu.VMEM((2, blocks * rows, width), jnp.bfloat16),
+                pltpu.VMEM((2, blocks, border, width), jnp.float32),
+                pltpu.VMEM((total, width), jnp.bfloat16),
+                pltpu.VMEM((total, width), jnp.bfloat16),
+                pltpu.VMEM((total, width), jnp.bfloat16),
+                pltpu.VMEM((2, width, width), jnp.bfloat16),
+                pltpu.SemaphoreType.DMA((2,)),
+            ],
+        ),
+        compiler_params=pltpu.CompilerParams(vmem_limit_bytes=48 * 1024 * 1024),
+        cost_estimate=pl.CostEstimate(
+            flops=2 * layers * blocks * rows * width * width,
+            bytes_accessed=2 * layers * width * width + 2 * pack.size,
+            transcendentals=layers * total * total,
+        ),
+    )(cols, where, pack, spread, pick, live[None, :], live[:, None], *weights)
+
+
+def local(
+    init_feats,
+    layer_weight,
+    tile_cols,
+    tile_vals,
+    send_rows,
+    send_count,
+    recv_rows,
+    recv_weight,
+    pair_owner,
+):
+    segment_count = lax.axis_size("segment")
+    vert_count = lax.axis_size("vert")
+    position = lax.axis_index("segment")
+    mine = lax.axis_index("vert")
+    span_count, row_count, width = init_feats.shape
+    capacity = 3 * row_count // (2 * vert_count)
+    slots = up_to(capacity, 16)
+    tile_size = tile_vals.shape[-1]
+    tiles = row_count // tile_size
+    slot_count = send_rows.shape[-1]
+    border = vert_count * slot_count
+    span = position % span_count
+    bf16 = jnp.bfloat16
+
+    def of_span(array):
+        return lax.dynamic_index_in_dim(array, span, 0, keepdims=False)
+
+    small = [send_rows, recv_rows, send_count, tile_cols, pair_owner, recv_weight]
+    small = [of_span(array).reshape(-1).astype(bf16) for array in small]
+    sizes = [array.shape[0] for array in small]
+    ends = [sum(sizes[: i + 1]) for i in range(len(sizes))]
+    adjacency_rows = tiles * tile_size * tile_size // width
+    small_rows = up_to(-(-ends[-1] // width), 16)
+    small = jnp.concatenate(small + [jnp.zeros((small_rows * width - ends[-1],), bf16)])
+    pack = jnp.concatenate(
+        [
+            of_span(init_feats),
+            of_span(tile_vals).reshape(adjacency_rows, width),
+            small.reshape(small_rows, width),
+        ]
+    )
+    pack = lax.all_gather(pack, "vert", axis=0, tiled=False)
+
+    weights = [layer_weight[0]]
+    reach = 1
+    while reach < segment_count:
+        weights = weights + [swap(w, "segment", reach) for w in weights]
+        reach *= 2
+    where = jnp.arange(segment_count, dtype=jnp.int32) ^ position
+
+    tables = pack[:, row_count + adjacency_rows :, :].reshape(vert_count, -1)
+    starts = [0] + ends
+    tables = [tables[:, starts[i] : ends[i]] for i in range(len(sizes))]
+    ints = [table.astype(jnp.int32) for table in tables[:-1]]
+    all_send, all_recv, all_count, all_cols, all_owner = ints
+    row_ids = jnp.arange(row_count, dtype=jnp.int32)
+    used = jnp.arange(slot_count)[None, None, :] < all_count[:, :, None]
+    used = used.reshape(vert_count, border)
+    sends = used[:, :, None] & (all_send[:, :, None] == row_ids)
+    owned = all_owner == mine
+    place = jnp.cumsum(owned.astype(jnp.int32), axis=1) - 1
+    fills = owned[:, None, :] & (
+        place[:, None, :] == jnp.arange(slots, dtype=jnp.int32)[None, :, None]
+    )
+    pick = jnp.concatenate([sends, fills], axis=1).astype(bf16)
+    live = jnp.any(fills, axis=2).astype(jnp.float32).reshape(-1)
+    placing = jnp.where(
+        all_recv[:, None, :] == row_ids[None, :, None], tables[-1][:, None, :], jnp.zeros((), bf16)
+    )
+    adjacency = pack[:, row_count : row_count + adjacency_rows, :]
+    adjacency = adjacency.reshape(vert_count * tiles, tile_size, tile_size)
+    spread = jnp.concatenate(
+        [adjacency, placing.reshape(vert_count * tiles, tile_size, border)], axis=2
+    )
+    losses = encode(
+        pack, weights, where, all_cols.reshape(-1), spread, pick, live,
+        row_count, tile_size, border, slots,
+    )
+    losses = losses.reshape(segment_count, vert_count, slots)[:, :, :capacity]
+    losses = losses.reshape(segment_count, -1)
+    losses = lax.all_to_all(losses, "segment", split_axis=0, concat_axis=0, tiled=True)
+    return losses[None, :span_count]
 
 
 def from_behind(block, axis, distance):
@@ -14,7 +285,7 @@
     return lax.ppermute(block, axis, route)
 
 
-def rms_unit(vectors):
+def rms_rows(vectors):
     vectors = vectors.astype(jnp.float32)
     return (
         vectors * lax.rsqrt(jnp.mean(vectors * vectors, axis=-1, keepdims=True) + 1e-06)
@@ -43,8 +314,8 @@
 
 def score_pairs(anchors, keys_all, flags):
     feature_columns = anchors.shape[-1]
-    query_rows = rms_unit(anchors.reshape(-1, feature_columns))
-    normalized_keys = rms_unit(keys_all.reshape(-1, feature_columns))
+    query_rows = rms_rows(anchors.reshape(-1, feature_columns))
+    normalized_keys = rms_rows(keys_all.reshape(-1, feature_columns))
     similarity_scores = jnp.dot(
         query_rows, normalized_keys.T, preferred_element_type=jnp.float32
     ) / (feature_columns * SOFTMAX_TEMP)
@@ -54,7 +325,7 @@
     return (jnp.log(totals + 1.0 - live_mask) - diagonal) * live_mask
 
 
-def local(
+def local_by_section(
     init_feats,
     layer_weight,
     tile_cols,
@@ -136,8 +407,13 @@
 
 
 def solution(mesh):
+    def run(init_feats, *rest):
+        fits = mesh.shape["vert"] * init_feats[0].size * 2 <= SPAN_BYTES
+        plan = local if fits and init_feats.shape[0] <= mesh.shape["segment"] else local_by_section
+        return plan(init_feats, *rest)
+
     return jax.shard_map(
-        local,
+        run,
         mesh=mesh,
         in_specs=(
             P(None, "vert", None),

time: 466 us -> 166 us (0.36)
  local copies, waits for them, and re-layouts: 139 us -> 5.8 us
  starting transfers between devices: 99 us -> 5.95 us
  waiting for transfers between devices: 141 us -> 82.4 us
  matrix products: 46.7 us -> 0 us
  Pallas kernels: 0 us -> 44.7 us
  other arithmetic: 36 us -> 6.84 us
  between operations: 0.27 us -> 13.6 us
  blocking collectives: 0 us -> 6.62 us
    all_to_all x10 -> x0, waiting for transfers between devices: 130 us -> none  [the longest x1 68.6 us: local(): lax.all_to_all(keys_all, 'vert', split_axis=1, concat_axis=1, tiled=True)]
    all_gather x0 -> x1, waiting for transfers between devices: none -> 78.4 us  [local(): pack = lax.all_gather(pack, 'vert', axis=0, tiled=False)]
    gather x18 -> x0, local copies, waits for them, and re-layouts: 62.5 us -> none  [the longest x2 22.6 us: pack_pairs(): anchors = padded_embed[lookup].reshape(vert_count, capacity, -1)]
    ppermute x7 -> x3, starting transfers between devices: 52.8 us -> 5.94 us  [swap(): lax.ppermute(block, axis, [(i, i ^ bit) for i in range(lax.axis_size(axis...]
    dot_general x22 -> x0, matrix products: 46.7 us -> none  [the longest x7 27.7 us: section(): product = jnp.dot(support, weight, preferred_element_type=jnp.float32)]
    all_to_all x10 -> x0, starting transfers between devices: 46.2 us -> none  [the longest x7 28.3 us: section(): lax.all_to_all(outgoing, 'vert', split_axis=0, concat_axis=0, tiled=True)]
    pallas_call x0 -> x1, Pallas kernels: none -> 44.7 us  [encode(): pl.pallas_call(functools.partial(encoder_kernel, dims), out_shape=jax.Sha...]
    div x1 -> x0, local copies, waits for them, and re-layouts: 36.5 us -> none  [score_pairs(): jnp.dot(query_rows, normalized_keys.T, preferred_element_type=jnp.float32)]
  transfers between devices with their start and end apart: 17 -> 4, of which waited for: 16 -> 3; matrix products, arithmetic and copies ran while one was open for 20% -> 4% of each run, Pallas kernels for 0% -> 0%
where the time goes in v1:
time: 166 us
  waiting for transfers between devices  82.4 us (50%)
  Pallas kernels  44.7 us (27%)
  between operations  13.6 us (8%)
  other arithmetic  6.84 us (4%)
  blocking collectives  6.62 us (4%)
  starting transfers between devices  5.95 us (4%)
  local copies, waits for them, and re-layouts  5.8 us (3%)
    all_gather x1, waiting for transfers between devices, local(): pack = lax.all_gather(pack, 'vert', axis=0, tiled=False)  78.4 us
    pallas_call x1, Pallas kernels, encode(): pl.pallas_call(functools.partial(encoder_kernel, dims), out_shape=jax.Sha...  44.7 us
    all_to_all x1, blocking collectives, local(): lax.all_to_all(losses, 'segment', split_axis=0, concat_axis=0, tiled=True)  6.62 us
    ppermute x3, starting transfers between devices, swap(): lax.ppermute(block, axis, [(i, i ^ bit) for i in range(lax.axis_size(axis...  5.94 us
    ppermute x3, waiting for transfers between devices, swap(): lax.ppermute(block, axis, [(i, i ^ bit) for i in range(lax.axis_size(axis...  4.01 us
  transfers between devices with their start and end apart: 4, of which 3 were waited for; matrix products, arithmetic and copies ran while one was open for 4% of the time, Pallas kernels for 0%

profile of v1, /device:TPU:0, one launch (start us, length us, event | category | flops | bytes accessed | tf_op | source)
XLA Modules:
  0.0 165.9 jit_solution(16780726600937990036)
XLA Ops:
  6.5 0.0 copy-start
  6.5 0.0 all-gather.3.cloned.1.call-start
  6.5 1.0 fusion.5
  7.6 0.7 fusion.7
  8.2 0.7 fusion.4
  8.9 0.7 constant_dynamic-slice_fusion
  9.6 0.1 reshape.109
  9.7 0.7 dynamic-slice_convert_fusion
  10.4 0.1 convert_element_type.75
  10.5 0.1 convert_element_type.73
  10.6 0.1 concatenate.12
  10.8 0.9 constant_dynamic-slice_fusion.4
  11.7 0.9 pad_maximum_fusion.1
  12.6 0.0 all-gather.3.cloned.1.call-update
  12.6 0.5 collective-permute-start
  13.1 2.6 %collective-permute-start.1 = (bf16[1024,1024]{1,0:T(8,128)(2,1)}, bf16[1024,1024]{1,0:T(8,128)(2,1)}, u32[]{:S(2)}, u32[]{:S(2)}) collective-permute-start(bf16[1024,1024]{1,0:T(8,128)(2,1)} %bitcast.22), channel_id=1, source_target_pairs={{0,16},{8,24},{16,0},{24,8},{1,17},{9,25},{17,1},{25,9},{2,18},{10... | collective-permute-start | bytes 6291464 | tf_op jit(solution)/shard_map/ppermute | solution.py:23
  15.7 0.1 lt.49
  15.8 1.5 collective-permute-done.rest_1_
  17.2 2.9 %collective-permute-start.2 = (bf16[1024,1024]{1,0:T(8,128)(2,1)}, bf16[1024,1024]{1,0:T(8,128)(2,1)}, u32[]{:S(2)}, u32[]{:S(2)}) collective-permute-start(bf16[1024,1024]{1,0:T(8,128)(2,1)} %collective-permute-done.rest_1_), channel_id=1, source_target_pairs={{0,16},{8,24},{16,0},{24,8},{1,17},{9,25},{17,1},{25,9},{2,18},{10... | collective-permute-start | bytes 6291464 | tf_op jit(solution)/shard_map/ppermute | solution.py:23
  20.1 78.4 %all-gather.3.cloned.1.call-done = bf16[2432,1024]{1,0:T(8,128)(2,1)} async-done(((bf16[304,1024]{1,0:T(8,128)(2,1)}), bf16[2432,1024]{1,0:T(8,128)(2,1)}) %all-gather.3.cloned.1.call-update) | async-done | bytes 4980752 | tf_op jit(solution)/shard_map/all_gather | solution.py:239
  98.5 1.0 slice_bitcast_fusion
  99.5 0.2 copy.14
  99.7 0.1 convert_bitcast_fusion
  99.7 0.6 reduce-window.6
  100.3 0.2 slice_reduce_fusion
  100.6 0.1 add_bitcast_fusion
  100.6 0.2 fusion.8
  100.9 0.1 reshape.120.live_row_ref
  101.0 0.1 reshape.123.live_col_ref
  101.1 1.1 slice.42
  102.2 0.1 slice_convert_fusion.3
  102.3 0.1 reshape.118.cols_ref
  102.3 0.1 lt.51
  102.4 0.0 copy-done.2
  102.4 0.1 lt.52
  102.5 0.2 reshape.114
  102.7 0.0 copy-start.1
  102.8 0.9 slice_convert_fusion
  103.7 0.2 fusion
  103.9 0.1 add_convert_fusion.pick_ref
  104.0 0.3 compare_select_fusion
  104.4 0.2 pad_maximum_fusion.spread_ref
  104.6 0.0 collective-permute-done.1.rest_2_
  104.6 2.5 %collective-permute-done.2.rest_3_ = bf16[1024,1024]{1,0:T(8,128)(2,1)} collective-permute-done((bf16[1024,1024]{1,0:T(8,128)(2,1)}, bf16[1024,1024]{1,0:T(8,128)(2,1)}, u32[]{:S(2)}, u32[]{:S(2)}) %collective-permute-start.2) | collective-permute-done | bytes 2097184 | tf_op jit(solution)/shard_map/ppermute | solution.py:23
  107.2 0.0 copy-done.1
  107.2 44.7 %shard_map.91 = f32[4,384]{1,0:T(4,128)S(1)} custom-call(s32[16]{0:T(128)S(1)} %reshape.118.cols_ref, s32[4]{0:T(128)S(1)} %iota_xor_fusion.where_ref, bf16[8,304,1024]{2,1,0:T(8,128)(2,1)} %bitcast.30, bf16[16,128,192]{2,1,0:T(8,128)(2,1)S(1)} %pad_maximum_fusion.spread_ref, bf16[8,112,256]{2,1,0:T(8,128)(2,1)S(1)} %add_convert_fusion.pick_ref, ...), custom_call_target="tpu_custom_call" | custom-call | flops 17179869184 | bytes 13369344 | tf_op jit(solution)/shard_map/pallas_call | solution.py:163
  151.8 6.6 %all_to_all.9 = f32[4,1,384]{2,1,0:T(1,128)S(1)} all-to-all(f32[4,1,384]{2,1,0:T(1,128)S(1)} %copy.12), channel_id=1, replica_groups=mesh['segment'=4,'vert'=8] {'segment'}, dimensions={0} | all-to-all | bytes 12288 | tf_op jit(solution)/shard_map/all_to_all | solution.py:278
  158.5 0.6 copy.13
  (18 shorter events, 0.2 us)
Async XLA Ops:
  6.5 5.1 %copy-start = (bf16[4,256,1024]{2,1,0:T(8,128)(2,1)S(1)}, bf16[4,256,1024]{2,1,0:T(8,128)(2,1)}, u32[]{:S(2)}) copy-start(bf16[4,256,1024]{2,1,0:T(8,128)(2,1)} %param.9) | copy-start | bytes 6291460
  6.5 92.0 %all-gather.3.cloned.1.call-start = ((), (), s32[]{:S(2)}) async-start(), calls=%async_computation.1 | async-start | bytes 5603328 | tf_op jit(solution)/shard_map/all_gather | solution.py:239
  12.6 4.6 %collective-permute-start = (bf16[1024,1024]{1,0:T(8,128)(2,1)}, bf16[1024,1024]{1,0:T(8,128)(2,1)}, u32[]{:S(2)}, u32[]{:S(2)}) collective-permute-start(bf16[1024,1024]{1,0:T(8,128)(2,1)} %bitcast.21), channel_id=1, source_target_pairs={{0,8},{8,0},{16,24},{24,16},{1,9},{9,1},{17,25},{25,17},{2,10},{10... | collective-permute-start | bytes 6291464 | tf_op jit(solution)/shard_map/ppermute | solution.py:23
  13.1 91.5 %collective-permute-start.1 = (bf16[1024,1024]{1,0:T(8,128)(2,1)}, bf16[1024,1024]{1,0:T(8,128)(2,1)}, u32[]{:S(2)}, u32[]{:S(2)}) collective-permute-start(bf16[1024,1024]{1,0:T(8,128)(2,1)} %bitcast.22), channel_id=1, source_target_pairs={{0,16},{8,24},{16,0},{24,8},{1,17},{9,25},{17,1},{25,9},{2,18},{10... | collective-permute-start | bytes 6291464 | tf_op jit(solution)/shard_map/ppermute | solution.py:23
  17.2 89.9 %collective-permute-start.2 = (bf16[1024,1024]{1,0:T(8,128)(2,1)}, bf16[1024,1024]{1,0:T(8,128)(2,1)}, u32[]{:S(2)}, u32[]{:S(2)}) collective-permute-start(bf16[1024,1024]{1,0:T(8,128)(2,1)} %collective-permute-done.rest_1_), channel_id=1, source_target_pairs={{0,16},{8,24},{16,0},{24,8},{1,17},{9,25},{17,1},{25,9},{2,18},{10... | collective-permute-start | bytes 6291464 | tf_op jit(solution)/shard_map/ppermute | solution.py:23
  99.6 2.8 %copy-start.2 = (bf16[1,8,16,1024]{3,1,2,0:T(8,128)(2,1)}, bf16[1,8,16,1024]{3,1,2,0:T(8,128)(2,1)S(1)}, u32[]{:S(2)}) copy-start(bf16[1,8,16,1024]{3,1,2,0:T(8,128)(2,1)S(1)} %copy.14) | copy-start | bytes 786436
  102.7 4.4 %copy-start.1 = (bf16[1,1024,1024]{2,1,0:T(8,128)(2,1)S(1)}, bf16[1,1024,1024]{2,1,0:T(8,128)(2,1)}, u32[]{:S(2)}) copy-start(bf16[1,1024,1024]{2,1,0:T(8,128)(2,1)} %param.10) | copy-start | bytes 6291460
Sparse Core Ops, SparseCore 0:
  12.7 85.7 all-gather.2

commit v2 on v0

--- a/solution.py
+++ b/solution.py
@@ -1,11 +1,510 @@
+import functools
+import itertools
+
 import jax
 import jax.numpy as jnp
+import numpy as np
 from jax import lax
+from jax.experimental import pallas as pl
+from jax.experimental.pallas import tpu as pltpu
+from jax.sharding import Mesh
 from jax.sharding import PartitionSpec as P
 
 ALPHA_MIX = 0.5
 LAMBDA_DECAY = 0.5
 SOFTMAX_TEMP = 0.1
+NORM_EPS = 1e-06
+
+AXES = ("x", "core", "zh", "zl", "y")
+SPANS, SEGMENTS, VERTS = 4, 4, 8
+SMALL_ROWS = 16
+LANES = 128
+SEND, RECV, WEIGHT, COLS, OWNER = 0, 128, 256, 512, 640
+
+
+def exchange(block, axis, core=None):
+    sizes = [range(lax.axis_size(name)) for name in AXES]
+    at = AXES.index(axis)
+    pairs = []
+    for index, here in enumerate(itertools.product(*sizes)):
+        there = list(here)
+        there[at] = 1 - there[at]
+        target = functools.reduce(lambda total, digit: total * 2 + digit, there, 0)
+        if core is None or here[1] == core:
+            pairs.append((index, target))
+    return lax.ppermute(block, AXES, pairs)
+
+
+def rms_unit(vectors):
+    scale = lax.rsqrt(jnp.mean(vectors * vectors, axis=-1, keepdims=True) + NORM_EPS)
+    return (vectors * scale).astype(jnp.bfloat16)
+
+
+def mixing_of(layer):
+    return float(np.log(np.float32(LAMBDA_DECAY) / np.float32(layer + 1) + np.float32(1.0)))
+
+
+def turned(matrix):
+    rows, columns = matrix.shape
+    whole = jnp.concatenate([matrix, jnp.zeros((rows, LANES - columns), matrix.dtype)], axis=1)
+    return jnp.transpose(whole)[:columns]
+
+
+def pack_kernel(
+    place_ref, init_ref, tiles_ref, send_ref, count_ref, recv_ref, weight_ref, cols_ref, owner_ref,
+    mine_ref, other_ref, small, sems,
+):
+    x, core, zh = place_ref[0], place_ref[1], place_ref[2]
+    half, width = mine_ref.shape[0] - SMALL_ROWS, init_ref.shape[-1]
+    peers, slots = send_ref.shape[1:]
+    tiles, rows = cols_ref.shape[-1], owner_ref.shape[-1]
+    first = pl.multiple_of(core * half, half)
+    spans = (zh * 2 + x, (1 - zh) * 2 + x)
+    copies = []
+    for i, out_ref in enumerate((mine_ref, other_ref)):
+        copies.append(
+            pltpu.make_async_copy(
+                init_ref.at[spans[i], pl.ds(first, half), :],
+                out_ref.at[pl.ds(0, half), pl.ds(0, width)],
+                sems.at[2 * i],
+            )
+        )
+        copies.append(
+            pltpu.make_async_copy(
+                tiles_ref.at[spans[i], core],
+                out_ref.at[pl.ds(0, half), pl.ds(width, half)],
+                sems.at[2 * i + 1],
+            )
+        )
+    for copy in copies:
+        copy.start()
+    small[...] = jnp.zeros_like(small)
+    for i, out_ref in enumerate((mine_ref, other_ref)):
+        span = spans[i]
+        sends = turned(send_ref[span].astype(jnp.float32))
+        used = lax.broadcasted_iota(jnp.int32, (slots, peers), 0) < count_ref[pl.ds(span, 1), :]
+        small[i, 0:slots, SEND : SEND + peers] = jnp.where(used, sends, float(rows))
+        small[i, 0:slots, RECV : RECV + peers] = turned(recv_ref[span].astype(jnp.float32))
+        small[i, 0:slots, WEIGHT : WEIGHT + peers] = turned(weight_ref[span].astype(jnp.float32))
+        small[i, 0:1, COLS : COLS + tiles] = cols_ref[pl.ds(span, 1), :].astype(jnp.float32)
+        small[i, 0:1, OWNER : OWNER + rows] = owner_ref[pl.ds(span, 1), :].astype(jnp.float32)
+        out_ref[half : half + SMALL_ROWS, :] = small[i].astype(jnp.bfloat16)
+    for copy in copies:
+        copy.wait()
+
+
+def support_of(block, spread_ref, cols_ref, init_ref, hidden, boundary):
+    tile = spread_ref.shape[1]
+    rows = init_ref.shape[1]
+    incoming = boundary[block].astype(jnp.bfloat16)
+    depth = tile + incoming.shape[0]
+    parts = []
+    for t in range(rows // tile):
+        column = cols_ref[block, t]
+        start = pl.multiple_of(column * tile, tile)
+        source = jnp.concatenate([hidden[block, pl.ds(start, tile), :], incoming], axis=0)
+        gathered = jnp.dot(
+            spread_ref[block * (rows // tile) + t, :, 0:depth],
+            source,
+            preferred_element_type=jnp.float32,
+        )
+        init = init_ref[block, t * tile : (t + 1) * tile, :].astype(jnp.float32)
+        parts.append(((1.0 - ALPHA_MIX) * gathered + ALPHA_MIX * init).astype(jnp.bfloat16))
+    return jnp.concatenate(parts, axis=0)
+
+
+def transform(support, weight, mixing):
+    product = jnp.dot(support, weight, preferred_element_type=jnp.float32)
+    blended = (1.0 - mixing) * support.astype(jnp.float32) + mixing * product
+    return jnp.maximum(blended, 0.0).astype(jnp.bfloat16)
+
+
+def publish(block, block_out, pick_ref, boundary, target):
+    receivers, border, _ = boundary.shape
+    each = border // receivers
+    picked = jnp.dot(pick_ref[block], block_out, preferred_element_type=jnp.float32)
+    border_start = pl.multiple_of(block * each, each)
+    for receiver in range(receivers):
+        boundary[receiver, pl.ds(border_start, each), :] = picked[
+            receiver * each : (receiver + 1) * each
+        ]
+    slots = target.shape[0] // receivers
+    slot_start = pl.multiple_of(block * slots, slots)
+    target[pl.ds(slot_start, slots), :] = rms_unit(picked[border:])
+
+
+def score(keys, anchors, live_ref):
+    total, width = keys.shape
+    logits = lax.dot_general(
+        keys[...], anchors[...], (((1,), (1,)), ((), ())), preferred_element_type=jnp.float32
+    ) / (width * SOFTMAX_TEMP)
+    live = live_ref[:, 0:1]
+    key_ids = lax.broadcasted_iota(jnp.int32, (total, total), 0)
+    anchor_ids = lax.broadcasted_iota(jnp.int32, (total, total), 1)
+    same = key_ids == anchor_ids
+    live_row = jnp.sum(jnp.where(same, live, 0.0), axis=0, keepdims=True)
+    totals = jnp.sum(jnp.exp(logits) * live, axis=0, keepdims=True)
+    diagonal = jnp.sum(jnp.where(same, logits, 0.0), axis=0, keepdims=True)
+    return (jnp.log(totals + 1.0 - live_row) - diagonal) * live_row
+
+
+def run_layer(spread_ref, cols_ref, init_ref, pick_ref, source, border_in, weight, mixing,
+              target, border_out, anchors, group=2, unroll=4):
+    blocks, rows, _ = init_ref.shape
+
+    def advance(chunk, carry):
+        support = jnp.concatenate(
+            [
+                support_of(chunk * group + k, spread_ref, cols_ref, init_ref, source, border_in)
+                for k in range(group)
+            ],
+            axis=0,
+        )
+        out = transform(support, weight[...], mixing)
+        for k in range(group):
+            block_out = out[k * rows : (k + 1) * rows]
+            target[chunk * group + k] = block_out
+            publish(chunk * group + k, block_out, pick_ref, border_out, anchors)
+        return carry
+
+    lax.fori_loop(0, blocks // group, advance, 0, unroll=unroll)
+
+
+def first_kernel(
+    place_ref, init_feats, tile_vals, mine_ref, *rest
+):
+    blocks = VERTS
+    nets, flips = rest[: blocks - 1], rest[blocks - 1 : 2 * blocks - 2]
+    weights = rest[2 * blocks - 2 : 2 * blocks + 2]
+    (init_ref, spread_ref, pick_ref, cols_out, live_ref, keys, hidden, boundary, loss_ref,
+     boundary0, anchors, small, weight, cols_ref, sems, weight_sems) = rest[2 * blocks + 2 :]
+    x, core, zh, zl, y = [place_ref[i] for i in range(5)]
+    vert = zh * 4 + zl * 2 + y
+    rows, width = init_ref.shape[1:]
+    half = rows // 2
+    tile = spread_ref.shape[1]
+    tiles = rows // tile
+    border = boundary.shape[1]
+    each = border // blocks
+    slots = keys.shape[0] // blocks
+
+    def start(source, target, sem):
+        copy = pltpu.make_async_copy(source, target, sem)
+        copy.start()
+        return copy
+
+    for place, source in enumerate(weights):
+        by_x, by_core = place // 2, place % 2
+
+        @pl.when((x == by_x) & (core == by_core))
+        def _():
+            pltpu.make_async_copy(source, weight, weight_sems.at[0]).start()
+
+    span = zh * 2 + x
+    copies = [
+        start(init_feats.at[span], init_ref.at[vert], sems.at[0]),
+        start(mine_ref.at[pl.ds(half, SMALL_ROWS), :], small.at[vert], sems.at[1]),
+    ]
+    at = 2
+    for t in range(tiles):
+        target = spread_ref.at[vert * tiles + t, :, pl.ds(0, tile)]
+        copies.append(start(tile_vals.at[span, t], target, sems.at[at]))
+        at += 1
+    for k in range(1, blocks):
+        block = vert ^ k
+        for part, source in ((core, nets[k - 1]), (1 - core, flips[k - 1])):
+            first = pl.multiple_of(part * half, half)
+            copies.append(
+                start(
+                    source.at[pl.ds(0, half), pl.ds(0, width)],
+                    init_ref.at[block, pl.ds(first, half), :],
+                    sems.at[at],
+                )
+            )
+            copies.append(
+                start(
+                    source.at[pl.ds(0, half), pl.ds(width, tile)],
+                    spread_ref.at[block * tiles + part, :, pl.ds(0, tile)],
+                    sems.at[at + 1],
+                )
+            )
+            at += 2
+        source = nets[k - 1].at[pl.ds(half, SMALL_ROWS), :]
+        copies.append(start(source, small.at[block], sems.at[at]))
+        at += 1
+    for copy in copies:
+        copy.wait()
+
+    owner = core * 4 + zl * 2 + y
+    tables = [small[block].astype(jnp.float32) for block in range(blocks)]
+    owners = jnp.concatenate([table[0:1, OWNER : OWNER + rows] for table in tables], axis=0)
+    cols_out[...] = jnp.concatenate(
+        [table[0:1, COLS : COLS + LANES] for table in tables], axis=0
+    ).astype(jnp.int32)
+    to_scalar = start(cols_out, cols_ref, sems.at[at])
+    owned = jnp.where(owners == owner.astype(jnp.float32), 1.0, 0.0)
+    earlier = lax.broadcasted_iota(jnp.int32, (rows, rows), 0) < lax.broadcasted_iota(
+        jnp.int32, (rows, rows), 1
+    )
+    rank = jnp.dot(
+        owned.astype(jnp.bfloat16),
+        jnp.where(earlier, 1.0, 0.0).astype(jnp.bfloat16),
+        preferred_element_type=jnp.float32,
+    )
+    row_ids = lax.broadcasted_iota(jnp.int32, (each, rows), 1).astype(jnp.float32)
+    slot_ids = lax.broadcasted_iota(jnp.int32, (slots, rows), 0).astype(jnp.float32)
+    for block in range(blocks):
+        table = tables[block]
+        sends = [
+            jnp.where(table[0:each, SEND + peer : SEND + peer + 1] == row_ids, 1.0, 0.0)
+            for peer in range(blocks)
+        ]
+        fills = jnp.where(
+            slot_ids == rank[block : block + 1], owned[block : block + 1], 0.0
+        )
+        pick_ref[block] = jnp.concatenate(sends + [fills], axis=0).astype(jnp.bfloat16)
+        live_ref[block * slots : (block + 1) * slots, :] = jnp.broadcast_to(
+            jnp.sum(fills, axis=1, keepdims=True), (slots, LANES)
+        )
+        placing = [
+            jnp.where(
+                table[0:each, RECV + peer : RECV + peer + 1] == row_ids,
+                table[0:each, WEIGHT + peer : WEIGHT + peer + 1],
+                0.0,
+            )
+            for peer in range(blocks)
+        ]
+        placing = jnp.concatenate(
+            placing + [jnp.zeros((LANES - border, rows), jnp.float32)], axis=0
+        )
+        placing = jnp.transpose(placing).astype(jnp.bfloat16)
+        for t in range(tiles):
+            spread_ref[block * tiles + t, :, tile : tile + LANES] = placing[
+                t * tile : (t + 1) * tile
+            ]
+
+    def begin(block, carry):
+        publish(block, init_ref[block], pick_ref, boundary0, keys)
+        return carry
+
+    lax.fori_loop(0, blocks, begin, 0, unroll=4)
+    to_scalar.wait()
+    pltpu.make_async_copy(weights[0], weight, weight_sems.at[0]).wait()
+    run_layer(
+        spread_ref, cols_ref, init_ref, pick_ref, init_ref, boundary0, weight, mixing_of(0),
+        hidden, boundary, anchors,
+    )
+    loss_ref[...] = score(keys, anchors, live_ref)
+
+
+def rest_kernel(
+    place_ref, cols_ref, init_ref, spread_ref, pick_ref, live_ref, keys, hidden, boundary,
+    loss0_ref, own_ref, flip_ref, even_ref, even_flip_ref, odd_ref, odd_other_ref,
+    odd_flip_ref, odd_other_flip_ref, loss_ref, held, border_held, anchors, last, weight,
+    weight_sems,
+):
+    x, core, zl = place_ref[0], place_ref[1], place_ref[3]
+    layers = SEGMENTS
+    blocks = init_ref.shape[0]
+    slots = keys.shape[0] // blocks
+    half = weight.shape[1] // 2
+
+    def fetch(layer):
+        slot, by_x, by_core = layer % 2, layer // 2, layer % 2
+
+        def load(source, part, to):
+            first = part * half if isinstance(part, int) else pl.multiple_of(part * half, half)
+            pltpu.make_async_copy(
+                source, weight.at[slot, pl.ds(first, half), :], weight_sems.at[slot, to]
+            ).start()
+
+        def load_whole(source):
+            for part in range(2):
+                load(source.at[pl.ds(part * half, half), :], part, part)
+
+        near = x == by_x
+        pl.when(near & (core == by_core))(lambda: load_whole(own_ref))
+        pl.when(near & (core != by_core))(lambda: load_whole(flip_ref))
+        if by_core == 0:
+            pl.when((x != by_x) & (core == 0))(lambda: load_whole(even_ref))
+            pl.when((x != by_x) & (core == 1))(lambda: load_whole(even_flip_ref))
+        else:
+
+            @pl.when((x != by_x) & (core == 1))
+            def _():
+                load(odd_ref, zl, 0)
+                load(odd_other_ref, 1 - zl, 1)
+
+            @pl.when((x != by_x) & (core == 0))
+            def _():
+                load(odd_flip_ref, zl, 0)
+                load(odd_other_flip_ref, 1 - zl, 1)
+
+    def arrive(layer):
+        slot = layer % 2
+        for part in range(2):
+            pltpu.make_async_copy(
+                own_ref.at[pl.ds(part * half, half), :],
+                weight.at[slot, pl.ds(part * half, half), :],
+                weight_sems.at[slot, part],
+            ).wait()
+
+    fetch(1)
+
+    def report(layer, losses):
+        for copy in range(2):
+            loss_ref[2 * layer + copy : 2 * layer + copy + 1, :] = losses
+
+    report(0, loss0_ref[...])
+    source, border_in = hidden, boundary
+    for layer in range(1, layers - 1):
+        arrive(layer)
+        fetch(layer + 1)
+        target, border_out = held.at[layer % 2], border_held.at[layer % 2]
+        run_layer(
+            spread_ref, cols_ref, init_ref, pick_ref, source, border_in, weight.at[layer % 2],
+            mixing_of(layer), target, border_out, anchors,
+        )
+        report(layer, score(keys, anchors, live_ref))
+        source, border_in = target, border_out
+
+    border = boundary.shape[1]
+
+    def choose(block, carry):
+        support = support_of(block, spread_ref, cols_ref, init_ref, source, border_in)
+        chosen = jnp.dot(pick_ref[block, border:, :], support, preferred_element_type=jnp.float32)
+        slot_start = pl.multiple_of(block * slots, slots)
+        last[pl.ds(slot_start, slots), :] = chosen.astype(jnp.bfloat16)
+        return carry
+
+    lax.fori_loop(0, blocks, choose, 0, unroll=4)
+    arrive(layers - 1)
+    final = transform(last[...], weight[(layers - 1) % 2], mixing_of(layers - 1))
+    anchors[...] = rms_unit(final.astype(jnp.float32))
+    report(layers - 1, score(keys, anchors, live_ref))
+
+
+VMEM = pl.BlockSpec(memory_space=pltpu.VMEM)
+SMEM = pl.BlockSpec(memory_space=pltpu.SMEM)
+HBM = pl.BlockSpec(memory_space=pltpu.HBM)
+VMEM_LIMIT = 40 * 1024 * 1024
+
+
+def local(
+    init_feats,
+    layer_weight,
+    tile_cols,
+    tile_vals,
+    send_rows,
+    send_count,
+    recv_rows,
+    recv_weight,
+    pair_owner,
+):
+    span_count, rows, width = init_feats.shape
+    tile = tile_vals.shape[-1]
+    tiles = rows // tile
+    blocks = VERTS
+    border = blocks * send_rows.shape[-1]
+    slots = 3 * rows // (2 * blocks)
+    total = blocks * slots
+    half = rows // 2
+    bf16, f32 = jnp.bfloat16, jnp.float32
+    shape = jax.ShapeDtypeStruct
+    zh, zl = lax.axis_index("zh"), lax.axis_index("zl")
+    place = jnp.stack([lax.axis_index(name) for name in AXES]).astype(jnp.int32)
+    own = layer_weight[0]
+    odd_part = lax.dynamic_slice(own, (zl * (width // 2), 0), (width // 2, width))
+
+    packed = shape((half + SMALL_ROWS, width + tile), bf16)
+    mine, other = pl.pallas_call(
+        pack_kernel,
+        out_shape=(packed, packed),
+        in_specs=[SMEM, HBM, HBM] + [VMEM] * 6,
+        out_specs=(VMEM, VMEM),
+        scratch_shapes=[
+            pltpu.VMEM((2, SMALL_ROWS, width + tile), f32),
+            pltpu.SemaphoreType.DMA((4,)),
+        ],
+    )(
+        place, init_feats, tile_vals, send_rows, send_count, recv_rows, recv_weight, tile_cols,
+        pair_owner[:, :, 0],
+    )
+
+    even = exchange(own, "x", core=0)
+    odd = exchange(odd_part, "x", core=1)
+    net = {4: exchange(other, "zh"), 2: exchange(mine, "zl"), 1: exchange(mine, "y")}
+    net[3] = exchange(net[2], "y")
+    net[6] = exchange(net[4], "zl")
+    net[5] = exchange(net[4], "y")
+    net[7] = exchange(net[6], "y")
+    flip = exchange(own, "core")
+    flips = {k: exchange(net[k], "core") for k in net}
+    odd_other = exchange(odd, "zl", core=1)
+    odd_flip = exchange(odd, "core", core=1)
+    even_flip = exchange(even, "core", core=0)
+    odd_other_flip = exchange(odd_other, "core", core=1)
+
+    keep = [
+        shape((blocks, rows, width), bf16),
+        shape((blocks * tiles, tile, tile + LANES), bf16),
+        shape((blocks, border + slots, rows), bf16),
+        shape((blocks, LANES), jnp.int32),
+        shape((total, LANES), f32),
+        shape((total, width), bf16),
+        shape((blocks, rows, width), bf16),
+        shape((blocks, border, width), f32),
+        shape((1, total), f32),
+    ]
+    order = range(1, blocks)
+    init, spread, pick, cols, live, keys, hidden, boundary, loss0 = pl.pallas_call(
+        first_kernel,
+        out_shape=keep,
+        in_specs=[SMEM] + [HBM] * (3 + 2 * (blocks - 1) + 4),
+        out_specs=[VMEM] * len(keep),
+        scratch_shapes=[
+            pltpu.VMEM((blocks, border, width), f32),
+            pltpu.VMEM((total, width), bf16),
+            pltpu.VMEM((blocks, SMALL_ROWS, width + tile), bf16),
+            pltpu.VMEM((width, width), bf16),
+            pltpu.SMEM((blocks, LANES), jnp.int32),
+            pltpu.SemaphoreType.DMA((8 * blocks,)),
+            pltpu.SemaphoreType.DMA((1,)),
+        ],
+        compiler_params=pltpu.CompilerParams(vmem_limit_bytes=VMEM_LIMIT),
+        cost_estimate=pl.CostEstimate(
+            flops=2 * blocks * rows * width * width, bytes_accessed=1 << 24, transcendentals=0
+        ),
+    )(
+        place, init_feats, tile_vals, mine, *[net[k] for k in order], *[flips[k] for k in order],
+        own, flip, even, even_flip,
+    )
+    losses = pl.pallas_call(
+        rest_kernel,
+        out_shape=shape((2 * SEGMENTS, total), f32),
+        in_specs=[SMEM, SMEM] + [VMEM] * 8 + [HBM] * 8,
+        out_specs=VMEM,
+        scratch_shapes=[
+            pltpu.VMEM((2, blocks, rows, width), bf16),
+            pltpu.VMEM((2, blocks, border, width), f32),
+            pltpu.VMEM((total, width), bf16),
+            pltpu.VMEM((total, width), bf16),
+            pltpu.VMEM((2, width, width), bf16),
+            pltpu.SemaphoreType.DMA((2, 2)),
+        ],
+        compiler_params=pltpu.CompilerParams(vmem_limit_bytes=VMEM_LIMIT),
+        cost_estimate=pl.CostEstimate(
+            flops=6 * blocks * rows * width * width, bytes_accessed=1 << 24, transcendentals=0
+        ),
+    )(
+        place, cols, init, spread, pick, live, keys, hidden, boundary, loss0, own, flip, even,
+        even_flip, odd, odd_other, odd_flip, odd_other_flip,
+    )
+    losses = lax.all_to_all(losses, ("x", "core", "zh"), split_axis=0, concat_axis=0, tiled=True)
+    losses = lax.dynamic_index_in_dim(
+        losses.reshape(2, 2, 2, total), zh, axis=1, keepdims=False
+    )
+    return jnp.swapaxes(losses, 0, 1).reshape(1, span_count, total)
 
 
 def from_behind(block, axis, distance):
@@ -14,7 +513,7 @@
     return lax.ppermute(block, axis, route)
 
 
-def rms_unit(vectors):
+def rms_rows(vectors):
     vectors = vectors.astype(jnp.float32)
     return (
         vectors * lax.rsqrt(jnp.mean(vectors * vectors, axis=-1, keepdims=True) + 1e-06)
@@ -43,8 +542,8 @@
 
 def score_pairs(anchors, keys_all, flags):
     feature_columns = anchors.shape[-1]
-    query_rows = rms_unit(anchors.reshape(-1, feature_columns))
-    normalized_keys = rms_unit(keys_all.reshape(-1, feature_columns))
+    query_rows = rms_rows(anchors.reshape(-1, feature_columns))
+    normalized_keys = rms_rows(keys_all.reshape(-1, feature_columns))
     similarity_scores = jnp.dot(
         query_rows, normalized_keys.T, preferred_element_type=jnp.float32
     ) / (feature_columns * SOFTMAX_TEMP)
@@ -54,7 +553,7 @@
     return (jnp.log(totals + 1.0 - live_mask) - diagonal) * live_mask
 
 
-def local(
+def local_by_section(
     init_feats,
     layer_weight,
     tile_cols,
@@ -136,20 +635,32 @@
 
 
 def solution(mesh):
+    specs = (
+        P(None, "vert", None),
+        P("segment", None, None),
+        P(None, "vert"),
+        P(None, "vert", None, None),
+        P(None, "vert", None),
+        P(None, "vert"),
+        P(None, "vert", None),
+        P(None, "vert", None),
+        P(None, "vert", None),
+    )
+    out_spec = P("segment", None, "vert")
+    if (mesh.shape["segment"], mesh.shape["vert"]) != (SEGMENTS, VERTS):
+        return jax.shard_map(
+            local_by_section, mesh=mesh, in_specs=specs, out_specs=out_spec, check_vma=False
+        )
+    parts = {"segment": AXES[:2], "vert": AXES[2:], None: None}
+    fine = Mesh(mesh.devices.reshape((2,) * len(AXES)), AXES)
+
+    def split(spec):
+        return P(*[parts[name] for name in spec])
+
     return jax.shard_map(
         local,
-        mesh=mesh,
-        in_specs=(
-            P(None, "vert", None),
-            P("segment", None, None),
-            P(None, "vert"),
-            P(None, "vert", None, None),
-            P(None, "vert", None),
-            P(None, "vert"),
-            P(None, "vert", None),
-            P(None, "vert", None),
-            P(None, "vert", None),
-        ),
-        out_specs=P("segment", None, "vert"),
+        mesh=fine,
+        in_specs=tuple(split(spec) for spec in specs),
+        out_specs=split(out_spec),
         check_vma=False,
     )

time: 466 us -> 130 us (0.28)
  local copies, waits for them, and re-layouts: 139 us -> 12.4 us
  waiting for transfers between devices: 141 us -> 48.9 us
  starting transfers between devices: 99 us -> 27.1 us
  matrix products: 46.7 us -> 0 us
  Pallas kernels: 0 us -> 40.4 us
  other arithmetic: 36 us -> 0.03 us
    all_to_all x10 -> x1, waiting for transfers between devices: 130 us -> 5.6 us  [local(): lax.all_to_all(losses, ('x', 'core', 'zh'), split_axis=0, concat_axis=0,...]
    gather x18 -> x0, local copies, waits for them, and re-layouts: 62.5 us -> none  [the longest x2 22.6 us: pack_pairs(): anchors = padded_embed[lookup].reshape(vert_count, capacity, -1)]
    dot_general x22 -> x0, matrix products: 46.7 us -> none  [the longest x7 27.7 us: section(): product = jnp.dot(support, weight, preferred_element_type=jnp.float32)]
    all_to_all x10 -> x1, starting transfers between devices: 46.2 us -> 4.24 us  [local(): lax.all_to_all(losses, ('x', 'core', 'zh'), split_axis=0, concat_axis=0,...]
    pallas_call x0 -> x3, Pallas kernels: none -> 40.4 us  [the longest x1 23.8 us: local(): pl.pallas_call(rest_kernel, out_shape=shape((2 * SEGMENTS, total), f32),...]
    div x1 -> x0, local copies, waits for them, and re-layouts: 36.5 us -> none  [score_pairs(): jnp.dot(query_rows, normalized_keys.T, preferred_element_type=jnp.float32)]
    ppermute x7 -> x21, waiting for transfers between devices: 10.4 us -> 43.3 us  [exchange(): return lax.ppermute(block, AXES, pairs)]
    ppermute x7 -> x21, starting transfers between devices: 52.8 us -> 22.9 us  [exchange(): return lax.ppermute(block, AXES, pairs)]
  transfers between devices with their start and end apart: 17 -> 22, of which waited for: 16 -> 9; matrix products, arithmetic and copies ran while one was open for 20% -> 3% of each run, Pallas kernels for 0% -> 13%
where the time goes in v2:
time: 130 us; the launch traced here: 129 us
  waiting for transfers between devices  48.9 us (38%)
  Pallas kernels  40.4 us (31%)
  starting transfers between devices  27.1 us (21%)
  local copies, waits for them, and re-layouts  12.4 us (10%)
    ppermute x21, waiting for transfers between devices, exchange(): return lax.ppermute(block, AXES, pairs)  43.3 us
    pallas_call x1, Pallas kernels, local(): pl.pallas_call(rest_kernel, out_shape=shape((2 * SEGMENTS, total), f32),...  23.8 us
    ppermute x21, starting transfers between devices, exchange(): return lax.ppermute(block, AXES, pairs)  22.9 us
    pallas_call x1, Pallas kernels, local(): pl.pallas_call(first_kernel, out_shape=keep, in_specs=[SMEM] + [HBM] * (3...  13.8 us
    unnamed x22, local copies, waits for them, and re-layouts  8.1 us
    all_to_all x1, waiting for transfers between devices, local(): lax.all_to_all(losses, ('x', 'core', 'zh'), split_axis=0, concat_axis=0,...  5.6 us
    all_to_all x1, starting transfers between devices, local(): lax.all_to_all(losses, ('x', 'core', 'zh'), split_axis=0, concat_axis=0,...  4.24 us
    pallas_call x1, Pallas kernels, local(): pl.pallas_call(pack_kernel, out_shape=(packed, packed), in_specs=[SMEM, H...  2.75 us
  transfers between devices with their start and end apart: 22, of which 9 were waited for; matrix products, arithmetic and copies ran while one was open for 3% of the time, Pallas kernels for 13%

profile of v2, /device:TPU:0, one launch (start us, length us, event | category | flops | bytes accessed | tf_op | source)
XLA Modules:
  0.0 129.1 jit_solution(11079834247522087641)
XLA Ops:
  0.0 5.0 %collective-permute-start.15 = (bf16[1024,1024]{1,0:T(8,128)(2,1)}, bf16[1024,1024]{1,0:T(8,128)(2,1)}, u32[]{:S(2)}, u32[]{:S(2)}) collective-permute-start(bf16[1024,1024]{1,0:T(8,128)(2,1)} %bitcast.18), channel_id=1, source_target_pairs={{0,16},{1,17},{2,18},{3,19},{4,20},{5,21},{6,22},{7,23},{16,0},{17... | collective-permute-start | bytes 6291464 | tf_op jit(solution)/shard_map/ppermute | solution.py:35
  5.0 0.0 copy-start
  5.0 0.0 copy-start.2
  5.0 2.4 %dynamic-slice_bitcast_fusion = bf16[512,1024]{1,0:T(8,128)(2,1)} fusion(bf16[1,1024,1024]{2,1,0:T(8,128)(2,1)} %param.10, s32[]{:T(128)S(6)} %select_n.7), kind=kLoop, calls=%fused_computation | loop fusion | bytes 2097156 | tf_op jit(solution)/shard_map/dynamic_slice | solution.py:417
  7.4 0.7 collective-permute-start.17
  8.2 0.6 copy.24
  8.8 0.7 copy.16.cols_ref
  9.5 0.7 stack.23.place_ref
  10.1 2.8 %shard_map.91 = (bf16[144,1152]{1,0:T(8,128)(2,1)}, bf16[144,1152]{1,0:T(8,128)(2,1)}) custom-call(s32[5]{0:T(128)} %stack.23.place_ref, bf16[4,256,1024]{2,1,0:T(8,128)(2,1)} %init_feats.1, bf16[4,2,128,128]{3,2,1,0:T(8,128)(2,1)} %tile_vals.1, s32[4,8,8]{2,1,0:T(8,128)} %send_ref.1, s32[4,8]{1,0:T(4,128)} %count_ref.1, s32[4,8,8]{2,1,0:T(8,128)} %recv_ref.1, ...), custom_call_target="tpu_custom_call" | custom-call | tf_op jit(solution)/shard_map/pallas_call | solution.py:420
  12.9 2.7 %collective-permute-start.3 = (bf16[144,1152]{1,0:T(8,128)(2,1)}, bf16[144,1152]{1,0:T(8,128)(2,1)S(1)}, u32[]{:S(2)}, u32[]{:S(2)}) collective-permute-start(bf16[144,1152]{1,0:T(8,128)(2,1)} %get-tuple-element.17), channel_id=1, source_target_pairs={{0,4},{1,5},{2,6},{3,7},{4,0},{5,1},{6,2},{7,3},{8,12},{9,13},{10,... | collective-permute-start | bytes 995336 | tf_op jit(solution)/shard_map/ppermute | solution.py:35
  15.5 1.6 %collective-permute-start.1 = (bf16[144,1152]{1,0:T(8,128)(2,1)}, bf16[144,1152]{1,0:T(8,128)(2,1)S(1)}, u32[]{:S(2)}, u32[]{:S(2)}) collective-permute-start(bf16[144,1152]{1,0:T(8,128)(2,1)} %get-tuple-element.16.mine_ref), channel_id=1, source_target_pairs={{0,2},{1,3},{2,0},{3,1},{4,6},{5,7},{6,4},{7,5},{8,10},{9,11},{10,... | collective-permute-start | bytes 995336 | tf_op jit(solution)/shard_map/ppermute | solution.py:35
  17.1 1.5 %collective-permute-start = (bf16[144,1152]{1,0:T(8,128)(2,1)}, bf16[144,1152]{1,0:T(8,128)(2,1)S(1)}, u32[]{:S(2)}, u32[]{:S(2)}) collective-permute-start(bf16[144,1152]{1,0:T(8,128)(2,1)} %get-tuple-element.16.mine_ref), channel_id=1, source_target_pairs={{0,1},{1,0},{2,3},{3,2},{4,5},{5,4},{6,7},{7,6},{8,9},{9,8},{10,11... | collective-permute-start | bytes 995336 | tf_op jit(solution)/shard_map/ppermute | solution.py:35
  18.6 13.2 %collective-permute-done.3.rest_3_ = bf16[144,1152]{1,0:T(8,128)(2,1)S(1)} collective-permute-done((bf16[144,1152]{1,0:T(8,128)(2,1)}, bf16[144,1152]{1,0:T(8,128)(2,1)S(1)}, u32[]{:S(2)}, u32[]{:S(2)}) %collective-permute-start.3) | collective-permute-done | bytes 331808 | tf_op jit(solution)/shard_map/ppermute | solution.py:35
  31.8 0.7 collective-permute-start.5
  32.5 0.0 collective-permute-done.1.rest_1_
  32.5 0.0 collective-permute-start.14
  32.5 8.1 %collective-permute-done.15.rest_16_.even_ref = bf16[1024,1024]{1,0:T(8,128)(2,1)} collective-permute-done((bf16[1024,1024]{1,0:T(8,128)(2,1)}, bf16[1024,1024]{1,0:T(8,128)(2,1)}, u32[]{:S(2)}, u32[]{:S(2)}) %collective-permute-start.15) | collective-permute-done | bytes 2097184 | tf_op jit(solution)/shard_map/ppermute | solution.py:35
  40.5 1.4 %collective-permute-start.16 = (bf16[1024,1024]{1,0:T(8,128)(2,1)}, bf16[1024,1024]{1,0:T(8,128)(2,1)S(1)}, u32[]{:S(2)}, u32[]{:S(2)}) collective-permute-start(bf16[1024,1024]{1,0:T(8,128)(2,1)} %collective-permute-done.15.rest_16_.even_ref), channel_id=1, source_target_pairs={{0,8},{1,9},{2,10},{3,11},{4,12},{5,13},{6,14},{7,15},{16,24},{17,... | collective-permute-start | bytes 6291464 | tf_op jit(solution)/shard_map/ppermute | solution.py:35
  42.0 0.0 collective-permute-done.rest_0_
  42.0 2.1 %collective-permute-start.2 = (bf16[144,1152]{1,0:T(8,128)(2,1)S(1)}, bf16[144,1152]{1,0:T(8,128)(2,1)S(1)}, u32[]{:S(2)}, u32[]{:S(2)}) collective-permute-start(bf16[144,1152]{1,0:T(8,128)(2,1)S(1)} %collective-permute-done.1.rest_1_), channel_id=1, source_target_pairs={{0,1},{1,0},{2,3},{3,2},{4,5},{5,4},{6,7},{7,6},{8,9},{9,8},{10,11... | collective-permute-start | bytes 995336 | tf_op jit(solution)/shard_map/ppermute | solution.py:35
  44.1 0.0 collective-permute-done.5.rest_5_
  44.1 0.1 collective-permute-start.4
  44.2 0.0 collective-permute-done.17.odd_ref
  44.2 0.7 collective-permute-start.18
  44.9 5.4 %collective-permute-done.2.rest_2_ = bf16[144,1152]{1,0:T(8,128)(2,1)S(1)} collective-permute-done((bf16[144,1152]{1,0:T(8,128)(2,1)S(1)}, bf16[144,1152]{1,0:T(8,128)(2,1)S(1)}, u32[]{:S(2)}, u32[]{:S(2)}) %collective-permute-start.2) | collective-permute-done | bytes 331808 | tf_op jit(solution)/shard_map/ppermute | solution.py:35
  50.3 0.0 collective-permute-start.8
  50.3 3.6 %collective-permute-done.4.rest_4_ = bf16[144,1152]{1,0:T(8,128)(2,1)S(1)} collective-permute-done((bf16[144,1152]{1,0:T(8,128)(2,1)S(1)}, bf16[144,1152]{1,0:T(8,128)(2,1)S(1)}, u32[]{:S(2)}, u32[]{:S(2)}) %collective-permute-start.4) | collective-permute-done | bytes 331808 | tf_op jit(solution)/shard_map/ppermute | solution.py:35
  53.8 0.5 collective-permute-start.7
  54.3 1.1 collective-permute-done.10.rest_10_
  55.5 1.5 %collective-permute-start.6 = (bf16[144,1152]{1,0:T(8,128)(2,1)S(1)}, bf16[144,1152]{1,0:T(8,128)(2,1)S(1)}, u32[]{:S(2)}, u32[]{:S(2)}) collective-permute-start(bf16[144,1152]{1,0:T(8,128)(2,1)S(1)} %collective-permute-done.5.rest_5_), channel_id=1, source_target_pairs={{0,1},{1,0},{2,3},{3,2},{4,5},{5,4},{6,7},{7,6},{8,9},{9,8},{10,11... | collective-permute-start | bytes 995336 | tf_op jit(solution)/shard_map/ppermute | solution.py:35
  57.0 8.3 %collective-permute-done.6.rest_6_ = bf16[144,1152]{1,0:T(8,128)(2,1)S(1)} collective-permute-done((bf16[144,1152]{1,0:T(8,128)(2,1)S(1)}, bf16[144,1152]{1,0:T(8,128)(2,1)S(1)}, u32[]{:S(2)}, u32[]{:S(2)}) %collective-permute-start.6) | collective-permute-done | bytes 331808 | tf_op jit(solution)/shard_map/ppermute | solution.py:35
  65.3 0.5 collective-permute-start.11
  65.8 1.1 collective-permute-done.9.rest_9_
  66.9 1.3 collective-permute-start.19
  68.2 1.3 %collective-permute-start.20 = (bf16[512,1024]{1,0:T(8,128)(2,1)S(1)}, bf16[512,1024]{1,0:T(8,128)(2,1)S(1)}, u32[]{:S(2)}, u32[]{:S(2)}) collective-permute-start(bf16[512,1024]{1,0:T(8,128)(2,1)S(1)} %collective-permute-done.18.odd_other_ref), channel_id=1, source_target_pairs={{8,0},{9,1},{10,2},{11,3},{12,4},{13,5},{14,6},{15,7},{24,16},{25,... | collective-permute-start | bytes 3145736 | tf_op jit(solution)/shard_map/ppermute | solution.py:35
  69.5 1.3 %collective-permute-start.13 = (bf16[144,1152]{1,0:T(8,128)(2,1)S(1)}, bf16[144,1152]{1,0:T(8,128)(2,1)S(1)}, u32[]{:S(2)}, u32[]{:S(2)}) collective-permute-start(bf16[144,1152]{1,0:T(8,128)(2,1)S(1)} %collective-permute-done.6.rest_6_), channel_id=1, source_target_pairs={{0,8},{1,9},{2,10},{3,11},{4,12},{5,13},{6,14},{7,15},{8,0},{9,1},... | collective-permute-start | bytes 995336 | tf_op jit(solution)/shard_map/ppermute | solution.py:35
  70.9 2.6 %collective-permute-done.13.rest_13_ = bf16[144,1152]{1,0:T(8,128)(2,1)S(1)} collective-permute-done((bf16[144,1152]{1,0:T(8,128)(2,1)S(1)}, bf16[144,1152]{1,0:T(8,128)(2,1)S(1)}, u32[]{:S(2)}, u32[]{:S(2)}) %collective-permute-start.13) | collective-permute-done | bytes 331808 | tf_op jit(solution)/shard_map/ppermute | solution.py:35
  73.5 1.3 %copy-done.4 = bf16[1024,1024]{1,0:T(8,128)(2,1)} copy-done((bf16[1024,1024]{1,0:T(8,128)(2,1)}, bf16[1024,1024]{1,0:T(8,128)(2,1)S(1)}, u32[]{:S(2)}) %copy-start.4) | copy-done | bytes 2097176
  74.8 1.4 %copy-done.9 = bf16[1024,1024]{1,0:T(8,128)(2,1)} copy-done((bf16[1024,1024]{1,0:T(8,128)(2,1)}, bf16[1024,1024]{1,0:T(8,128)(2,1)S(1)}, u32[]{:S(2)}) %copy-start.9) | copy-done | bytes 2097176
  76.1 1.6 %copy-done.1 = bf16[1,1024,1024]{2,1,0:T(8,128)(2,1)S(1)} copy-done((bf16[1,1024,1024]{2,1,0:T(8,128)(2,1)S(1)}, bf16[1,1024,1024]{2,1,0:T(8,128)(2,1)}, u32[]{:S(2)}) %copy-start.1) | copy-done | bytes 2097176
  77.7 1.0 copy-done.6
  78.7 13.8 %shard_map.92 = (bf16[8,256,1024]{2,1,0:T(8,128)(2,1)}, bf16[16,128,256]{2,1,0:T(8,128)(2,1)S(1)}, bf16[8,112,256]{2,1,0:T(8,128)(2,1)S(1)}, s32[8,128]{1,0:T(8,...) custom-call(s32[5]{0:T(128)S(1)} %copy-done.3, ...), custom_call_target="tpu_custom_call" | custom-call | flops 4294967296 | bytes 16777216 | tf_op jit(solution)/shard_map/pallas_call | solution.py:460
  92.5 1.6 %copy-done.5 = bf16[1024,1024]{1,0:T(8,128)(2,1)S(1)} copy-done((bf16[1024,1024]{1,0:T(8,128)(2,1)S(1)}, bf16[1024,1024]{1,0:T(8,128)(2,1)}, u32[]{:S(2)}) %copy-start.5) | copy-done | bytes 2097176
  94.1 23.8 %shard_map.93 = f32[8,384]{1,0:T(8,128)S(1)} custom-call(s32[5]{0:T(128)S(1)} %copy-done.3, s32[8,128]{1,0:T(8,128)S(1)} %get-tuple-element.18.cols_ref, bf16[8,256,1024]{2,1,0:T(8,128)(2,1)} %get-tuple-element.19.init_ref, bf16[16,128,256]{2,1,0:T(8,128)(2,1)S(1)} %get-tuple-element.20.spread_ref, bf16[8,112,256]{2,1,0:T(8,128)(2,1)S(1)} %get-tuple-element.21.pick_ref, ...), custom_call_target="tpu_custom_call" | custom-call | flops 12884901888 | bytes 16777216 | tf_op jit(solution)/shard_map/pallas_call | solution.py:482
  118.0 0.6 copy.17
  118.6 4.2 %all-to-all-start = ((f32[8,1,384]{2,1,0:T(1,128)}), f32[8,1,384]{2,1,0:T(1,128)S(1)}, u32[]{:S(2)}, u32[]{:S(2)}) async-start(f32[8,1,384]{2,1,0:T(1,128)} %copy.17), calls=%async_computation | async-start | bytes 24576 | tf_op jit(solution)/shard_map/all_to_all | solution.py:503
  122.8 5.6 %all-to-all-done = f32[8,1,384]{2,1,0:T(1,128)S(1)} async-done(((f32[8,1,384]{2,1,0:T(1,128)}), f32[8,1,384]{2,1,0:T(1,128)S(1)}, u32[]{:S(2)}, u32[]{:S(2)}) %all-to-all-start) | async-done | bytes 12320 | tf_op jit(solution)/shard_map/all_to_all | solution.py:503
  128.5 0.6 reshape.11
  (29 shorter events, 0.1 us)
Async XLA Ops:
  0.0 8.2 %copy-start.7 = (s32[4,256,1]{1,2,0:T(1,128)S(1)}, s32[4,256,1]{1,2,0:T(1,128)}, u32[]{:S(2)}) copy-start(s32[4,256,1]{1,2,0:T(1,128)} %param.17) | copy-start | bytes 12292
  0.0 8.8 %copy-start.8 = (s32[4,2]{0,1:T(2,128)S(1)}, s32[4,2]{0,1:T(2,128)}, u32[]{:S(2)}) copy-start(s32[4,2]{0,1:T(2,128)} %param.11) | copy-start | bytes 100
  0.0 40.5 %collective-permute-start.15 = (bf16[1024,1024]{1,0:T(8,128)(2,1)}, bf16[1024,1024]{1,0:T(8,128)(2,1)}, u32[]{:S(2)}, u32[]{:S(2)}) collective-permute-start(bf16[1024,1024]{1,0:T(8,128)(2,1)} %bitcast.18), channel_id=1, source_target_pairs={{0,16},{1,17},{2,18},{3,19},{4,20},{5,21},{6,22},{7,23},{16,0},{17... | collective-permute-start | bytes 6291464 | tf_op jit(solution)/shard_map/ppermute | solution.py:35
  5.0 71.1 %copy-start = (bf16[4,256,1024]{2,1,0:T(8,128)(2,1)S(1)}, bf16[4,256,1024]{2,1,0:T(8,128)(2,1)}, u32[]{:S(2)}) copy-start(bf16[4,256,1024]{2,1,0:T(8,128)(2,1)} %init_feats.1) | copy-start | bytes 6291460
  5.0 71.1 %copy-start.2 = (bf16[4,2,128,128]{3,2,1,0:T(8,128)(2,1)S(1)}, bf16[4,2,128,128]{3,2,1,0:T(8,128)(2,1)}, u32[]{:S(2)}) copy-start(bf16[4,2,128,128]{3,2,1,0:T(8,128)(2,1)} %tile_vals.1) | copy-start | bytes 786436
  7.4 36.7 %collective-permute-start.17 = (bf16[512,1024]{1,0:T(8,128)(2,1)}, bf16[512,1024]{1,0:T(8,128)(2,1)S(1)}, u32[]{:S(2)}, u32[]{:S(2)}) collective-permute-start(bf16[512,1024]{1,0:T(8,128)(2,1)} %dynamic-slice_bitcast_fusion), channel_id=1, source_target_pairs={{8,24},{9,25},{10,26},{11,27},{12,28},{13,29},{14,30},{15,31},{24,... | collective-permute-start | bytes 3145736 | tf_op jit(solution)/shard_map/ppermute | solution.py:35
  10.1 66.0 %copy-start.3 = (s32[5]{0:T(128)S(1)}, s32[5]{0:T(128)}, u32[]{:S(2)}) copy-start(s32[5]{0:T(128)} %stack.23.place_ref) | copy-start | bytes 64
  12.9 18.9 %collective-permute-start.3 = (bf16[144,1152]{1,0:T(8,128)(2,1)}, bf16[144,1152]{1,0:T(8,128)(2,1)S(1)}, u32[]{:S(2)}, u32[]{:S(2)}) collective-permute-start(bf16[144,1152]{1,0:T(8,128)(2,1)} %get-tuple-element.17), channel_id=1, source_target_pairs={{0,4},{1,5},{2,6},{3,7},{4,0},{5,1},{6,2},{7,3},{8,12},{9,13},{10,... | collective-permute-start | bytes 995336 | tf_op jit(solution)/shard_map/ppermute | solution.py:35
  15.5 16.9 %collective-permute-start.1 = (bf16[144,1152]{1,0:T(8,128)(2,1)}, bf16[144,1152]{1,0:T(8,128)(2,1)S(1)}, u32[]{:S(2)}, u32[]{:S(2)}) collective-permute-start(bf16[144,1152]{1,0:T(8,128)(2,1)} %get-tuple-element.16.mine_ref), channel_id=1, source_target_pairs={{0,2},{1,3},{2,0},{3,1},{4,6},{5,7},{6,4},{7,5},{8,10},{9,11},{10,... | collective-permute-start | bytes 995336 | tf_op jit(solution)/shard_map/ppermute | solution.py:35
  17.1 24.8 %collective-permute-start = (bf16[144,1152]{1,0:T(8,128)(2,1)}, bf16[144,1152]{1,0:T(8,128)(2,1)S(1)}, u32[]{:S(2)}, u32[]{:S(2)}) collective-permute-start(bf16[144,1152]{1,0:T(8,128)(2,1)} %get-tuple-element.16.mine_ref), channel_id=1, source_target_pairs={{0,1},{1,0},{2,3},{3,2},{4,5},{5,4},{6,7},{7,6},{8,9},{9,8},{10,11... | collective-permute-start | bytes 995336 | tf_op jit(solution)/shard_map/ppermute | solution.py:35
  31.8 12.3 %collective-permute-start.5 = (bf16[144,1152]{1,0:T(8,128)(2,1)S(1)}, bf16[144,1152]{1,0:T(8,128)(2,1)S(1)}, u32[]{:S(2)}, u32[]{:S(2)}) collective-permute-start(bf16[144,1152]{1,0:T(8,128)(2,1)S(1)} %collective-permute-done.3.rest_3_), channel_id=1, source_target_pairs={{0,2},{1,3},{2,0},{3,1},{4,6},{5,7},{6,4},{7,5},{8,10},{9,11},{10,... | collective-permute-start | bytes 995336 | tf_op jit(solution)/shard_map/ppermute | solution.py:35
  32.5 41.0 %collective-permute-start.14 = (bf16[1024,1024]{1,0:T(8,128)(2,1)}, bf16[1024,1024]{1,0:T(8,128)(2,1)S(1)}, u32[]{:S(2)}, u32[]{:S(2)}) collective-permute-start(bf16[1024,1024]{1,0:T(8,128)(2,1)} %bitcast.19), channel_id=1, source_target_pairs={{0,8},{1,9},{2,10},{3,11},{4,12},{5,13},{6,14},{7,15},{8,0},{9,1},... | collective-permute-start | bytes 6291464 | tf_op jit(solution)/shard_map/ppermute | solution.py:35
  40.5 32.9 %collective-permute-start.16 = (bf16[1024,1024]{1,0:T(8,128)(2,1)}, bf16[1024,1024]{1,0:T(8,128)(2,1)S(1)}, u32[]{:S(2)}, u32[]{:S(2)}) collective-permute-start(bf16[1024,1024]{1,0:T(8,128)(2,1)} %collective-permute-done.15.rest_16_.even_ref), channel_id=1, source_target_pairs={{0,8},{1,9},{2,10},{3,11},{4,12},{5,13},{6,14},{7,15},{16,24},{17,... | collective-permute-start | bytes 6291464 | tf_op jit(solution)/shard_map/ppermute | solution.py:35
  42.0 8.3 %collective-permute-start.2 = (bf16[144,1152]{1,0:T(8,128)(2,1)S(1)}, bf16[144,1152]{1,0:T(8,128)(2,1)S(1)}, u32[]{:S(2)}, u32[]{:S(2)}) collective-permute-start(bf16[144,1152]{1,0:T(8,128)(2,1)S(1)} %collective-permute-done.1.rest_1_), channel_id=1, source_target_pairs={{0,1},{1,0},{2,3},{3,2},{4,5},{5,4},{6,7},{7,6},{8,9},{9,8},{10,11... | collective-permute-start | bytes 995336 | tf_op jit(solution)/shard_map/ppermute | solution.py:35
  44.1 9.7 %collective-permute-start.4 = (bf16[144,1152]{1,0:T(8,128)(2,1)S(1)}, bf16[144,1152]{1,0:T(8,128)(2,1)S(1)}, u32[]{:S(2)}, u32[]{:S(2)}) collective-permute-start(bf16[144,1152]{1,0:T(8,128)(2,1)S(1)} %collective-permute-done.3.rest_3_), channel_id=1, source_target_pairs={{0,1},{1,0},{2,3},{3,2},{4,5},{5,4},{6,7},{7,6},{8,9},{9,8},{10,11... | collective-permute-start | bytes 995336 | tf_op jit(solution)/shard_map/ppermute | solution.py:35
  44.2 24.1 %collective-permute-start.18 = (bf16[512,1024]{1,0:T(8,128)(2,1)S(1)}, bf16[512,1024]{1,0:T(8,128)(2,1)S(1)}, u32[]{:S(2)}, u32[]{:S(2)}) collective-permute-start(bf16[512,1024]{1,0:T(8,128)(2,1)S(1)} %collective-permute-done.17.odd_ref), channel_id=1, source_target_pairs={{8,10},{9,11},{10,8},{11,9},{12,14},{13,15},{14,12},{15,13},{24,26... | collective-permute-start | bytes 3145736 | tf_op jit(solution)/shard_map/ppermute | solution.py:35
  50.3 3.6 %collective-permute-start.8 = (bf16[144,1152]{1,0:T(8,128)(2,1)S(1)}, bf16[144,1152]{1,0:T(8,128)(2,1)S(1)}, u32[]{:S(2)}, u32[]{:S(2)}) collective-permute-start(bf16[144,1152]{1,0:T(8,128)(2,1)S(1)} %collective-permute-done.1.rest_1_), channel_id=1, source_target_pairs={{0,8},{1,9},{2,10},{3,11},{4,12},{5,13},{6,14},{7,15},{8,0},{9,1},... | collective-permute-start | bytes 995336 | tf_op jit(solution)/shard_map/ppermute | solution.py:35
  53.8 1.6 %collective-permute-start.10 = (bf16[144,1152]{1,0:T(8,128)(2,1)S(1)}, bf16[144,1152]{1,0:T(8,128)(2,1)S(1)}, u32[]{:S(2)}, u32[]{:S(2)}) collective-permute-start(bf16[144,1152]{1,0:T(8,128)(2,1)S(1)} %collective-permute-done.3.rest_3_), channel_id=1, source_target_pairs={{0,8},{1,9},{2,10},{3,11},{4,12},{5,13},{6,14},{7,15},{8,0},{9,1},... | collective-permute-start | bytes 995336 | tf_op jit(solution)/shard_map/ppermute | solution.py:35
  53.8 3.2 %collective-permute-start.7 = (bf16[144,1152]{1,0:T(8,128)(2,1)S(1)}, bf16[144,1152]{1,0:T(8,128)(2,1)S(1)}, u32[]{:S(2)}, u32[]{:S(2)}) collective-permute-start(bf16[144,1152]{1,0:T(8,128)(2,1)S(1)} %collective-permute-done.rest_0_), channel_id=1, source_target_pairs={{0,8},{1,9},{2,10},{3,11},{4,12},{5,13},{6,14},{7,15},{8,0},{9,1},... | collective-permute-start | bytes 995336 | tf_op jit(solution)/shard_map/ppermute | solution.py:35
  55.5 9.8 %collective-permute-start.6 = (bf16[144,1152]{1,0:T(8,128)(2,1)S(1)}, bf16[144,1152]{1,0:T(8,128)(2,1)S(1)}, u32[]{:S(2)}, u32[]{:S(2)}) collective-permute-start(bf16[144,1152]{1,0:T(8,128)(2,1)S(1)} %collective-permute-done.5.rest_5_), channel_id=1, source_target_pairs={{0,1},{1,0},{2,3},{3,2},{4,5},{5,4},{6,7},{7,6},{8,9},{9,8},{10,11... | collective-permute-start | bytes 995336 | tf_op jit(solution)/shard_map/ppermute | solution.py:35
  57.0 8.3 %collective-permute-start.12 = (bf16[144,1152]{1,0:T(8,128)(2,1)S(1)}, bf16[144,1152]{1,0:T(8,128)(2,1)S(1)}, u32[]{:S(2)}, u32[]{:S(2)}) collective-permute-start(bf16[144,1152]{1,0:T(8,128)(2,1)S(1)} %collective-permute-done.5.rest_5_), channel_id=1, source_target_pairs={{0,8},{1,9},{2,10},{3,11},{4,12},{5,13},{6,14},{7,15},{8,0},{9,1},... | collective-permute-start | bytes 995336 | tf_op jit(solution)/shard_map/ppermute | solution.py:35
  65.3 1.6 %collective-permute-start.9 = (bf16[144,1152]{1,0:T(8,128)(2,1)S(1)}, bf16[144,1152]{1,0:T(8,128)(2,1)S(1)}, u32[]{:S(2)}, u32[]{:S(2)}) collective-permute-start(bf16[144,1152]{1,0:T(8,128)(2,1)S(1)} %collective-permute-done.2.rest_2_), channel_id=1, source_target_pairs={{0,8},{1,9},{2,10},{3,11},{4,12},{5,13},{6,14},{7,15},{8,0},{9,1},... | collective-permute-start | bytes 995336 | tf_op jit(solution)/shard_map/ppermute | solution.py:35
  65.3 4.2 %collective-permute-start.11 = (bf16[144,1152]{1,0:T(8,128)(2,1)S(1)}, bf16[144,1152]{1,0:T(8,128)(2,1)S(1)}, u32[]{:S(2)}, u32[]{:S(2)}) collective-permute-start(bf16[144,1152]{1,0:T(8,128)(2,1)S(1)} %collective-permute-done.4.rest_4_), channel_id=1, source_target_pairs={{0,8},{1,9},{2,10},{3,11},{4,12},{5,13},{6,14},{7,15},{8,0},{9,1},... | collective-permute-start | bytes 995336 | tf_op jit(solution)/shard_map/ppermute | solution.py:35
  66.9 25.6 %collective-permute-start.19 = (bf16[512,1024]{1,0:T(8,128)(2,1)S(1)}, bf16[512,1024]{1,0:T(8,128)(2,1)S(1)}, u32[]{:S(2)}, u32[]{:S(2)}) collective-permute-start(bf16[512,1024]{1,0:T(8,128)(2,1)S(1)} %collective-permute-done.17.odd_ref), channel_id=1, source_target_pairs={{8,0},{9,1},{10,2},{11,3},{12,4},{13,5},{14,6},{15,7},{24,16},{25,... | collective-permute-start | bytes 3145736 | tf_op jit(solution)/shard_map/ppermute | solution.py:35
  68.2 24.3 %collective-permute-start.20 = (bf16[512,1024]{1,0:T(8,128)(2,1)S(1)}, bf16[512,1024]{1,0:T(8,128)(2,1)S(1)}, u32[]{:S(2)}, u32[]{:S(2)}) collective-permute-start(bf16[512,1024]{1,0:T(8,128)(2,1)S(1)} %collective-permute-done.18.odd_other_ref), channel_id=1, source_target_pairs={{8,0},{9,1},{10,2},{11,3},{12,4},{13,5},{14,6},{15,7},{24,16},{25,... | collective-permute-start | bytes 3145736 | tf_op jit(solution)/shard_map/ppermute | solution.py:35
  69.5 3.9 %collective-permute-start.13 = (bf16[144,1152]{1,0:T(8,128)(2,1)S(1)}, bf16[144,1152]{1,0:T(8,128)(2,1)S(1)}, u32[]{:S(2)}, u32[]{:S(2)}) collective-permute-start(bf16[144,1152]{1,0:T(8,128)(2,1)S(1)} %collective-permute-done.6.rest_6_), channel_id=1, source_target_pairs={{0,8},{1,9},{2,10},{3,11},{4,12},{5,13},{6,14},{7,15},{8,0},{9,1},... | collective-permute-start | bytes 995336 | tf_op jit(solution)/shard_map/ppermute | solution.py:35
  73.5 1.3 %copy-start.4 = (bf16[1024,1024]{1,0:T(8,128)(2,1)}, bf16[1024,1024]{1,0:T(8,128)(2,1)S(1)}, u32[]{:S(2)}) copy-start(bf16[1024,1024]{1,0:T(8,128)(2,1)S(1)} %collective-permute-done.14.rest_15_.flip_ref) | copy-start | bytes 6291460
  74.8 1.4 %copy-start.9 = (bf16[1024,1024]{1,0:T(8,128)(2,1)}, bf16[1024,1024]{1,0:T(8,128)(2,1)S(1)}, u32[]{:S(2)}) copy-start(bf16[1024,1024]{1,0:T(8,128)(2,1)S(1)} %collective-permute-done.16.rest_17_.even_flip_ref) | copy-start | bytes 6291460
  76.1 1.6 %copy-start.1 = (bf16[1,1024,1024]{2,1,0:T(8,128)(2,1)S(1)}, bf16[1,1024,1024]{2,1,0:T(8,128)(2,1)}, u32[]{:S(2)}) copy-start(bf16[1,1024,1024]{2,1,0:T(8,128)(2,1)} %param.10) | copy-start | bytes 6291460
  77.7 1.0 copy-start.6
  92.5 1.6 %copy-start.5 = (bf16[1024,1024]{1,0:T(8,128)(2,1)S(1)}, bf16[1024,1024]{1,0:T(8,128)(2,1)}, u32[]{:S(2)}) copy-start(bf16[1024,1024]{1,0:T(8,128)(2,1)} %copy-done.4) | copy-start | bytes 6291460
  118.6 9.8 %all-to-all-start = ((f32[8,1,384]{2,1,0:T(1,128)}), f32[8,1,384]{2,1,0:T(1,128)S(1)}, u32[]{:S(2)}, u32[]{:S(2)}) async-start(f32[8,1,384]{2,1,0:T(1,128)} %copy.17), calls=%async_computation | async-start | bytes 24576 | tf_op jit(solution)/shard_map/all_to_all | solution.py:503

commit v3 on v2

--- a/solution.py
+++ b/solution.py
@@ -22,13 +22,14 @@
 SEND, RECV, WEIGHT, COLS, OWNER = 0, 128, 256, 512, 640
 
 
-def exchange(block, axis, core=None):
+ARRIVALS = {1: (0, 0), 2: (0, 1), 4: (0, 2), 3: (1, 0), 5: (1, 1), 6: (2, 0), 7: (3, 0)}
+
+
+def exchange(block, *across, core=None):
     sizes = [range(lax.axis_size(name)) for name in AXES]
-    at = AXES.index(axis)
     pairs = []
     for index, here in enumerate(itertools.product(*sizes)):
-        there = list(here)
-        there[at] = 1 - there[at]
+        there = [1 - at if name in across else at for name, at in zip(AXES, here, strict=True)]
         target = functools.reduce(lambda total, digit: total * 2 + digit, there, 0)
         if core is None or here[1] == core:
             pairs.append((index, target))
@@ -51,13 +52,14 @@
 
 
 def pack_kernel(
-    place_ref, init_ref, tiles_ref, send_ref, count_ref, recv_ref, weight_ref, cols_ref, owner_ref,
+    init_ref, tiles_ref, send_ref, count_ref, recv_ref, weight_ref, cols_ref, owner_ref,
     mine_ref, other_ref, small, sems,
 ):
-    x, core, zh = place_ref[0], place_ref[1], place_ref[2]
+    x, core, zh = [lax.axis_index(name) for name in AXES[:3]]
     half, width = mine_ref.shape[0] - SMALL_ROWS, init_ref.shape[-1]
     peers, slots = send_ref.shape[1:]
-    tiles, rows = cols_ref.shape[-1], owner_ref.shape[-1]
+    tiles, rows = cols_ref.shape[0], owner_ref.shape[-1]
+    lane = lax.broadcasted_iota(jnp.int32, (1, LANES), 1)
     first = pl.multiple_of(core * half, half)
     spans = (zh * 2 + x, (1 - zh) * 2 + x)
     copies = []
@@ -86,8 +88,11 @@
         small[i, 0:slots, SEND : SEND + peers] = jnp.where(used, sends, float(rows))
         small[i, 0:slots, RECV : RECV + peers] = turned(recv_ref[span].astype(jnp.float32))
         small[i, 0:slots, WEIGHT : WEIGHT + peers] = turned(weight_ref[span].astype(jnp.float32))
-        small[i, 0:1, COLS : COLS + tiles] = cols_ref[pl.ds(span, 1), :].astype(jnp.float32)
-        small[i, 0:1, OWNER : OWNER + rows] = owner_ref[pl.ds(span, 1), :].astype(jnp.float32)
+        columns = jnp.zeros((1, LANES), jnp.int32)
+        for t in range(tiles):
+            columns = jnp.where(lane == t, cols_ref[t, span], columns)
+        small[i, 0:1, COLS : COLS + LANES] = columns.astype(jnp.float32)
+        small[i, 0:1, OWNER : OWNER + rows] = owner_ref[span].astype(jnp.float32)
         out_ref[half : half + SMALL_ROWS, :] = small[i].astype(jnp.bfloat16)
     for copy in copies:
         copy.wait()
@@ -171,14 +176,13 @@
 
 
 def first_kernel(
-    place_ref, init_feats, tile_vals, mine_ref, *rest
+    init_feats, tile_vals, mine_ref, *rest
 ):
     blocks = VERTS
-    nets, flips = rest[: blocks - 1], rest[blocks - 1 : 2 * blocks - 2]
-    weights = rest[2 * blocks - 2 : 2 * blocks + 2]
+    nets, flips, weights = rest[:4], rest[4:8], rest[8:12]
     (init_ref, spread_ref, pick_ref, cols_out, live_ref, keys, hidden, boundary, loss_ref,
-     boundary0, anchors, small, weight, cols_ref, sems, weight_sems) = rest[2 * blocks + 2 :]
-    x, core, zh, zl, y = [place_ref[i] for i in range(5)]
+     boundary0, anchors, small, weight, cols_ref, sems, weight_sems) = rest[12:]
+    x, core, zh, zl, y = [lax.axis_index(name) for name in AXES]
     vert = zh * 4 + zl * 2 + y
     rows, width = init_ref.shape[1:]
     half = rows // 2
@@ -212,24 +216,26 @@
         at += 1
     for k in range(1, blocks):
         block = vert ^ k
-        for part, source in ((core, nets[k - 1]), (1 - core, flips[k - 1])):
+        group, index = ARRIVALS[k]
+        base = index * (half + SMALL_ROWS)
+        for part, source in ((core, nets[group]), (1 - core, flips[group])):
             first = pl.multiple_of(part * half, half)
             copies.append(
                 start(
-                    source.at[pl.ds(0, half), pl.ds(0, width)],
+                    source.at[pl.ds(base, half), pl.ds(0, width)],
                     init_ref.at[block, pl.ds(first, half), :],
                     sems.at[at],
                 )
             )
             copies.append(
                 start(
-                    source.at[pl.ds(0, half), pl.ds(width, tile)],
+                    source.at[pl.ds(base, half), pl.ds(width, tile)],
                     spread_ref.at[block * tiles + part, :, pl.ds(0, tile)],
                     sems.at[at + 1],
                 )
             )
             at += 2
-        source = nets[k - 1].at[pl.ds(half, SMALL_ROWS), :]
+        source = nets[group].at[pl.ds(base + half, SMALL_ROWS), :]
         copies.append(start(source, small.at[block], sems.at[at]))
         at += 1
     for copy in copies:
@@ -298,12 +304,12 @@
 
 
 def rest_kernel(
-    place_ref, cols_ref, init_ref, spread_ref, pick_ref, live_ref, keys, hidden, boundary,
+    cols_ref, init_ref, spread_ref, pick_ref, live_ref, keys, hidden, boundary,
     loss0_ref, own_ref, flip_ref, even_ref, even_flip_ref, odd_ref, odd_other_ref,
     odd_flip_ref, odd_other_flip_ref, loss_ref, held, border_held, anchors, last, weight,
     weight_sems,
 ):
-    x, core, zl = place_ref[0], place_ref[1], place_ref[3]
+    x, core, zl = [lax.axis_index(name) for name in ("x", "core", "zl")]
     layers = SEGMENTS
     blocks = init_ref.shape[0]
     slots = keys.shape[0] // blocks
@@ -353,7 +359,7 @@
 
     def report(layer, losses):
         for copy in range(2):
-            loss_ref[2 * layer + copy : 2 * layer + copy + 1, :] = losses
+            loss_ref[2 * layer + copy] = losses
 
     report(0, loss0_ref[...])
     source, border_in = hidden, boundary
@@ -387,7 +393,8 @@
 VMEM = pl.BlockSpec(memory_space=pltpu.VMEM)
 SMEM = pl.BlockSpec(memory_space=pltpu.SMEM)
 HBM = pl.BlockSpec(memory_space=pltpu.HBM)
-VMEM_LIMIT = 40 * 1024 * 1024
+FIRST_VMEM = 20 * 1024 * 1024
+REST_VMEM = 26 * 1024 * 1024
 
 
 def local(
@@ -412,38 +419,41 @@
     bf16, f32 = jnp.bfloat16, jnp.float32
     shape = jax.ShapeDtypeStruct
     zh, zl = lax.axis_index("zh"), lax.axis_index("zl")
-    place = jnp.stack([lax.axis_index(name) for name in AXES]).astype(jnp.int32)
     own = layer_weight[0]
-    odd_part = lax.dynamic_slice(own, (zl * (width // 2), 0), (width // 2, width))
 
     packed = shape((half + SMALL_ROWS, width + tile), bf16)
     mine, other = pl.pallas_call(
         pack_kernel,
         out_shape=(packed, packed),
-        in_specs=[SMEM, HBM, HBM] + [VMEM] * 6,
+        in_specs=[HBM, HBM] + [VMEM] * 4 + [SMEM, VMEM],
         out_specs=(VMEM, VMEM),
         scratch_shapes=[
             pltpu.VMEM((2, SMALL_ROWS, width + tile), f32),
             pltpu.SemaphoreType.DMA((4,)),
         ],
     )(
-        place, init_feats, tile_vals, send_rows, send_count, recv_rows, recv_weight, tile_cols,
-        pair_owner[:, :, 0],
-    )
-
+        init_feats, tile_vals, send_rows, send_count, recv_rows, recv_weight, tile_cols.T,
+        jnp.swapaxes(pair_owner, 1, 2),
+    )
+
+    own, mine, other = lax.optimization_barrier((own, mine, other))
+    net4, net2, net1 = exchange(other, "zh"), exchange(mine, "zl"), exchange(mine, "y")
     even = exchange(own, "x", core=0)
+    odd_part = lax.dynamic_slice(own, (zl * (width // 2), 0), (width // 2, width))
     odd = exchange(odd_part, "x", core=1)
-    net = {4: exchange(other, "zh"), 2: exchange(mine, "zl"), 1: exchange(mine, "y")}
-    net[3] = exchange(net[2], "y")
-    net[6] = exchange(net[4], "zl")
-    net[5] = exchange(net[4], "y")
-    net[7] = exchange(net[6], "y")
+    net1, net2, net4 = lax.optimization_barrier((net1, net2, net4))
+    net6 = exchange(net4, "zl")
+    net35 = exchange(jnp.concatenate([net2, net4]), "y")
+    net124 = jnp.concatenate([net1, net2, net4])
+    flip124 = exchange(net124, "core")
+    net7 = exchange(net6, "y")
     flip = exchange(own, "core")
-    flips = {k: exchange(net[k], "core") for k in net}
+    net35, flip124, net6, odd, even = lax.optimization_barrier((net35, flip124, net6, odd, even))
+    flip35, flip6 = exchange(net35, "core"), exchange(net6, "core")
+    even_flip = exchange(even, "core", core=0)
     odd_other = exchange(odd, "zl", core=1)
-    odd_flip = exchange(odd, "core", core=1)
-    even_flip = exchange(even, "core", core=0)
-    odd_other_flip = exchange(odd_other, "core", core=1)
+    net7, flip35, flip6, even_flip = lax.optimization_barrier((net7, flip35, flip6, even_flip))
+    flip7 = exchange(net7, "core")
 
     keep = [
         shape((blocks, rows, width), bf16),
@@ -456,11 +466,10 @@
         shape((blocks, border, width), f32),
         shape((1, total), f32),
     ]
-    order = range(1, blocks)
     init, spread, pick, cols, live, keys, hidden, boundary, loss0 = pl.pallas_call(
         first_kernel,
         out_shape=keep,
-        in_specs=[SMEM] + [HBM] * (3 + 2 * (blocks - 1) + 4),
+        in_specs=[HBM] * 15,
         out_specs=[VMEM] * len(keep),
         scratch_shapes=[
             pltpu.VMEM((blocks, border, width), f32),
@@ -471,18 +480,21 @@
             pltpu.SemaphoreType.DMA((8 * blocks,)),
             pltpu.SemaphoreType.DMA((1,)),
         ],
-        compiler_params=pltpu.CompilerParams(vmem_limit_bytes=VMEM_LIMIT),
+        compiler_params=pltpu.CompilerParams(vmem_limit_bytes=FIRST_VMEM),
         cost_estimate=pl.CostEstimate(
             flops=2 * blocks * rows * width * width, bytes_accessed=1 << 24, transcendentals=0
         ),
     )(
-        place, init_feats, tile_vals, mine, *[net[k] for k in order], *[flips[k] for k in order],
+        init_feats, tile_vals, mine, net124, net35, net6, net7, flip124, flip35, flip6, flip7,
         own, flip, even, even_flip,
     )
+    odd, odd_other, loss0 = lax.optimization_barrier((odd, odd_other, loss0))
+    odd_flip = exchange(odd, "core", core=1)
+    odd_other_flip = exchange(odd_other, "core", core=1)
     losses = pl.pallas_call(
         rest_kernel,
-        out_shape=shape((2 * SEGMENTS, total), f32),
-        in_specs=[SMEM, SMEM] + [VMEM] * 8 + [HBM] * 8,
+        out_shape=shape((2 * SEGMENTS, 1, total), f32),
+        in_specs=[SMEM] + [VMEM] * 8 + [HBM] * 8,
         out_specs=VMEM,
         scratch_shapes=[
             pltpu.VMEM((2, blocks, rows, width), bf16),
@@ -492,12 +504,12 @@
             pltpu.VMEM((2, width, width), bf16),
             pltpu.SemaphoreType.DMA((2, 2)),
         ],
-        compiler_params=pltpu.CompilerParams(vmem_limit_bytes=VMEM_LIMIT),
+        compiler_params=pltpu.CompilerParams(vmem_limit_bytes=REST_VMEM),
         cost_estimate=pl.CostEstimate(
             flops=6 * blocks * rows * width * width, bytes_accessed=1 << 24, transcendentals=0
         ),
     )(
-        place, cols, init, spread, pick, live, keys, hidden, boundary, loss0, own, flip, even,
+        cols, init, spread, pick, live, keys, hidden, boundary, loss0, own, flip, even,
         even_flip, odd, odd_other, odd_flip, odd_other_flip,
     )
     losses = lax.all_to_all(losses, ("x", "core", "zh"), split_axis=0, concat_axis=0, tiled=True)

time: 130 us -> 110 us (0.85)
  local copies, waits for them, and re-layouts: 12.4 us -> 0.82 us
  Pallas kernels: 40.4 us -> 35.7 us
  starting transfers between devices: 27.1 us -> 24.3 us
    unnamed x22 -> x10, local copies, waits for them, and re-layouts: 8.1 us -> 0.08 us
    pallas_call x3, Pallas kernels: 40.4 us -> 35.7 us  [the longest x1 21.9 us: local(): pl.pallas_call(rest_kernel, out_shape=shape((2 * SEGMENTS, 1, total), f32...]
    ppermute x21 -> x17, starting transfers between devices: 22.9 us -> 19.5 us  [exchange(): return lax.ppermute(block, AXES, pairs)]
    dynamic_slice x1, local copies, waits for them, and re-layouts: 2.43 us -> 0.07 us  [local(): lax.dynamic_slice(own, (zl * (width // 2), 0), (width // 2, width))]
    ppermute x21 -> x17, waiting for transfers between devices: 43.3 us -> 42.5 us  [exchange(): return lax.ppermute(block, AXES, pairs)]
  transfers between devices with their start and end apart: 22 -> 18, of which waited for: 9 -> 10; matrix products, arithmetic and copies ran while one was open for 3% -> 0% of each run, Pallas kernels for 13% -> 10%
where the time goes in v3:
time: 110 us; the launch traced here: 109 us
  waiting for transfers between devices  48.1 us (44%)
  Pallas kernels  35.7 us (32%)
  starting transfers between devices  24.3 us (22%)
    ppermute x17, waiting for transfers between devices, exchange(): return lax.ppermute(block, AXES, pairs)  42.5 us
    pallas_call x1, Pallas kernels, local(): pl.pallas_call(rest_kernel, out_shape=shape((2 * SEGMENTS, 1, total), f32...  21.9 us
    ppermute x17, starting transfers between devices, exchange(): return lax.ppermute(block, AXES, pairs)  19.5 us
    pallas_call x1, Pallas kernels, local(): pl.pallas_call(first_kernel, out_shape=keep, in_specs=[HBM] * 15, out_spe...  11 us
    all_to_all x1, waiting for transfers between devices, local(): lax.all_to_all(losses, ('x', 'core', 'zh'), split_axis=0, concat_axis=0,...  5.64 us
    all_to_all x1, starting transfers between devices, local(): lax.all_to_all(losses, ('x', 'core', 'zh'), split_axis=0, concat_axis=0,...  4.8 us
    pallas_call x1, Pallas kernels, local(): pl.pallas_call(pack_kernel, out_shape=(packed, packed), in_specs=[HBM, HB...  2.9 us
  transfers between devices with their start and end apart: 18, of which 10 were waited for; matrix products, arithmetic and copies ran while one was open for 0% of the time, Pallas kernels for 10%

profile of v3, /device:TPU:0, one launch (start us, length us, event | category | flops | bytes accessed | tf_op | source)
XLA Modules:
  0.0 109.3 jit_solution(1486415788888212286)
XLA Ops:
  0.0 2.9 %shard_map.91 = (bf16[144,1152]{1,0:T(8,128)(2,1)}, bf16[144,1152]{1,0:T(8,128)(2,1)}) custom-call(bf16[4,256,1024]{2,1,0:T(8,128)(2,1)} %init_feats.1, bf16[4,2,128,128]{3,2,1,0:T(8,128)(2,1)} %tile_vals.1, s32[4,8,8]{2,1,0:T(8,128)} %send_ref.1, s32[4,8]{1,0:T(4,128)} %count_ref.1, s32[4,8,8]{2,1,0:T(8,128)} %recv_ref.1, bf16[4,8,8]{2,1,0:T(8,128)(2,1)} %weight_ref.1, ...), custom_call_target="tpu_custom_call" | custom-call | tf_op jit(solution)/shard_map/pallas_call | solution.py:425
  2.9 0.0 copy-done.1
  2.9 4.8 %collective-permute-start.7 = (bf16[1024,1024]{1,0:T(8,128)(2,1)S(1)}, bf16[1024,1024]{1,0:T(8,128)(2,1)}, u32[]{:S(2)}, u32[]{:S(2)}) collective-permute-start(bf16[1024,1024]{1,0:T(8,128)(2,1)S(1)} %bitcast.9), channel_id=1, source_target_pairs={{0,16},{1,17},{2,18},{3,19},{4,20},{5,21},{6,22},{7,23},{16,0},{17... | collective-permute-start | bytes 6291464 | tf_op jit(solution)/shard_map/ppermute | solution.py:36
  7.8 1.6 %collective-permute-start = (bf16[144,1152]{1,0:T(8,128)(2,1)}, bf16[144,1152]{1,0:T(8,128)(2,1)S(1)}, u32[]{:S(2)}, u32[]{:S(2)}) collective-permute-start(bf16[144,1152]{1,0:T(8,128)(2,1)} %get-tuple-element.36.mine_ref), channel_id=1, source_target_pairs={{0,1},{1,0},{2,3},{3,2},{4,5},{5,4},{6,7},{7,6},{8,9},{9,8},{10,11... | collective-permute-start | bytes 995336 | tf_op jit(solution)/shard_map/ppermute | solution.py:36
  9.4 1.6 %collective-permute-start.1 = (bf16[144,1152]{1,0:T(8,128)(2,1)}, bf16[144,1152]{1,0:T(8,128)(2,1)S(1)}, u32[]{:S(2)}, u32[]{:S(2)}) collective-permute-start(bf16[144,1152]{1,0:T(8,128)(2,1)} %get-tuple-element.36.mine_ref), channel_id=1, source_target_pairs={{0,2},{1,3},{2,0},{3,1},{4,6},{5,7},{6,4},{7,5},{8,10},{9,11},{10,... | collective-permute-start | bytes 995336 | tf_op jit(solution)/shard_map/ppermute | solution.py:36
  10.9 2.6 %collective-permute-start.2 = (bf16[144,1152]{1,0:T(8,128)(2,1)}, bf16[144,1152]{1,0:T(8,128)(2,1)S(1)}, u32[]{:S(2)}, u32[]{:S(2)}) collective-permute-start(bf16[144,1152]{1,0:T(8,128)(2,1)} %get-tuple-element.37), channel_id=1, source_target_pairs={{0,4},{1,5},{2,6},{3,7},{4,0},{5,1},{6,2},{7,3},{8,12},{9,13},{10,... | collective-permute-start | bytes 995336 | tf_op jit(solution)/shard_map/ppermute | solution.py:36
  13.5 0.1 constant_dynamic-slice_fusion
  13.6 0.0 copy-start
  13.6 0.0 copy-start.2
  13.6 0.0 copy-start.3
  13.6 0.9 collective-permute-start.6
  14.5 1.4 %collective-permute-done = bf16[144,1152]{1,0:T(8,128)(2,1)S(1)} collective-permute-done((bf16[144,1152]{1,0:T(8,128)(2,1)}, bf16[144,1152]{1,0:T(8,128)(2,1)S(1)}, u32[]{:S(2)}, u32[]{:S(2)}) %collective-permute-start) | collective-permute-done | bytes 331808 | tf_op jit(solution)/shard_map/ppermute | solution.py:36
  15.9 8.5 %collective-permute-done.1 = bf16[144,1152]{1,0:T(8,128)(2,1)S(1)} collective-permute-done((bf16[144,1152]{1,0:T(8,128)(2,1)}, bf16[144,1152]{1,0:T(8,128)(2,1)S(1)}, u32[]{:S(2)}, u32[]{:S(2)}) %collective-permute-start.1) | collective-permute-done | bytes 331808 | tf_op jit(solution)/shard_map/ppermute | solution.py:36
  24.3 2.4 %collective-permute-done.2 = bf16[144,1152]{1,0:T(8,128)(2,1)S(1)} collective-permute-done((bf16[144,1152]{1,0:T(8,128)(2,1)}, bf16[144,1152]{1,0:T(8,128)(2,1)S(1)}, u32[]{:S(2)}, u32[]{:S(2)}) %collective-permute-start.2) | collective-permute-done | bytes 331808 | tf_op jit(solution)/shard_map/ppermute | solution.py:36
  26.8 0.1 collective-permute-start.4
  26.9 0.1 pad_maximum_fusion
  27.0 0.6 collective-permute-start.3
  27.5 0.4 collective-permute-start.5
  28.0 9.5 %collective-permute-done.5.rest_2_ = bf16[144,1152]{1,0:T(8,128)(2,1)S(1)} collective-permute-done((bf16[144,1152]{1,0:T(8,128)(2,1)S(1)}, bf16[144,1152]{1,0:T(8,128)(2,1)S(1)}, u32[]{:S(2)}, u32[]{:S(2)}) %collective-permute-start.5) | collective-permute-done | bytes 331808 | tf_op jit(solution)/shard_map/ppermute | solution.py:36
  37.4 6.9 %collective-permute-done.3.rest_1_ = bf16[288,1152]{1,0:T(8,128)(2,1)S(1)} collective-permute-done((bf16[288,1152]{1,0:T(8,128)(2,1)S(1)}, bf16[288,1152]{1,0:T(8,128)(2,1)S(1)}, u32[]{:S(2)}, u32[]{:S(2)}) %collective-permute-start.3) | collective-permute-done | bytes 663584 | tf_op jit(solution)/shard_map/ppermute | solution.py:36
  44.3 0.0 collective-permute-done.6.odd_ref
  44.3 0.0 collective-permute-done.4.rest_4_
  44.3 0.0 collective-permute-done.7.rest_10_.even_ref
  44.3 1.7 %collective-permute-start.11 = (bf16[1024,1024]{1,0:T(8,128)(2,1)}, bf16[1024,1024]{1,0:T(8,128)(2,1)S(1)}, u32[]{:S(2)}, u32[]{:S(2)}) collective-permute-start(bf16[1024,1024]{1,0:T(8,128)(2,1)} %collective-permute-done.7.rest_10_.even_ref), channel_id=1, source_target_pairs={{0,8},{1,9},{2,10},{3,11},{4,12},{5,13},{6,14},{7,15},{16,24},{17,... | collective-permute-start | bytes 6291464 | tf_op jit(solution)/shard_map/ppermute | solution.py:36
  46.1 0.1 collective-permute-start.13
  46.2 0.5 collective-permute-start.9
  46.7 0.6 collective-permute-start.8
  47.3 0.0 collective-permute-start.10
  47.3 9.2 %collective-permute-done.8.rest_3_ = bf16[144,1152]{1,0:T(8,128)(2,1)S(1)} collective-permute-done((bf16[144,1152]{1,0:T(8,128)(2,1)S(1)}, bf16[144,1152]{1,0:T(8,128)(2,1)S(1)}, u32[]{:S(2)}, u32[]{:S(2)}) %collective-permute-start.8) | collective-permute-done | bytes 331808 | tf_op jit(solution)/shard_map/ppermute | solution.py:36
  56.5 0.7 collective-permute-start.14
  57.2 0.0 collective-permute-done.10.rest_6_
  57.2 0.0 collective-permute-done.9.rest_5_
  57.2 0.0 collective-permute-done.11.rest_11_.even_flip_ref
  57.2 0.8 collective-permute-start.12
  58.0 0.0 collective-permute-done.13.rest_9_.flip_ref
  58.0 1.3 %collective-permute-done.12.rest_7_ = bf16[144,1152]{1,0:T(8,128)(2,1)S(1)} collective-permute-done((bf16[144,1152]{1,0:T(8,128)(2,1)S(1)}, bf16[144,1152]{1,0:T(8,128)(2,1)S(1)}, u32[]{:S(2)}, u32[]{:S(2)}) %collective-permute-start.12) | collective-permute-done | bytes 331808 | tf_op jit(solution)/shard_map/ppermute | solution.py:36
  59.2 0.0 copy-done
  59.2 0.0 copy-done.2
  59.2 11.0 %shard_map.92 = (bf16[8,256,1024]{2,1,0:T(8,128)(2,1)S(1)}, bf16[16,128,256]{2,1,0:T(8,128)(2,1)S(1)}, bf16[8,112,256]{2,1,0:T(8,128)(2,1)S(1)}, s32[8,128]{1,0:...) custom-call(bf16[4,256,1024]{2,1,0:T(8,128)(2,1)S(1)} %copy-done, ...), custom_call_target="tpu_custom_call" | custom-call | flops 4294967296 | bytes 16777216 | tf_op jit(solution)/shard_map/pallas_call | solution.py:469
  70.2 0.0 collective-permute-done.14.odd_other_ref
  70.2 1.3 %collective-permute-start.15 = (bf16[512,1024]{1,0:T(8,128)(2,1)S(1)}, bf16[512,1024]{1,0:T(8,128)(2,1)S(1)}, u32[]{:S(2)}, u32[]{:S(2)}) collective-permute-start(bf16[512,1024]{1,0:T(8,128)(2,1)S(1)} %collective-permute-done.6.odd_ref), channel_id=1, source_target_pairs={{8,0},{9,1},{10,2},{11,3},{12,4},{13,5},{14,6},{15,7},{24,16},{25,... | collective-permute-start | bytes 3145736 | tf_op jit(solution)/shard_map/ppermute | solution.py:36
  71.5 1.3 %collective-permute-start.16 = (bf16[512,1024]{1,0:T(8,128)(2,1)S(1)}, bf16[512,1024]{1,0:T(8,128)(2,1)S(1)}, u32[]{:S(2)}, u32[]{:S(2)}) collective-permute-start(bf16[512,1024]{1,0:T(8,128)(2,1)S(1)} %collective-permute-done.14.odd_other_ref), channel_id=1, source_target_pairs={{8,0},{9,1},{10,2},{11,3},{12,4},{13,5},{14,6},{15,7},{24,16},{25,... | collective-permute-start | bytes 3145736 | tf_op jit(solution)/shard_map/ppermute | solution.py:36
  72.8 2.0 %collective-permute-done.15.odd_flip_ref = bf16[512,1024]{1,0:T(8,128)(2,1)S(1)} collective-permute-done((bf16[512,1024]{1,0:T(8,128)(2,1)S(1)}, bf16[512,1024]{1,0:T(8,128)(2,1)S(1)}, u32[]{:S(2)}, u32[]{:S(2)}) %collective-permute-start.15) | collective-permute-done | bytes 1048608 | tf_op jit(solution)/shard_map/ppermute | solution.py:36
  74.8 1.5 %collective-permute-done.16.odd_other_flip_ref = bf16[512,1024]{1,0:T(8,128)(2,1)S(1)} collective-permute-done((bf16[512,1024]{1,0:T(8,128)(2,1)S(1)}, bf16[512,1024]{1,0:T(8,128)(2,1)S(1)}, u32[]{:S(2)}, u32[]{:S(2)}) %collective-permute-start.16) | collective-permute-done | bytes 1048608 | tf_op jit(solution)/shard_map/ppermute | solution.py:36
  76.3 21.9 %shard_map.93 = f32[8,1,384]{2,1,0:T(1,128)} custom-call(s32[8,128]{1,0:T(8,128)S(1)} %get-tuple-element.50.cols_ref, bf16[8,256,1024]{2,1,0:T(8,128)(2,1)S(1)} %get-tuple-element.51.init_ref, bf16[16,128,256]{2,1,0:T(8,128)(2,1)S(1)} %get-tuple-element.52.spread_ref, bf16[8,112,256]{2,1,0:T(8,128)(2,1)S(1)} %get-tuple-element.53.pick_ref, ...), custom_call_target="tpu_custom_call" | custom-call | flops 12884901888 | bytes 16777216 | tf_op jit(solution)/shard_map/pallas_call | solution.py:494
  98.2 4.8 %all-to-all-start = ((f32[8,1,384]{2,1,0:T(1,128)}), f32[8,1,384]{2,1,0:T(1,128)S(1)}, u32[]{:S(2)}, u32[]{:S(2)}) async-start(f32[8,1,384]{2,1,0:T(1,128)} %shard_map.93), calls=%async_computation | async-start | bytes 24576 | tf_op jit(solution)/shard_map/all_to_all | solution.py:515
  103.0 5.6 %all-to-all-done = f32[8,1,384]{2,1,0:T(1,128)S(1)} async-done(((f32[8,1,384]{2,1,0:T(1,128)}), f32[8,1,384]{2,1,0:T(1,128)S(1)}, u32[]{:S(2)}, u32[]{:S(2)}) %all-to-all-start) | async-done | bytes 12320 | tf_op jit(solution)/shard_map/all_to_all | solution.py:515
  108.7 0.6 reshape.7
  (9 shorter events, 0.2 us)
Async XLA Ops:
  0.0 2.9 %copy-start.1 = (bf16[1,1024,1024]{2,1,0:T(8,128)(2,1)S(1)}, bf16[1,1024,1024]{2,1,0:T(8,128)(2,1)}, u32[]{:S(2)}) copy-start(bf16[1,1024,1024]{2,1,0:T(8,128)(2,1)} %param.10) | copy-start | bytes 6291460
  2.9 41.4 %collective-permute-start.7 = (bf16[1024,1024]{1,0:T(8,128)(2,1)S(1)}, bf16[1024,1024]{1,0:T(8,128)(2,1)}, u32[]{:S(2)}, u32[]{:S(2)}) collective-permute-start(bf16[1024,1024]{1,0:T(8,128)(2,1)S(1)} %bitcast.9), channel_id=1, source_target_pairs={{0,16},{1,17},{2,18},{3,19},{4,20},{5,21},{6,22},{7,23},{16,0},{17... | collective-permute-start | bytes 6291464 | tf_op jit(solution)/shard_map/ppermute | solution.py:36
  7.8 8.1 %collective-permute-start = (bf16[144,1152]{1,0:T(8,128)(2,1)}, bf16[144,1152]{1,0:T(8,128)(2,1)S(1)}, u32[]{:S(2)}, u32[]{:S(2)}) collective-permute-start(bf16[144,1152]{1,0:T(8,128)(2,1)} %get-tuple-element.36.mine_ref), channel_id=1, source_target_pairs={{0,1},{1,0},{2,3},{3,2},{4,5},{5,4},{6,7},{7,6},{8,9},{9,8},{10,11... | collective-permute-start | bytes 995336 | tf_op jit(solution)/shard_map/ppermute | solution.py:36
  9.4 15.0 %collective-permute-start.1 = (bf16[144,1152]{1,0:T(8,128)(2,1)}, bf16[144,1152]{1,0:T(8,128)(2,1)S(1)}, u32[]{:S(2)}, u32[]{:S(2)}) collective-permute-start(bf16[144,1152]{1,0:T(8,128)(2,1)} %get-tuple-element.36.mine_ref), channel_id=1, source_target_pairs={{0,2},{1,3},{2,0},{3,1},{4,6},{5,7},{6,4},{7,5},{8,10},{9,11},{10,... | collective-permute-start | bytes 995336 | tf_op jit(solution)/shard_map/ppermute | solution.py:36
  10.9 15.8 %collective-permute-start.2 = (bf16[144,1152]{1,0:T(8,128)(2,1)}, bf16[144,1152]{1,0:T(8,128)(2,1)S(1)}, u32[]{:S(2)}, u32[]{:S(2)}) collective-permute-start(bf16[144,1152]{1,0:T(8,128)(2,1)} %get-tuple-element.37), channel_id=1, source_target_pairs={{0,4},{1,5},{2,6},{3,7},{4,0},{5,1},{6,2},{7,3},{8,12},{9,13},{10,... | collective-permute-start | bytes 995336 | tf_op jit(solution)/shard_map/ppermute | solution.py:36
  13.6 45.6 %copy-start = (bf16[4,256,1024]{2,1,0:T(8,128)(2,1)S(1)}, bf16[4,256,1024]{2,1,0:T(8,128)(2,1)}, u32[]{:S(2)}) copy-start(bf16[4,256,1024]{2,1,0:T(8,128)(2,1)} %init_feats.1) | copy-start | bytes 6291460
  13.6 45.6 %copy-start.2 = (bf16[4,2,128,128]{3,2,1,0:T(8,128)(2,1)S(1)}, bf16[4,2,128,128]{3,2,1,0:T(8,128)(2,1)}, u32[]{:S(2)}) copy-start(bf16[4,2,128,128]{3,2,1,0:T(8,128)(2,1)} %tile_vals.1) | copy-start | bytes 786436
  13.6 45.6 %copy-start.3 = (bf16[144,1152]{1,0:T(8,128)(2,1)S(1)}, bf16[144,1152]{1,0:T(8,128)(2,1)}, u32[]{:S(2)}) copy-start(bf16[144,1152]{1,0:T(8,128)(2,1)} %get-tuple-element.36.mine_ref) | copy-start | bytes 995332
  13.6 30.7 %collective-permute-start.6 = (bf16[512,1024]{1,0:T(8,128)(2,1)S(1)}, bf16[512,1024]{1,0:T(8,128)(2,1)S(1)}, u32[]{:S(2)}, u32[]{:S(2)}) collective-permute-start(bf16[512,1024]{1,0:T(8,128)(2,1)S(1)} %constant_dynamic-slice_fusion), channel_id=1, source_target_pairs={{8,24},{9,25},{10,26},{11,27},{12,28},{13,29},{14,30},{15,31},{24,... | collective-permute-start | bytes 3145736 | tf_op jit(solution)/shard_map/ppermute | solution.py:36
  26.8 17.5 %collective-permute-start.4 = (bf16[432,1152]{1,0:T(8,128)(2,1)S(1)}, bf16[432,1152]{1,0:T(8,128)(2,1)S(1)}, u32[]{:S(2)}, u32[]{:S(2)}) collective-permute-start(bf16[432,1152]{1,0:T(8,128)(2,1)S(1)} %constant_dynamic-update-slice_fusion.rest_0_), channel_id=1, source_target_pairs={{0,8},{1,9},{2,10},{3,11},{4,12},{5,13},{6,14},{7,15},{8,0},{9,1},... | collective-permute-start | bytes 2985992 | tf_op jit(solution)/shard_map/ppermute | solution.py:36
  27.0 17.4 %collective-permute-start.3 = (bf16[288,1152]{1,0:T(8,128)(2,1)S(1)}, bf16[288,1152]{1,0:T(8,128)(2,1)S(1)}, u32[]{:S(2)}, u32[]{:S(2)}) collective-permute-start(bf16[288,1152]{1,0:T(8,128)(2,1)S(1)} %pad_maximum_fusion), channel_id=1, source_target_pairs={{0,1},{1,0},{2,3},{3,2},{4,5},{5,4},{6,7},{7,6},{8,9},{9,8},{10,11... | collective-permute-start | bytes 1990664 | tf_op jit(solution)/shard_map/ppermute | solution.py:36
  27.5 9.9 %collective-permute-start.5 = (bf16[144,1152]{1,0:T(8,128)(2,1)S(1)}, bf16[144,1152]{1,0:T(8,128)(2,1)S(1)}, u32[]{:S(2)}, u32[]{:S(2)}) collective-permute-start(bf16[144,1152]{1,0:T(8,128)(2,1)S(1)} %collective-permute-done.2), channel_id=1, source_target_pairs={{0,2},{1,3},{2,0},{3,1},{4,6},{5,7},{6,4},{7,5},{8,10},{9,11},{10,... | collective-permute-start | bytes 995336 | tf_op jit(solution)/shard_map/ppermute | solution.py:36
  44.3 12.9 %collective-permute-start.11 = (bf16[1024,1024]{1,0:T(8,128)(2,1)}, bf16[1024,1024]{1,0:T(8,128)(2,1)S(1)}, u32[]{:S(2)}, u32[]{:S(2)}) collective-permute-start(bf16[1024,1024]{1,0:T(8,128)(2,1)} %collective-permute-done.7.rest_10_.even_ref), channel_id=1, source_target_pairs={{0,8},{1,9},{2,10},{3,11},{4,12},{5,13},{6,14},{7,15},{16,24},{17,... | collective-permute-start | bytes 6291464 | tf_op jit(solution)/shard_map/ppermute | solution.py:36
  46.1 11.9 %collective-permute-start.13 = (bf16[1024,1024]{1,0:T(8,128)(2,1)S(1)}, bf16[1024,1024]{1,0:T(8,128)(2,1)S(1)}, u32[]{:S(2)}, u32[]{:S(2)}) collective-permute-start(bf16[1024,1024]{1,0:T(8,128)(2,1)S(1)} %bitcast.11), channel_id=1, source_target_pairs={{0,8},{1,9},{2,10},{3,11},{4,12},{5,13},{6,14},{7,15},{8,0},{9,1},... | collective-permute-start | bytes 6291464 | tf_op jit(solution)/shard_map/ppermute | solution.py:36
  46.2 11.0 %collective-permute-start.9 = (bf16[288,1152]{1,0:T(8,128)(2,1)S(1)}, bf16[288,1152]{1,0:T(8,128)(2,1)S(1)}, u32[]{:S(2)}, u32[]{:S(2)}) collective-permute-start(bf16[288,1152]{1,0:T(8,128)(2,1)S(1)} %collective-permute-done.3.rest_1_), channel_id=1, source_target_pairs={{0,8},{1,9},{2,10},{3,11},{4,12},{5,13},{6,14},{7,15},{8,0},{9,1},... | collective-permute-start | bytes 1990664 | tf_op jit(solution)/shard_map/ppermute | solution.py:36
  46.7 9.8 %collective-permute-start.8 = (bf16[144,1152]{1,0:T(8,128)(2,1)S(1)}, bf16[144,1152]{1,0:T(8,128)(2,1)S(1)}, u32[]{:S(2)}, u32[]{:S(2)}) collective-permute-start(bf16[144,1152]{1,0:T(8,128)(2,1)S(1)} %collective-permute-done.5.rest_2_), channel_id=1, source_target_pairs={{0,1},{1,0},{2,3},{3,2},{4,5},{5,4},{6,7},{7,6},{8,9},{9,8},{10,11... | collective-permute-start | bytes 995336 | tf_op jit(solution)/shard_map/ppermute | solution.py:36
  47.3 9.9 %collective-permute-start.10 = (bf16[144,1152]{1,0:T(8,128)(2,1)S(1)}, bf16[144,1152]{1,0:T(8,128)(2,1)S(1)}, u32[]{:S(2)}, u32[]{:S(2)}) collective-permute-start(bf16[144,1152]{1,0:T(8,128)(2,1)S(1)} %collective-permute-done.5.rest_2_), channel_id=1, source_target_pairs={{0,8},{1,9},{2,10},{3,11},{4,12},{5,13},{6,14},{7,15},{8,0},{9,1},... | collective-permute-start | bytes 995336 | tf_op jit(solution)/shard_map/ppermute | solution.py:36
  56.5 13.8 %collective-permute-start.14 = (bf16[512,1024]{1,0:T(8,128)(2,1)S(1)}, bf16[512,1024]{1,0:T(8,128)(2,1)S(1)}, u32[]{:S(2)}, u32[]{:S(2)}) collective-permute-start(bf16[512,1024]{1,0:T(8,128)(2,1)S(1)} %collective-permute-done.6.odd_ref), channel_id=1, source_target_pairs={{8,10},{9,11},{10,8},{11,9},{12,14},{13,15},{14,12},{15,13},{24,26... | collective-permute-start | bytes 3145736 | tf_op jit(solution)/shard_map/ppermute | solution.py:36
  57.2 2.0 %collective-permute-start.12 = (bf16[144,1152]{1,0:T(8,128)(2,1)S(1)}, bf16[144,1152]{1,0:T(8,128)(2,1)S(1)}, u32[]{:S(2)}, u32[]{:S(2)}) collective-permute-start(bf16[144,1152]{1,0:T(8,128)(2,1)S(1)} %collective-permute-done.8.rest_3_), channel_id=1, source_target_pairs={{0,8},{1,9},{2,10},{3,11},{4,12},{5,13},{6,14},{7,15},{8,0},{9,1},... | collective-permute-start | bytes 995336 | tf_op jit(solution)/shard_map/ppermute | solution.py:36
  70.2 4.6 %collective-permute-start.15 = (bf16[512,1024]{1,0:T(8,128)(2,1)S(1)}, bf16[512,1024]{1,0:T(8,128)(2,1)S(1)}, u32[]{:S(2)}, u32[]{:S(2)}) collective-permute-start(bf16[512,1024]{1,0:T(8,128)(2,1)S(1)} %collective-permute-done.6.odd_ref), channel_id=1, source_target_pairs={{8,0},{9,1},{10,2},{11,3},{12,4},{13,5},{14,6},{15,7},{24,16},{25,... | collective-permute-start | bytes 3145736 | tf_op jit(solution)/shard_map/ppermute | solution.py:36
  71.5 4.8 %collective-permute-start.16 = (bf16[512,1024]{1,0:T(8,128)(2,1)S(1)}, bf16[512,1024]{1,0:T(8,128)(2,1)S(1)}, u32[]{:S(2)}, u32[]{:S(2)}) collective-permute-start(bf16[512,1024]{1,0:T(8,128)(2,1)S(1)} %collective-permute-done.14.odd_other_ref), channel_id=1, source_target_pairs={{8,0},{9,1},{10,2},{11,3},{12,4},{13,5},{14,6},{15,7},{24,16},{25,... | collective-permute-start | bytes 3145736 | tf_op jit(solution)/shard_map/ppermute | solution.py:36
  98.2 10.4 %all-to-all-start = ((f32[8,1,384]{2,1,0:T(1,128)}), f32[8,1,384]{2,1,0:T(1,128)S(1)}, u32[]{:S(2)}, u32[]{:S(2)}) async-start(f32[8,1,384]{2,1,0:T(1,128)} %shard_map.93), calls=%async_computation | async-start | bytes 24576 | tf_op jit(solution)/shard_map/all_to_all | solution.py:515

commit v4 on v3

--- a/solution.py
+++ b/solution.py
@@ -154,25 +154,23 @@
 
 
 def run_layer(spread_ref, cols_ref, init_ref, pick_ref, source, border_in, weight, mixing,
-              target, border_out, anchors, group=2, unroll=4):
+              target, border_out, anchors, meanwhile, group=2):
     blocks, rows, _ = init_ref.shape
-
-    def advance(chunk, carry):
+    for first in range(0, blocks, group):
         support = jnp.concatenate(
             [
-                support_of(chunk * group + k, spread_ref, cols_ref, init_ref, source, border_in)
+                support_of(first + k, spread_ref, cols_ref, init_ref, source, border_in)
                 for k in range(group)
             ],
             axis=0,
         )
+        if first == 0:
+            meanwhile()
         out = transform(support, weight[...], mixing)
         for k in range(group):
             block_out = out[k * rows : (k + 1) * rows]
-            target[chunk * group + k] = block_out
-            publish(chunk * group + k, block_out, pick_ref, border_out, anchors)
-        return carry
-
-    lax.fori_loop(0, blocks // group, advance, 0, unroll=unroll)
+            target[first + k] = block_out
+            publish(first + k, block_out, pick_ref, border_out, anchors)
 
 
 def first_kernel(
@@ -205,11 +203,15 @@
             pltpu.make_async_copy(source, weight, weight_sems.at[0]).start()
 
     span = zh * 2 + x
-    copies = [
-        start(init_feats.at[span], init_ref.at[vert], sems.at[0]),
-        start(mine_ref.at[pl.ds(half, SMALL_ROWS), :], small.at[vert], sems.at[1]),
-    ]
-    at = 2
+    tables = [start(mine_ref.at[pl.ds(half, SMALL_ROWS), :], small.at[vert], sems.at[0])]
+    at = 1
+    for k in range(1, blocks):
+        group, index = ARRIVALS[k]
+        source = nets[group].at[pl.ds((index + 1) * half + index * SMALL_ROWS, SMALL_ROWS), :]
+        tables.append(start(source, small.at[vert ^ k], sems.at[at]))
+        at += 1
+    copies = [start(init_feats.at[span], init_ref.at[vert], sems.at[at])]
+    at += 1
     for t in range(tiles):
         target = spread_ref.at[vert * tiles + t, :, pl.ds(0, tile)]
         copies.append(start(tile_vals.at[span, t], target, sems.at[at]))
@@ -235,10 +237,7 @@
                 )
             )
             at += 2
-        source = nets[group].at[pl.ds(base + half, SMALL_ROWS), :]
-        copies.append(start(source, small.at[block], sems.at[at]))
-        at += 1
-    for copy in copies:
+    for copy in tables:
         copy.wait()
 
     owner = core * 4 + zl * 2 + y
@@ -289,16 +288,15 @@
                 t * tile : (t + 1) * tile
             ]
 
-    def begin(block, carry):
+    to_scalar.wait()
+    for copy in copies:
+        copy.wait()
+    for block in range(blocks):
         publish(block, init_ref[block], pick_ref, boundary0, keys)
-        return carry
-
-    lax.fori_loop(0, blocks, begin, 0, unroll=4)
-    to_scalar.wait()
-    pltpu.make_async_copy(weights[0], weight, weight_sems.at[0]).wait()
     run_layer(
         spread_ref, cols_ref, init_ref, pick_ref, init_ref, boundary0, weight, mixing_of(0),
         hidden, boundary, anchors,
+        pltpu.make_async_copy(weights[0], weight, weight_sems.at[0]).wait,
     )
     loss_ref[...] = score(keys, anchors, live_ref)
 
@@ -364,30 +362,32 @@
     report(0, loss0_ref[...])
     source, border_in = hidden, boundary
     for layer in range(1, layers - 1):
-        arrive(layer)
-        fetch(layer + 1)
         target, border_out = held.at[layer % 2], border_held.at[layer % 2]
+        now, before = anchors.at[layer % 2], anchors.at[1 - layer % 2]
+
+        def meanwhile():
+            arrive(layer)
+            fetch(layer + 1)
+            if layer > 1:
+                report(layer - 1, score(keys, before, live_ref))
+
         run_layer(
             spread_ref, cols_ref, init_ref, pick_ref, source, border_in, weight.at[layer % 2],
-            mixing_of(layer), target, border_out, anchors,
-        )
-        report(layer, score(keys, anchors, live_ref))
+            mixing_of(layer), target, border_out, now, meanwhile,
+        )
         source, border_in = target, border_out
 
     border = boundary.shape[1]
 
-    def choose(block, carry):
+    report(layers - 2, score(keys, anchors.at[layers % 2], live_ref))
+    for block in range(blocks):
         support = support_of(block, spread_ref, cols_ref, init_ref, source, border_in)
         chosen = jnp.dot(pick_ref[block, border:, :], support, preferred_element_type=jnp.float32)
-        slot_start = pl.multiple_of(block * slots, slots)
-        last[pl.ds(slot_start, slots), :] = chosen.astype(jnp.bfloat16)
-        return carry
-
-    lax.fori_loop(0, blocks, choose, 0, unroll=4)
+        last[block * slots : (block + 1) * slots, :] = chosen.astype(jnp.bfloat16)
     arrive(layers - 1)
     final = transform(last[...], weight[(layers - 1) % 2], mixing_of(layers - 1))
-    anchors[...] = rms_unit(final.astype(jnp.float32))
-    report(layers - 1, score(keys, anchors, live_ref))
+    last[...] = rms_unit(final.astype(jnp.float32))
+    report(layers - 1, score(keys, last, live_ref))
 
 
 VMEM = pl.BlockSpec(memory_space=pltpu.VMEM)
@@ -441,6 +441,8 @@
     even = exchange(own, "x", core=0)
     odd_part = lax.dynamic_slice(own, (zl * (width // 2), 0), (width // 2, width))
     odd = exchange(odd_part, "x", core=1)
+    net4, later = lax.optimization_barrier((net4, own))
+    net4, net2 = lax.optimization_barrier((net4, net2))
     net1, net2, net4 = lax.optimization_barrier((net1, net2, net4))
     net6 = exchange(net4, "zl")
     net35 = exchange(jnp.concatenate([net2, net4]), "y")
@@ -454,6 +456,9 @@
     odd_other = exchange(odd, "zl", core=1)
     net7, flip35, flip6, even_flip = lax.optimization_barrier((net7, flip35, flip6, even_flip))
     flip7 = exchange(net7, "core")
+    odd, odd_other, flip7 = lax.optimization_barrier((odd, odd_other, flip7))
+    odd_flip = exchange(odd, "core", core=1)
+    odd_other_flip = exchange(odd_other, "core", core=1)
 
     keep = [
         shape((blocks, rows, width), bf16),
@@ -488,9 +493,6 @@
         init_feats, tile_vals, mine, net124, net35, net6, net7, flip124, flip35, flip6, flip7,
         own, flip, even, even_flip,
     )
-    odd, odd_other, loss0 = lax.optimization_barrier((odd, odd_other, loss0))
-    odd_flip = exchange(odd, "core", core=1)
-    odd_other_flip = exchange(odd_other, "core", core=1)
     losses = pl.pallas_call(
         rest_kernel,
         out_shape=shape((2 * SEGMENTS, 1, total), f32),
@@ -499,7 +501,7 @@
         scratch_shapes=[
             pltpu.VMEM((2, blocks, rows, width), bf16),
             pltpu.VMEM((2, blocks, border, width), f32),
-            pltpu.VMEM((total, width), bf16),
+            pltpu.VMEM((2, total, width), bf16),
             pltpu.VMEM((total, width), bf16),
             pltpu.VMEM((2, width, width), bf16),
             pltpu.SemaphoreType.DMA((2, 2)),

time: 110 us -> 108 us (0.982)
  waiting for transfers between devices: 48.1 us -> 36.9 us
  starting transfers between devices: 24.3 us -> 33.9 us
    ppermute x17, waiting for transfers between devices: 42.5 us -> 31.3 us  [exchange(): return lax.ppermute(block, AXES, pairs)]
    ppermute x17, starting transfers between devices: 19.5 us -> 26.9 us  [exchange(): return lax.ppermute(block, AXES, pairs)]
    all_to_all x1, starting transfers between devices: 4.8 us -> 7 us  [local(): lax.all_to_all(losses, ('x', 'core', 'zh'), split_axis=0, concat_axis=0,...]
  transfers between devices with their start and end apart: 18 -> 18, of which waited for: 10 -> 9; matrix products, arithmetic and copies ran while one was open for 0% -> 0% of each run, Pallas kernels for 10% -> 11%
where the time goes in v4:
time: 108 us
  waiting for transfers between devices  36.9 us (34%)
  Pallas kernels  35.9 us (33%)
  starting transfers between devices  33.9 us (31%)
    ppermute x17, waiting for transfers between devices, exchange(): return lax.ppermute(block, AXES, pairs)  31.3 us
    ppermute x17, starting transfers between devices, exchange(): return lax.ppermute(block, AXES, pairs)  26.9 us
    pallas_call x1, Pallas kernels, local(): pl.pallas_call(rest_kernel, out_shape=shape((2 * SEGMENTS, 1, total), f32...  21.5 us
    pallas_call x1, Pallas kernels, local(): pl.pallas_call(first_kernel, out_shape=keep, in_specs=[HBM] * 15, out_spe...  11.5 us
    all_to_all x1, starting transfers between devices, local(): lax.all_to_all(losses, ('x', 'core', 'zh'), split_axis=0, concat_axis=0,...  7 us
    all_to_all x1, waiting for transfers between devices, local(): lax.all_to_all(losses, ('x', 'core', 'zh'), split_axis=0, concat_axis=0,...  5.6 us
    pallas_call x1, Pallas kernels, local(): pl.pallas_call(pack_kernel, out_shape=(packed, packed), in_specs=[HBM, HB...  2.9 us
  transfers between devices with their start and end apart: 18, of which 9 were waited for; matrix products, arithmetic and copies ran while one was open for 0% of the time, Pallas kernels for 11%

profile of v4, /device:TPU:0, one launch (start us, length us, event | category | flops | bytes accessed | tf_op | source)
XLA Modules:
  0.0 107.8 jit_solution(9250810676892975459)
XLA Ops:
  0.0 2.9 %shard_map.91 = (bf16[144,1152]{1,0:T(8,128)(2,1)}, bf16[144,1152]{1,0:T(8,128)(2,1)}) custom-call(bf16[4,256,1024]{2,1,0:T(8,128)(2,1)} %init_feats.1, bf16[4,2,128,128]{3,2,1,0:T(8,128)(2,1)} %tile_vals.1, s32[4,8,8]{2,1,0:T(8,128)} %send_ref.1, s32[4,8]{1,0:T(4,128)} %count_ref.1, s32[4,8,8]{2,1,0:T(8,128)} %recv_ref.1, bf16[4,8,8]{2,1,0:T(8,128)(2,1)} %weight_ref.1, ...), custom_call_target="tpu_custom_call" | custom-call | tf_op jit(solution)/shard_map/pallas_call | solution.py:425
  2.9 0.0 copy-done.1
  2.9 4.8 %collective-permute-start.7 = (bf16[1024,1024]{1,0:T(8,128)(2,1)S(1)}, bf16[1024,1024]{1,0:T(8,128)(2,1)}, u32[]{:S(2)}, u32[]{:S(2)}) collective-permute-start(bf16[1024,1024]{1,0:T(8,128)(2,1)S(1)} %bitcast.9), channel_id=1, source_target_pairs={{0,16},{1,17},{2,18},{3,19},{4,20},{5,21},{6,22},{7,23},{16,0},{17... | collective-permute-start | bytes 6291464 | tf_op jit(solution)/shard_map/ppermute | solution.py:36
  7.8 2.7 %collective-permute-start.1 = (bf16[144,1152]{1,0:T(8,128)(2,1)}, bf16[144,1152]{1,0:T(8,128)(2,1)S(1)}, u32[]{:S(2)}, u32[]{:S(2)}) collective-permute-start(bf16[144,1152]{1,0:T(8,128)(2,1)} %get-tuple-element.40), channel_id=1, source_target_pairs={{0,4},{1,5},{2,6},{3,7},{4,0},{5,1},{6,2},{7,3},{8,12},{9,13},{10,... | collective-permute-start | bytes 995336 | tf_op jit(solution)/shard_map/ppermute | solution.py:36
  10.4 1.6 %collective-permute-start.2 = (bf16[144,1152]{1,0:T(8,128)(2,1)}, bf16[144,1152]{1,0:T(8,128)(2,1)S(1)}, u32[]{:S(2)}, u32[]{:S(2)}) collective-permute-start(bf16[144,1152]{1,0:T(8,128)(2,1)} %get-tuple-element.39.mine_ref), channel_id=1, source_target_pairs={{0,2},{1,3},{2,0},{3,1},{4,6},{5,7},{6,4},{7,5},{8,10},{9,11},{10,... | collective-permute-start | bytes 995336 | tf_op jit(solution)/shard_map/ppermute | solution.py:36
  12.0 1.5 %collective-permute-start = (bf16[144,1152]{1,0:T(8,128)(2,1)}, bf16[144,1152]{1,0:T(8,128)(2,1)S(1)}, u32[]{:S(2)}, u32[]{:S(2)}) collective-permute-start(bf16[144,1152]{1,0:T(8,128)(2,1)} %get-tuple-element.39.mine_ref), channel_id=1, source_target_pairs={{0,1},{1,0},{2,3},{3,2},{4,5},{5,4},{6,7},{7,6},{8,9},{9,8},{10,11... | collective-permute-start | bytes 995336 | tf_op jit(solution)/shard_map/ppermute | solution.py:36
  13.5 0.1 constant_dynamic-slice_fusion
  13.6 0.0 copy-start
  13.6 0.0 copy-start.2
  13.6 0.0 copy-start.3
  13.6 0.9 collective-permute-start.6
  14.5 9.7 %collective-permute-done.1 = bf16[144,1152]{1,0:T(8,128)(2,1)S(1)} collective-permute-done((bf16[144,1152]{1,0:T(8,128)(2,1)}, bf16[144,1152]{1,0:T(8,128)(2,1)S(1)}, u32[]{:S(2)}, u32[]{:S(2)}) %collective-permute-start.1) | collective-permute-done | bytes 331808 | tf_op jit(solution)/shard_map/ppermute | solution.py:36
  24.2 0.2 collective-permute-done.2
  24.4 0.0 collective-permute-done
  24.5 0.1 collective-permute-start.4
  24.6 0.1 pad_maximum_fusion
  24.6 1.6 %collective-permute-start.3 = (bf16[288,1152]{1,0:T(8,128)(2,1)S(1)}, bf16[288,1152]{1,0:T(8,128)(2,1)S(1)}, u32[]{:S(2)}, u32[]{:S(2)}) collective-permute-start(bf16[288,1152]{1,0:T(8,128)(2,1)S(1)} %pad_maximum_fusion), channel_id=1, source_target_pairs={{0,1},{1,0},{2,3},{3,2},{4,5},{5,4},{6,7},{7,6},{8,9},{9,8},{10,11... | collective-permute-start | bytes 1990664 | tf_op jit(solution)/shard_map/ppermute | solution.py:36
  26.3 1.4 %collective-permute-start.5 = (bf16[144,1152]{1,0:T(8,128)(2,1)S(1)}, bf16[144,1152]{1,0:T(8,128)(2,1)S(1)}, u32[]{:S(2)}, u32[]{:S(2)}) collective-permute-start(bf16[144,1152]{1,0:T(8,128)(2,1)S(1)} %collective-permute-done.1), channel_id=1, source_target_pairs={{0,2},{1,3},{2,0},{3,1},{4,6},{5,7},{6,4},{7,5},{8,10},{9,11},{10,... | collective-permute-start | bytes 995336 | tf_op jit(solution)/shard_map/ppermute | solution.py:36
  27.7 8.5 %collective-permute-done.5.rest_2_ = bf16[144,1152]{1,0:T(8,128)(2,1)S(1)} collective-permute-done((bf16[144,1152]{1,0:T(8,128)(2,1)S(1)}, bf16[144,1152]{1,0:T(8,128)(2,1)S(1)}, u32[]{:S(2)}, u32[]{:S(2)}) %collective-permute-start.5) | collective-permute-done | bytes 331808 | tf_op jit(solution)/shard_map/ppermute | solution.py:36
  36.2 5.8 %collective-permute-done.3.rest_1_ = bf16[288,1152]{1,0:T(8,128)(2,1)S(1)} collective-permute-done((bf16[288,1152]{1,0:T(8,128)(2,1)S(1)}, bf16[288,1152]{1,0:T(8,128)(2,1)S(1)}, u32[]{:S(2)}, u32[]{:S(2)}) %collective-permute-start.3) | collective-permute-done | bytes 663584 | tf_op jit(solution)/shard_map/ppermute | solution.py:36
  42.0 0.0 collective-permute-done.6.odd_ref
  42.0 0.0 collective-permute-done.4.rest_4_
  42.0 1.1 %collective-permute-done.7.rest_10_.even_ref = bf16[1024,1024]{1,0:T(8,128)(2,1)} collective-permute-done((bf16[1024,1024]{1,0:T(8,128)(2,1)S(1)}, bf16[1024,1024]{1,0:T(8,128)(2,1)}, u32[]{:S(2)}, u32[]{:S(2)}) %collective-permute-start.7) | collective-permute-done | bytes 2097184 | tf_op jit(solution)/shard_map/ppermute | solution.py:36
  43.1 1.4 %collective-permute-start.11 = (bf16[1024,1024]{1,0:T(8,128)(2,1)}, bf16[1024,1024]{1,0:T(8,128)(2,1)S(1)}, u32[]{:S(2)}, u32[]{:S(2)}) collective-permute-start(bf16[1024,1024]{1,0:T(8,128)(2,1)} %collective-permute-done.7.rest_10_.even_ref), channel_id=1, source_target_pairs={{0,8},{1,9},{2,10},{3,11},{4,12},{5,13},{6,14},{7,15},{16,24},{17,... | collective-permute-start | bytes 6291464 | tf_op jit(solution)/shard_map/ppermute | solution.py:36
  44.5 0.1 collective-permute-start.14
  44.6 0.7 collective-permute-start.12
  45.3 2.1 %collective-permute-start.8 = (bf16[144,1152]{1,0:T(8,128)(2,1)S(1)}, bf16[144,1152]{1,0:T(8,128)(2,1)S(1)}, u32[]{:S(2)}, u32[]{:S(2)}) collective-permute-start(bf16[144,1152]{1,0:T(8,128)(2,1)S(1)} %collective-permute-done.5.rest_2_), channel_id=1, source_target_pairs={{0,1},{1,0},{2,3},{3,2},{4,5},{5,4},{6,7},{7,6},{8,9},{9,8},{10,11... | collective-permute-start | bytes 995336 | tf_op jit(solution)/shard_map/ppermute | solution.py:36
  47.5 2.7 %collective-permute-start.9 = (bf16[288,1152]{1,0:T(8,128)(2,1)S(1)}, bf16[288,1152]{1,0:T(8,128)(2,1)S(1)}, u32[]{:S(2)}, u32[]{:S(2)}) collective-permute-start(bf16[288,1152]{1,0:T(8,128)(2,1)S(1)} %collective-permute-done.3.rest_1_), channel_id=1, source_target_pairs={{0,8},{1,9},{2,10},{3,11},{4,12},{5,13},{6,14},{7,15},{8,0},{9,1},... | collective-permute-start | bytes 1990664 | tf_op jit(solution)/shard_map/ppermute | solution.py:36
  50.1 3.4 %collective-permute-done.8.rest_3_ = bf16[144,1152]{1,0:T(8,128)(2,1)S(1)} collective-permute-done((bf16[144,1152]{1,0:T(8,128)(2,1)S(1)}, bf16[144,1152]{1,0:T(8,128)(2,1)S(1)}, u32[]{:S(2)}, u32[]{:S(2)}) %collective-permute-start.8) | collective-permute-done | bytes 331808 | tf_op jit(solution)/shard_map/ppermute | solution.py:36
  53.6 2.3 %collective-permute-start.10 = (bf16[144,1152]{1,0:T(8,128)(2,1)S(1)}, bf16[144,1152]{1,0:T(8,128)(2,1)S(1)}, u32[]{:S(2)}, u32[]{:S(2)}) collective-permute-start(bf16[144,1152]{1,0:T(8,128)(2,1)S(1)} %collective-permute-done.5.rest_2_), channel_id=1, source_target_pairs={{0,8},{1,9},{2,10},{3,11},{4,12},{5,13},{6,14},{7,15},{8,0},{9,1},... | collective-permute-start | bytes 995336 | tf_op jit(solution)/shard_map/ppermute | solution.py:36
  55.9 1.3 %collective-permute-done.10.rest_6_ = bf16[144,1152]{1,0:T(8,128)(2,1)S(1)} collective-permute-done((bf16[144,1152]{1,0:T(8,128)(2,1)S(1)}, bf16[144,1152]{1,0:T(8,128)(2,1)S(1)}, u32[]{:S(2)}, u32[]{:S(2)}) %collective-permute-start.10) | collective-permute-done | bytes 331808 | tf_op jit(solution)/shard_map/ppermute | solution.py:36
  57.2 0.0 collective-permute-done.9.rest_5_
  57.2 0.0 collective-permute-done.11.rest_11_.even_flip_ref
  57.2 0.4 collective-permute-start.13
  57.6 0.0 collective-permute-done.12.odd_other_ref
  57.6 1.3 %collective-permute-done.13.rest_7_ = bf16[144,1152]{1,0:T(8,128)(2,1)S(1)} collective-permute-done((bf16[144,1152]{1,0:T(8,128)(2,1)S(1)}, bf16[144,1152]{1,0:T(8,128)(2,1)S(1)}, u32[]{:S(2)}, u32[]{:S(2)}) %collective-permute-start.13) | collective-permute-done | bytes 331808 | tf_op jit(solution)/shard_map/ppermute | solution.py:36
  58.8 1.3 %collective-permute-start.15 = (bf16[512,1024]{1,0:T(8,128)(2,1)S(1)}, bf16[512,1024]{1,0:T(8,128)(2,1)S(1)}, u32[]{:S(2)}, u32[]{:S(2)}) collective-permute-start(bf16[512,1024]{1,0:T(8,128)(2,1)S(1)} %collective-permute-done.6.odd_ref), channel_id=1, source_target_pairs={{8,0},{9,1},{10,2},{11,3},{12,4},{13,5},{14,6},{15,7},{24,16},{25,... | collective-permute-start | bytes 3145736 | tf_op jit(solution)/shard_map/ppermute | solution.py:36
  60.1 1.3 %collective-permute-start.16 = (bf16[512,1024]{1,0:T(8,128)(2,1)S(1)}, bf16[512,1024]{1,0:T(8,128)(2,1)S(1)}, u32[]{:S(2)}, u32[]{:S(2)}) collective-permute-start(bf16[512,1024]{1,0:T(8,128)(2,1)S(1)} %collective-permute-done.12.odd_other_ref), channel_id=1, source_target_pairs={{8,0},{9,1},{10,2},{11,3},{12,4},{13,5},{14,6},{15,7},{24,16},{25,... | collective-permute-start | bytes 3145736 | tf_op jit(solution)/shard_map/ppermute | solution.py:36
  61.4 0.0 collective-permute-done.14.rest_9_.flip_ref
  61.4 0.0 copy-done
  61.4 0.0 copy-done.2
  61.5 11.5 %shard_map.92 = (bf16[8,256,1024]{2,1,0:T(8,128)(2,1)S(1)}, bf16[16,128,256]{2,1,0:T(8,128)(2,1)S(1)}, bf16[8,112,256]{2,1,0:T(8,128)(2,1)S(1)}, s32[8,128]{1,0:...) custom-call(bf16[4,256,1024]{2,1,0:T(8,128)(2,1)S(1)} %copy-done, ...), custom_call_target="tpu_custom_call" | custom-call | flops 4294967296 | bytes 16777216 | tf_op jit(solution)/shard_map/pallas_call | solution.py:474
  73.0 0.0 collective-permute-done.15.odd_flip_ref
  73.0 0.0 collective-permute-done.16.odd_other_flip_ref
  73.0 21.5 %shard_map.93 = f32[8,1,384]{2,1,0:T(1,128)} custom-call(s32[8,128]{1,0:T(8,128)S(1)} %get-tuple-element.58.cols_ref, bf16[8,256,1024]{2,1,0:T(8,128)(2,1)S(1)} %get-tuple-element.59.init_ref, bf16[16,128,256]{2,1,0:T(8,128)(2,1)S(1)} %get-tuple-element.60.spread_ref, bf16[8,112,256]{2,1,0:T(8,128)(2,1)S(1)} %get-tuple-element.61.pick_ref, ...), custom_call_target="tpu_custom_call" | custom-call | flops 12884901888 | bytes 16777216 | tf_op jit(solution)/shard_map/pallas_call | solution.py:496
  94.5 7.0 %all-to-all-start = ((f32[8,1,384]{2,1,0:T(1,128)}), f32[8,1,384]{2,1,0:T(1,128)S(1)}, u32[]{:S(2)}, u32[]{:S(2)}) async-start(f32[8,1,384]{2,1,0:T(1,128)} %shard_map.93), calls=%async_computation | async-start | bytes 24576 | tf_op jit(solution)/shard_map/all_to_all | solution.py:517
  101.5 5.6 %all-to-all-done = f32[8,1,384]{2,1,0:T(1,128)S(1)} async-done(((f32[8,1,384]{2,1,0:T(1,128)}), f32[8,1,384]{2,1,0:T(1,128)S(1)}, u32[]{:S(2)}, u32[]{:S(2)}) %all-to-all-start) | async-done | bytes 12320 | tf_op jit(solution)/shard_map/all_to_all | solution.py:517
  107.1 0.6 reshape.7
  (9 shorter events, 0.2 us)
Async XLA Ops:
  0.0 2.9 %copy-start.1 = (bf16[1,1024,1024]{2,1,0:T(8,128)(2,1)S(1)}, bf16[1,1024,1024]{2,1,0:T(8,128)(2,1)}, u32[]{:S(2)}) copy-start(bf16[1,1024,1024]{2,1,0:T(8,128)(2,1)} %param.10) | copy-start | bytes 6291460
  2.9 40.2 %collective-permute-start.7 = (bf16[1024,1024]{1,0:T(8,128)(2,1)S(1)}, bf16[1024,1024]{1,0:T(8,128)(2,1)}, u32[]{:S(2)}, u32[]{:S(2)}) collective-permute-start(bf16[1024,1024]{1,0:T(8,128)(2,1)S(1)} %bitcast.9), channel_id=1, source_target_pairs={{0,16},{1,17},{2,18},{3,19},{4,20},{5,21},{6,22},{7,23},{16,0},{17... | collective-permute-start | bytes 6291464 | tf_op jit(solution)/shard_map/ppermute | solution.py:36
  7.8 16.4 %collective-permute-start.1 = (bf16[144,1152]{1,0:T(8,128)(2,1)}, bf16[144,1152]{1,0:T(8,128)(2,1)S(1)}, u32[]{:S(2)}, u32[]{:S(2)}) collective-permute-start(bf16[144,1152]{1,0:T(8,128)(2,1)} %get-tuple-element.40), channel_id=1, source_target_pairs={{0,4},{1,5},{2,6},{3,7},{4,0},{5,1},{6,2},{7,3},{8,12},{9,13},{10,... | collective-permute-start | bytes 995336 | tf_op jit(solution)/shard_map/ppermute | solution.py:36
  10.4 13.9 %collective-permute-start.2 = (bf16[144,1152]{1,0:T(8,128)(2,1)}, bf16[144,1152]{1,0:T(8,128)(2,1)S(1)}, u32[]{:S(2)}, u32[]{:S(2)}) collective-permute-start(bf16[144,1152]{1,0:T(8,128)(2,1)} %get-tuple-element.39.mine_ref), channel_id=1, source_target_pairs={{0,2},{1,3},{2,0},{3,1},{4,6},{5,7},{6,4},{7,5},{8,10},{9,11},{10,... | collective-permute-start | bytes 995336 | tf_op jit(solution)/shard_map/ppermute | solution.py:36
  12.0 12.4 %collective-permute-start = (bf16[144,1152]{1,0:T(8,128)(2,1)}, bf16[144,1152]{1,0:T(8,128)(2,1)S(1)}, u32[]{:S(2)}, u32[]{:S(2)}) collective-permute-start(bf16[144,1152]{1,0:T(8,128)(2,1)} %get-tuple-element.39.mine_ref), channel_id=1, source_target_pairs={{0,1},{1,0},{2,3},{3,2},{4,5},{5,4},{6,7},{7,6},{8,9},{9,8},{10,11... | collective-permute-start | bytes 995336 | tf_op jit(solution)/shard_map/ppermute | solution.py:36
  13.6 47.8 %copy-start = (bf16[4,256,1024]{2,1,0:T(8,128)(2,1)S(1)}, bf16[4,256,1024]{2,1,0:T(8,128)(2,1)}, u32[]{:S(2)}) copy-start(bf16[4,256,1024]{2,1,0:T(8,128)(2,1)} %init_feats.1) | copy-start | bytes 6291460
  13.6 47.8 %copy-start.2 = (bf16[4,2,128,128]{3,2,1,0:T(8,128)(2,1)S(1)}, bf16[4,2,128,128]{3,2,1,0:T(8,128)(2,1)}, u32[]{:S(2)}) copy-start(bf16[4,2,128,128]{3,2,1,0:T(8,128)(2,1)} %tile_vals.1) | copy-start | bytes 786436
  13.6 47.8 %copy-start.3 = (bf16[144,1152]{1,0:T(8,128)(2,1)S(1)}, bf16[144,1152]{1,0:T(8,128)(2,1)}, u32[]{:S(2)}) copy-start(bf16[144,1152]{1,0:T(8,128)(2,1)} %get-tuple-element.39.mine_ref) | copy-start | bytes 995332
  13.6 28.4 %collective-permute-start.6 = (bf16[512,1024]{1,0:T(8,128)(2,1)S(1)}, bf16[512,1024]{1,0:T(8,128)(2,1)S(1)}, u32[]{:S(2)}, u32[]{:S(2)}) collective-permute-start(bf16[512,1024]{1,0:T(8,128)(2,1)S(1)} %constant_dynamic-slice_fusion), channel_id=1, source_target_pairs={{8,24},{9,25},{10,26},{11,27},{12,28},{13,29},{14,30},{15,31},{24,... | collective-permute-start | bytes 3145736 | tf_op jit(solution)/shard_map/ppermute | solution.py:36
  24.5 17.5 %collective-permute-start.4 = (bf16[432,1152]{1,0:T(8,128)(2,1)S(1)}, bf16[432,1152]{1,0:T(8,128)(2,1)S(1)}, u32[]{:S(2)}, u32[]{:S(2)}) collective-permute-start(bf16[432,1152]{1,0:T(8,128)(2,1)S(1)} %constant_dynamic-update-slice_fusion.rest_0_), channel_id=1, source_target_pairs={{0,8},{1,9},{2,10},{3,11},{4,12},{5,13},{6,14},{7,15},{8,0},{9,1},... | collective-permute-start | bytes 2985992 | tf_op jit(solution)/shard_map/ppermute | solution.py:36
  24.6 17.4 %collective-permute-start.3 = (bf16[288,1152]{1,0:T(8,128)(2,1)S(1)}, bf16[288,1152]{1,0:T(8,128)(2,1)S(1)}, u32[]{:S(2)}, u32[]{:S(2)}) collective-permute-start(bf16[288,1152]{1,0:T(8,128)(2,1)S(1)} %pad_maximum_fusion), channel_id=1, source_target_pairs={{0,1},{1,0},{2,3},{3,2},{4,5},{5,4},{6,7},{7,6},{8,9},{9,8},{10,11... | collective-permute-start | bytes 1990664 | tf_op jit(solution)/shard_map/ppermute | solution.py:36
  26.3 9.9 %collective-permute-start.5 = (bf16[144,1152]{1,0:T(8,128)(2,1)S(1)}, bf16[144,1152]{1,0:T(8,128)(2,1)S(1)}, u32[]{:S(2)}, u32[]{:S(2)}) collective-permute-start(bf16[144,1152]{1,0:T(8,128)(2,1)S(1)} %collective-permute-done.1), channel_id=1, source_target_pairs={{0,2},{1,3},{2,0},{3,1},{4,6},{5,7},{6,4},{7,5},{8,10},{9,11},{10,... | collective-permute-start | bytes 995336 | tf_op jit(solution)/shard_map/ppermute | solution.py:36
  43.1 14.1 %collective-permute-start.11 = (bf16[1024,1024]{1,0:T(8,128)(2,1)}, bf16[1024,1024]{1,0:T(8,128)(2,1)S(1)}, u32[]{:S(2)}, u32[]{:S(2)}) collective-permute-start(bf16[1024,1024]{1,0:T(8,128)(2,1)} %collective-permute-done.7.rest_10_.even_ref), channel_id=1, source_target_pairs={{0,8},{1,9},{2,10},{3,11},{4,12},{5,13},{6,14},{7,15},{16,24},{17,... | collective-permute-start | bytes 6291464 | tf_op jit(solution)/shard_map/ppermute | solution.py:36
  44.5 16.9 %collective-permute-start.14 = (bf16[1024,1024]{1,0:T(8,128)(2,1)S(1)}, bf16[1024,1024]{1,0:T(8,128)(2,1)S(1)}, u32[]{:S(2)}, u32[]{:S(2)}) collective-permute-start(bf16[1024,1024]{1,0:T(8,128)(2,1)S(1)} %bitcast.11), channel_id=1, source_target_pairs={{0,8},{1,9},{2,10},{3,11},{4,12},{5,13},{6,14},{7,15},{8,0},{9,1},... | collective-permute-start | bytes 6291464 | tf_op jit(solution)/shard_map/ppermute | solution.py:36
  44.6 13.0 %collective-permute-start.12 = (bf16[512,1024]{1,0:T(8,128)(2,1)S(1)}, bf16[512,1024]{1,0:T(8,128)(2,1)S(1)}, u32[]{:S(2)}, u32[]{:S(2)}) collective-permute-start(bf16[512,1024]{1,0:T(8,128)(2,1)S(1)} %collective-permute-done.6.odd_ref), channel_id=1, source_target_pairs={{8,10},{9,11},{10,8},{11,9},{12,14},{13,15},{14,12},{15,13},{24,26... | collective-permute-start | bytes 3145736 | tf_op jit(solution)/shard_map/ppermute | solution.py:36
  45.3 8.2 %collective-permute-start.8 = (bf16[144,1152]{1,0:T(8,128)(2,1)S(1)}, bf16[144,1152]{1,0:T(8,128)(2,1)S(1)}, u32[]{:S(2)}, u32[]{:S(2)}) collective-permute-start(bf16[144,1152]{1,0:T(8,128)(2,1)S(1)} %collective-permute-done.5.rest_2_), channel_id=1, source_target_pairs={{0,1},{1,0},{2,3},{3,2},{4,5},{5,4},{6,7},{7,6},{8,9},{9,8},{10,11... | collective-permute-start | bytes 995336 | tf_op jit(solution)/shard_map/ppermute | solution.py:36
  47.5 9.7 %collective-permute-start.9 = (bf16[288,1152]{1,0:T(8,128)(2,1)S(1)}, bf16[288,1152]{1,0:T(8,128)(2,1)S(1)}, u32[]{:S(2)}, u32[]{:S(2)}) collective-permute-start(bf16[288,1152]{1,0:T(8,128)(2,1)S(1)} %collective-permute-done.3.rest_1_), channel_id=1, source_target_pairs={{0,8},{1,9},{2,10},{3,11},{4,12},{5,13},{6,14},{7,15},{8,0},{9,1},... | collective-permute-start | bytes 1990664 | tf_op jit(solution)/shard_map/ppermute | solution.py:36
  53.6 3.6 %collective-permute-start.10 = (bf16[144,1152]{1,0:T(8,128)(2,1)S(1)}, bf16[144,1152]{1,0:T(8,128)(2,1)S(1)}, u32[]{:S(2)}, u32[]{:S(2)}) collective-permute-start(bf16[144,1152]{1,0:T(8,128)(2,1)S(1)} %collective-permute-done.5.rest_2_), channel_id=1, source_target_pairs={{0,8},{1,9},{2,10},{3,11},{4,12},{5,13},{6,14},{7,15},{8,0},{9,1},... | collective-permute-start | bytes 995336 | tf_op jit(solution)/shard_map/ppermute | solution.py:36
  57.2 1.6 %collective-permute-start.13 = (bf16[144,1152]{1,0:T(8,128)(2,1)S(1)}, bf16[144,1152]{1,0:T(8,128)(2,1)S(1)}, u32[]{:S(2)}, u32[]{:S(2)}) collective-permute-start(bf16[144,1152]{1,0:T(8,128)(2,1)S(1)} %collective-permute-done.8.rest_3_), channel_id=1, source_target_pairs={{0,8},{1,9},{2,10},{3,11},{4,12},{5,13},{6,14},{7,15},{8,0},{9,1},... | collective-permute-start | bytes 995336 | tf_op jit(solution)/shard_map/ppermute | solution.py:36
  58.8 14.1 %collective-permute-start.15 = (bf16[512,1024]{1,0:T(8,128)(2,1)S(1)}, bf16[512,1024]{1,0:T(8,128)(2,1)S(1)}, u32[]{:S(2)}, u32[]{:S(2)}) collective-permute-start(bf16[512,1024]{1,0:T(8,128)(2,1)S(1)} %collective-permute-done.6.odd_ref), channel_id=1, source_target_pairs={{8,0},{9,1},{10,2},{11,3},{12,4},{13,5},{14,6},{15,7},{24,16},{25,... | collective-permute-start | bytes 3145736 | tf_op jit(solution)/shard_map/ppermute | solution.py:36
  60.1 12.9 %collective-permute-start.16 = (bf16[512,1024]{1,0:T(8,128)(2,1)S(1)}, bf16[512,1024]{1,0:T(8,128)(2,1)S(1)}, u32[]{:S(2)}, u32[]{:S(2)}) collective-permute-start(bf16[512,1024]{1,0:T(8,128)(2,1)S(1)} %collective-permute-done.12.odd_other_ref), channel_id=1, source_target_pairs={{8,0},{9,1},{10,2},{11,3},{12,4},{13,5},{14,6},{15,7},{24,16},{25,... | collective-permute-start | bytes 3145736 | tf_op jit(solution)/shard_map/ppermute | solution.py:36
  94.5 12.6 %all-to-all-start = ((f32[8,1,384]{2,1,0:T(1,128)}), f32[8,1,384]{2,1,0:T(1,128)S(1)}, u32[]{:S(2)}, u32[]{:S(2)}) async-start(f32[8,1,384]{2,1,0:T(1,128)} %shard_map.93), calls=%async_computation | async-start | bytes 24576 | tf_op jit(solution)/shard_map/all_to_all | solution.py:517

commit v5 on v4

--- a/solution.py
+++ b/solution.py
@@ -237,7 +237,7 @@
                 )
             )
             at += 2
-    for copy in tables:
+    for copy in tables + copies:
         copy.wait()
 
     owner = core * 4 + zl * 2 + y
@@ -288,15 +288,16 @@
                 t * tile : (t + 1) * tile
             ]
 
+    def begin(block, carry):
+        publish(block, init_ref[block], pick_ref, boundary0, keys)
+        return carry
+
+    lax.fori_loop(0, blocks, begin, 0, unroll=4)
     to_scalar.wait()
-    for copy in copies:
-        copy.wait()
-    for block in range(blocks):
-        publish(block, init_ref[block], pick_ref, boundary0, keys)
+    pltpu.make_async_copy(weights[0], weight, weight_sems.at[0]).wait()
     run_layer(
         spread_ref, cols_ref, init_ref, pick_ref, init_ref, boundary0, weight, mixing_of(0),
-        hidden, boundary, anchors,
-        pltpu.make_async_copy(weights[0], weight, weight_sems.at[0]).wait,
+        hidden, boundary, anchors, lambda: None,
     )
     loss_ref[...] = score(keys, anchors, live_ref)
 

time: 108 us -> 108 us (level)
  transfers between devices with their start and end apart: 18 -> 18, of which waited for: 9 -> 9; matrix products, arithmetic and copies ran while one was open for 0% -> 0% of each run, Pallas kernels for 11% -> 10%
where the time goes in v5:
time: 108 us; the launch traced here: 107 us
  waiting for transfers between devices  36.9 us (34%)
  Pallas kernels  35.4 us (33%)
  starting transfers between devices  33.9 us (31%)
    ppermute x17, waiting for transfers between devices, exchange(): return lax.ppermute(block, AXES, pairs)  31.3 us
    ppermute x17, starting transfers between devices, exchange(): return lax.ppermute(block, AXES, pairs)  26.9 us
    pallas_call x1, Pallas kernels, local(): pl.pallas_call(rest_kernel, out_shape=shape((2 * SEGMENTS, 1, total), f32...  21.5 us
    pallas_call x1, Pallas kernels, local(): pl.pallas_call(first_kernel, out_shape=keep, in_specs=[HBM] * 15, out_spe...  11 us
    all_to_all x1, starting transfers between devices, local(): lax.all_to_all(losses, ('x', 'core', 'zh'), split_axis=0, concat_axis=0,...  6.99 us
    all_to_all x1, waiting for transfers between devices, local(): lax.all_to_all(losses, ('x', 'core', 'zh'), split_axis=0, concat_axis=0,...  5.6 us
    pallas_call x1, Pallas kernels, local(): pl.pallas_call(pack_kernel, out_shape=(packed, packed), in_specs=[HBM, HB...  2.9 us
  transfers between devices with their start and end apart: 18, of which 9 were waited for; matrix products, arithmetic and copies ran while one was open for 0% of the time, Pallas kernels for 10%

profile of v5, /device:TPU:0, one launch (start us, length us, event | category | flops | bytes accessed | tf_op | source)
XLA Modules:
  0.0 107.3 jit_solution(5187467870448497676)
XLA Ops:
  0.0 2.9 %shard_map.91 = (bf16[144,1152]{1,0:T(8,128)(2,1)}, bf16[144,1152]{1,0:T(8,128)(2,1)}) custom-call(bf16[4,256,1024]{2,1,0:T(8,128)(2,1)} %init_feats.1, bf16[4,2,128,128]{3,2,1,0:T(8,128)(2,1)} %tile_vals.1, s32[4,8,8]{2,1,0:T(8,128)} %send_ref.1, s32[4,8]{1,0:T(4,128)} %count_ref.1, s32[4,8,8]{2,1,0:T(8,128)} %recv_ref.1, bf16[4,8,8]{2,1,0:T(8,128)(2,1)} %weight_ref.1, ...), custom_call_target="tpu_custom_call" | custom-call | tf_op jit(solution)/shard_map/pallas_call | solution.py:426
  2.9 0.0 copy-done.1
  2.9 4.8 %collective-permute-start.7 = (bf16[1024,1024]{1,0:T(8,128)(2,1)S(1)}, bf16[1024,1024]{1,0:T(8,128)(2,1)}, u32[]{:S(2)}, u32[]{:S(2)}) collective-permute-start(bf16[1024,1024]{1,0:T(8,128)(2,1)S(1)} %bitcast.9), channel_id=1, source_target_pairs={{0,16},{1,17},{2,18},{3,19},{4,20},{5,21},{6,22},{7,23},{16,0},{17... | collective-permute-start | bytes 6291464 | tf_op jit(solution)/shard_map/ppermute | solution.py:36
  7.8 2.7 %collective-permute-start.1 = (bf16[144,1152]{1,0:T(8,128)(2,1)}, bf16[144,1152]{1,0:T(8,128)(2,1)S(1)}, u32[]{:S(2)}, u32[]{:S(2)}) collective-permute-start(bf16[144,1152]{1,0:T(8,128)(2,1)} %get-tuple-element.40), channel_id=1, source_target_pairs={{0,4},{1,5},{2,6},{3,7},{4,0},{5,1},{6,2},{7,3},{8,12},{9,13},{10,... | collective-permute-start | bytes 995336 | tf_op jit(solution)/shard_map/ppermute | solution.py:36
  10.4 1.6 %collective-permute-start.2 = (bf16[144,1152]{1,0:T(8,128)(2,1)}, bf16[144,1152]{1,0:T(8,128)(2,1)S(1)}, u32[]{:S(2)}, u32[]{:S(2)}) collective-permute-start(bf16[144,1152]{1,0:T(8,128)(2,1)} %get-tuple-element.39.mine_ref), channel_id=1, source_target_pairs={{0,2},{1,3},{2,0},{3,1},{4,6},{5,7},{6,4},{7,5},{8,10},{9,11},{10,... | collective-permute-start | bytes 995336 | tf_op jit(solution)/shard_map/ppermute | solution.py:36
  12.0 1.5 %collective-permute-start = (bf16[144,1152]{1,0:T(8,128)(2,1)}, bf16[144,1152]{1,0:T(8,128)(2,1)S(1)}, u32[]{:S(2)}, u32[]{:S(2)}) collective-permute-start(bf16[144,1152]{1,0:T(8,128)(2,1)} %get-tuple-element.39.mine_ref), channel_id=1, source_target_pairs={{0,1},{1,0},{2,3},{3,2},{4,5},{5,4},{6,7},{7,6},{8,9},{9,8},{10,11... | collective-permute-start | bytes 995336 | tf_op jit(solution)/shard_map/ppermute | solution.py:36
  13.5 0.1 constant_dynamic-slice_fusion
  13.6 0.0 copy-start
  13.6 0.0 copy-start.2
  13.6 0.0 copy-start.3
  13.6 0.9 collective-permute-start.6
  14.5 9.7 %collective-permute-done.1 = bf16[144,1152]{1,0:T(8,128)(2,1)S(1)} collective-permute-done((bf16[144,1152]{1,0:T(8,128)(2,1)}, bf16[144,1152]{1,0:T(8,128)(2,1)S(1)}, u32[]{:S(2)}, u32[]{:S(2)}) %collective-permute-start.1) | collective-permute-done | bytes 331808 | tf_op jit(solution)/shard_map/ppermute | solution.py:36
  24.2 0.2 collective-permute-done.2
  24.4 0.0 collective-permute-done
  24.5 0.1 collective-permute-start.4
  24.6 0.1 pad_maximum_fusion
  24.6 1.6 %collective-permute-start.3 = (bf16[288,1152]{1,0:T(8,128)(2,1)S(1)}, bf16[288,1152]{1,0:T(8,128)(2,1)S(1)}, u32[]{:S(2)}, u32[]{:S(2)}) collective-permute-start(bf16[288,1152]{1,0:T(8,128)(2,1)S(1)} %pad_maximum_fusion), channel_id=1, source_target_pairs={{0,1},{1,0},{2,3},{3,2},{4,5},{5,4},{6,7},{7,6},{8,9},{9,8},{10,11... | collective-permute-start | bytes 1990664 | tf_op jit(solution)/shard_map/ppermute | solution.py:36
  26.3 1.4 %collective-permute-start.5 = (bf16[144,1152]{1,0:T(8,128)(2,1)S(1)}, bf16[144,1152]{1,0:T(8,128)(2,1)S(1)}, u32[]{:S(2)}, u32[]{:S(2)}) collective-permute-start(bf16[144,1152]{1,0:T(8,128)(2,1)S(1)} %collective-permute-done.1), channel_id=1, source_target_pairs={{0,2},{1,3},{2,0},{3,1},{4,6},{5,7},{6,4},{7,5},{8,10},{9,11},{10,... | collective-permute-start | bytes 995336 | tf_op jit(solution)/shard_map/ppermute | solution.py:36
  27.7 8.5 %collective-permute-done.5.rest_2_ = bf16[144,1152]{1,0:T(8,128)(2,1)S(1)} collective-permute-done((bf16[144,1152]{1,0:T(8,128)(2,1)S(1)}, bf16[144,1152]{1,0:T(8,128)(2,1)S(1)}, u32[]{:S(2)}, u32[]{:S(2)}) %collective-permute-start.5) | collective-permute-done | bytes 331808 | tf_op jit(solution)/shard_map/ppermute | solution.py:36
  36.2 5.8 %collective-permute-done.3.rest_1_ = bf16[288,1152]{1,0:T(8,128)(2,1)S(1)} collective-permute-done((bf16[288,1152]{1,0:T(8,128)(2,1)S(1)}, bf16[288,1152]{1,0:T(8,128)(2,1)S(1)}, u32[]{:S(2)}, u32[]{:S(2)}) %collective-permute-start.3) | collective-permute-done | bytes 663584 | tf_op jit(solution)/shard_map/ppermute | solution.py:36
  42.0 0.0 collective-permute-done.6.odd_ref
  42.0 0.0 collective-permute-done.4.rest_4_
  42.0 1.1 %collective-permute-done.7.rest_10_.even_ref = bf16[1024,1024]{1,0:T(8,128)(2,1)} collective-permute-done((bf16[1024,1024]{1,0:T(8,128)(2,1)S(1)}, bf16[1024,1024]{1,0:T(8,128)(2,1)}, u32[]{:S(2)}, u32[]{:S(2)}) %collective-permute-start.7) | collective-permute-done | bytes 2097184 | tf_op jit(solution)/shard_map/ppermute | solution.py:36
  43.1 1.4 %collective-permute-start.11 = (bf16[1024,1024]{1,0:T(8,128)(2,1)}, bf16[1024,1024]{1,0:T(8,128)(2,1)S(1)}, u32[]{:S(2)}, u32[]{:S(2)}) collective-permute-start(bf16[1024,1024]{1,0:T(8,128)(2,1)} %collective-permute-done.7.rest_10_.even_ref), channel_id=1, source_target_pairs={{0,8},{1,9},{2,10},{3,11},{4,12},{5,13},{6,14},{7,15},{16,24},{17,... | collective-permute-start | bytes 6291464 | tf_op jit(solution)/shard_map/ppermute | solution.py:36
  44.5 0.1 collective-permute-start.14
  44.6 0.7 collective-permute-start.12
  45.3 2.1 %collective-permute-start.8 = (bf16[144,1152]{1,0:T(8,128)(2,1)S(1)}, bf16[144,1152]{1,0:T(8,128)(2,1)S(1)}, u32[]{:S(2)}, u32[]{:S(2)}) collective-permute-start(bf16[144,1152]{1,0:T(8,128)(2,1)S(1)} %collective-permute-done.5.rest_2_), channel_id=1, source_target_pairs={{0,1},{1,0},{2,3},{3,2},{4,5},{5,4},{6,7},{7,6},{8,9},{9,8},{10,11... | collective-permute-start | bytes 995336 | tf_op jit(solution)/shard_map/ppermute | solution.py:36
  47.5 2.7 %collective-permute-start.9 = (bf16[288,1152]{1,0:T(8,128)(2,1)S(1)}, bf16[288,1152]{1,0:T(8,128)(2,1)S(1)}, u32[]{:S(2)}, u32[]{:S(2)}) collective-permute-start(bf16[288,1152]{1,0:T(8,128)(2,1)S(1)} %collective-permute-done.3.rest_1_), channel_id=1, source_target_pairs={{0,8},{1,9},{2,10},{3,11},{4,12},{5,13},{6,14},{7,15},{8,0},{9,1},... | collective-permute-start | bytes 1990664 | tf_op jit(solution)/shard_map/ppermute | solution.py:36
  50.1 3.4 %collective-permute-done.8.rest_3_ = bf16[144,1152]{1,0:T(8,128)(2,1)S(1)} collective-permute-done((bf16[144,1152]{1,0:T(8,128)(2,1)S(1)}, bf16[144,1152]{1,0:T(8,128)(2,1)S(1)}, u32[]{:S(2)}, u32[]{:S(2)}) %collective-permute-start.8) | collective-permute-done | bytes 331808 | tf_op jit(solution)/shard_map/ppermute | solution.py:36
  53.6 2.3 %collective-permute-start.10 = (bf16[144,1152]{1,0:T(8,128)(2,1)S(1)}, bf16[144,1152]{1,0:T(8,128)(2,1)S(1)}, u32[]{:S(2)}, u32[]{:S(2)}) collective-permute-start(bf16[144,1152]{1,0:T(8,128)(2,1)S(1)} %collective-permute-done.5.rest_2_), channel_id=1, source_target_pairs={{0,8},{1,9},{2,10},{3,11},{4,12},{5,13},{6,14},{7,15},{8,0},{9,1},... | collective-permute-start | bytes 995336 | tf_op jit(solution)/shard_map/ppermute | solution.py:36
  55.9 1.3 %collective-permute-done.10.rest_6_ = bf16[144,1152]{1,0:T(8,128)(2,1)S(1)} collective-permute-done((bf16[144,1152]{1,0:T(8,128)(2,1)S(1)}, bf16[144,1152]{1,0:T(8,128)(2,1)S(1)}, u32[]{:S(2)}, u32[]{:S(2)}) %collective-permute-start.10) | collective-permute-done | bytes 331808 | tf_op jit(solution)/shard_map/ppermute | solution.py:36
  57.2 0.0 collective-permute-done.9.rest_5_
  57.2 0.0 collective-permute-done.11.rest_11_.even_flip_ref
  57.2 0.4 collective-permute-start.13
  57.6 0.0 collective-permute-done.12.odd_other_ref
  57.6 1.3 %collective-permute-done.13.rest_7_ = bf16[144,1152]{1,0:T(8,128)(2,1)S(1)} collective-permute-done((bf16[144,1152]{1,0:T(8,128)(2,1)S(1)}, bf16[144,1152]{1,0:T(8,128)(2,1)S(1)}, u32[]{:S(2)}, u32[]{:S(2)}) %collective-permute-start.13) | collective-permute-done | bytes 331808 | tf_op jit(solution)/shard_map/ppermute | solution.py:36
  58.8 1.3 %collective-permute-start.15 = (bf16[512,1024]{1,0:T(8,128)(2,1)S(1)}, bf16[512,1024]{1,0:T(8,128)(2,1)S(1)}, u32[]{:S(2)}, u32[]{:S(2)}) collective-permute-start(bf16[512,1024]{1,0:T(8,128)(2,1)S(1)} %collective-permute-done.6.odd_ref), channel_id=1, source_target_pairs={{8,0},{9,1},{10,2},{11,3},{12,4},{13,5},{14,6},{15,7},{24,16},{25,... | collective-permute-start | bytes 3145736 | tf_op jit(solution)/shard_map/ppermute | solution.py:36
  60.1 1.3 %collective-permute-start.16 = (bf16[512,1024]{1,0:T(8,128)(2,1)S(1)}, bf16[512,1024]{1,0:T(8,128)(2,1)S(1)}, u32[]{:S(2)}, u32[]{:S(2)}) collective-permute-start(bf16[512,1024]{1,0:T(8,128)(2,1)S(1)} %collective-permute-done.12.odd_other_ref), channel_id=1, source_target_pairs={{8,0},{9,1},{10,2},{11,3},{12,4},{13,5},{14,6},{15,7},{24,16},{25,... | collective-permute-start | bytes 3145736 | tf_op jit(solution)/shard_map/ppermute | solution.py:36
  61.4 0.0 collective-permute-done.14.rest_9_.flip_ref
  61.4 0.0 copy-done
  61.4 0.0 copy-done.2
  61.5 11.0 %shard_map.92 = (bf16[8,256,1024]{2,1,0:T(8,128)(2,1)S(1)}, bf16[16,128,256]{2,1,0:T(8,128)(2,1)S(1)}, bf16[8,112,256]{2,1,0:T(8,128)(2,1)S(1)}, s32[8,128]{1,0:...) custom-call(bf16[4,256,1024]{2,1,0:T(8,128)(2,1)S(1)} %copy-done, ...), custom_call_target="tpu_custom_call" | custom-call | flops 4294967296 | bytes 16777216 | tf_op jit(solution)/shard_map/pallas_call | solution.py:475
  72.5 0.0 collective-permute-done.15.odd_flip_ref
  72.5 0.0 collective-permute-done.16.odd_other_flip_ref
  72.5 21.5 %shard_map.93 = f32[8,1,384]{2,1,0:T(1,128)} custom-call(s32[8,128]{1,0:T(8,128)S(1)} %get-tuple-element.58.cols_ref, bf16[8,256,1024]{2,1,0:T(8,128)(2,1)S(1)} %get-tuple-element.59.init_ref, bf16[16,128,256]{2,1,0:T(8,128)(2,1)S(1)} %get-tuple-element.60.spread_ref, bf16[8,112,256]{2,1,0:T(8,128)(2,1)S(1)} %get-tuple-element.61.pick_ref, ...), custom_call_target="tpu_custom_call" | custom-call | flops 12884901888 | bytes 16777216 | tf_op jit(solution)/shard_map/pallas_call | solution.py:497
  94.0 7.0 %all-to-all-start = ((f32[8,1,384]{2,1,0:T(1,128)}), f32[8,1,384]{2,1,0:T(1,128)S(1)}, u32[]{:S(2)}, u32[]{:S(2)}) async-start(f32[8,1,384]{2,1,0:T(1,128)} %shard_map.93), calls=%async_computation | async-start | bytes 24576 | tf_op jit(solution)/shard_map/all_to_all | solution.py:518
  101.0 5.6 %all-to-all-done = f32[8,1,384]{2,1,0:T(1,128)S(1)} async-done(((f32[8,1,384]{2,1,0:T(1,128)}), f32[8,1,384]{2,1,0:T(1,128)S(1)}, u32[]{:S(2)}, u32[]{:S(2)}) %all-to-all-start) | async-done | bytes 12320 | tf_op jit(solution)/shard_map/all_to_all | solution.py:518
  106.7 0.6 reshape.7
  (9 shorter events, 0.2 us)
Async XLA Ops:
  0.0 2.9 %copy-start.1 = (bf16[1,1024,1024]{2,1,0:T(8,128)(2,1)S(1)}, bf16[1,1024,1024]{2,1,0:T(8,128)(2,1)}, u32[]{:S(2)}) copy-start(bf16[1,1024,1024]{2,1,0:T(8,128)(2,1)} %param.10) | copy-start | bytes 6291460
  2.9 40.2 %collective-permute-start.7 = (bf16[1024,1024]{1,0:T(8,128)(2,1)S(1)}, bf16[1024,1024]{1,0:T(8,128)(2,1)}, u32[]{:S(2)}, u32[]{:S(2)}) collective-permute-start(bf16[1024,1024]{1,0:T(8,128)(2,1)S(1)} %bitcast.9), channel_id=1, source_target_pairs={{0,16},{1,17},{2,18},{3,19},{4,20},{5,21},{6,22},{7,23},{16,0},{17... | collective-permute-start | bytes 6291464 | tf_op jit(solution)/shard_map/ppermute | solution.py:36
  7.8 16.4 %collective-permute-start.1 = (bf16[144,1152]{1,0:T(8,128)(2,1)}, bf16[144,1152]{1,0:T(8,128)(2,1)S(1)}, u32[]{:S(2)}, u32[]{:S(2)}) collective-permute-start(bf16[144,1152]{1,0:T(8,128)(2,1)} %get-tuple-element.40), channel_id=1, source_target_pairs={{0,4},{1,5},{2,6},{3,7},{4,0},{5,1},{6,2},{7,3},{8,12},{9,13},{10,... | collective-permute-start | bytes 995336 | tf_op jit(solution)/shard_map/ppermute | solution.py:36
  10.4 13.9 %collective-permute-start.2 = (bf16[144,1152]{1,0:T(8,128)(2,1)}, bf16[144,1152]{1,0:T(8,128)(2,1)S(1)}, u32[]{:S(2)}, u32[]{:S(2)}) collective-permute-start(bf16[144,1152]{1,0:T(8,128)(2,1)} %get-tuple-element.39.mine_ref), channel_id=1, source_target_pairs={{0,2},{1,3},{2,0},{3,1},{4,6},{5,7},{6,4},{7,5},{8,10},{9,11},{10,... | collective-permute-start | bytes 995336 | tf_op jit(solution)/shard_map/ppermute | solution.py:36
  12.0 12.4 %collective-permute-start = (bf16[144,1152]{1,0:T(8,128)(2,1)}, bf16[144,1152]{1,0:T(8,128)(2,1)S(1)}, u32[]{:S(2)}, u32[]{:S(2)}) collective-permute-start(bf16[144,1152]{1,0:T(8,128)(2,1)} %get-tuple-element.39.mine_ref), channel_id=1, source_target_pairs={{0,1},{1,0},{2,3},{3,2},{4,5},{5,4},{6,7},{7,6},{8,9},{9,8},{10,11... | collective-permute-start | bytes 995336 | tf_op jit(solution)/shard_map/ppermute | solution.py:36
  13.6 47.8 %copy-start = (bf16[4,256,1024]{2,1,0:T(8,128)(2,1)S(1)}, bf16[4,256,1024]{2,1,0:T(8,128)(2,1)}, u32[]{:S(2)}) copy-start(bf16[4,256,1024]{2,1,0:T(8,128)(2,1)} %init_feats.1) | copy-start | bytes 6291460
  13.6 47.8 %copy-start.2 = (bf16[4,2,128,128]{3,2,1,0:T(8,128)(2,1)S(1)}, bf16[4,2,128,128]{3,2,1,0:T(8,128)(2,1)}, u32[]{:S(2)}) copy-start(bf16[4,2,128,128]{3,2,1,0:T(8,128)(2,1)} %tile_vals.1) | copy-start | bytes 786436
  13.6 47.8 %copy-start.3 = (bf16[144,1152]{1,0:T(8,128)(2,1)S(1)}, bf16[144,1152]{1,0:T(8,128)(2,1)}, u32[]{:S(2)}) copy-start(bf16[144,1152]{1,0:T(8,128)(2,1)} %get-tuple-element.39.mine_ref) | copy-start | bytes 995332
  13.6 28.4 %collective-permute-start.6 = (bf16[512,1024]{1,0:T(8,128)(2,1)S(1)}, bf16[512,1024]{1,0:T(8,128)(2,1)S(1)}, u32[]{:S(2)}, u32[]{:S(2)}) collective-permute-start(bf16[512,1024]{1,0:T(8,128)(2,1)S(1)} %constant_dynamic-slice_fusion), channel_id=1, source_target_pairs={{8,24},{9,25},{10,26},{11,27},{12,28},{13,29},{14,30},{15,31},{24,... | collective-permute-start | bytes 3145736 | tf_op jit(solution)/shard_map/ppermute | solution.py:36
  24.5 17.5 %collective-permute-start.4 = (bf16[432,1152]{1,0:T(8,128)(2,1)S(1)}, bf16[432,1152]{1,0:T(8,128)(2,1)S(1)}, u32[]{:S(2)}, u32[]{:S(2)}) collective-permute-start(bf16[432,1152]{1,0:T(8,128)(2,1)S(1)} %constant_dynamic-update-slice_fusion.rest_0_), channel_id=1, source_target_pairs={{0,8},{1,9},{2,10},{3,11},{4,12},{5,13},{6,14},{7,15},{8,0},{9,1},... | collective-permute-start | bytes 2985992 | tf_op jit(solution)/shard_map/ppermute | solution.py:36
  24.6 17.4 %collective-permute-start.3 = (bf16[288,1152]{1,0:T(8,128)(2,1)S(1)}, bf16[288,1152]{1,0:T(8,128)(2,1)S(1)}, u32[]{:S(2)}, u32[]{:S(2)}) collective-permute-start(bf16[288,1152]{1,0:T(8,128)(2,1)S(1)} %pad_maximum_fusion), channel_id=1, source_target_pairs={{0,1},{1,0},{2,3},{3,2},{4,5},{5,4},{6,7},{7,6},{8,9},{9,8},{10,11... | collective-permute-start | bytes 1990664 | tf_op jit(solution)/shard_map/ppermute | solution.py:36
  26.3 9.9 %collective-permute-start.5 = (bf16[144,1152]{1,0:T(8,128)(2,1)S(1)}, bf16[144,1152]{1,0:T(8,128)(2,1)S(1)}, u32[]{:S(2)}, u32[]{:S(2)}) collective-permute-start(bf16[144,1152]{1,0:T(8,128)(2,1)S(1)} %collective-permute-done.1), channel_id=1, source_target_pairs={{0,2},{1,3},{2,0},{3,1},{4,6},{5,7},{6,4},{7,5},{8,10},{9,11},{10,... | collective-permute-start | bytes 995336 | tf_op jit(solution)/shard_map/ppermute | solution.py:36
  43.1 14.1 %collective-permute-start.11 = (bf16[1024,1024]{1,0:T(8,128)(2,1)}, bf16[1024,1024]{1,0:T(8,128)(2,1)S(1)}, u32[]{:S(2)}, u32[]{:S(2)}) collective-permute-start(bf16[1024,1024]{1,0:T(8,128)(2,1)} %collective-permute-done.7.rest_10_.even_ref), channel_id=1, source_target_pairs={{0,8},{1,9},{2,10},{3,11},{4,12},{5,13},{6,14},{7,15},{16,24},{17,... | collective-permute-start | bytes 6291464 | tf_op jit(solution)/shard_map/ppermute | solution.py:36
  44.5 16.9 %collective-permute-start.14 = (bf16[1024,1024]{1,0:T(8,128)(2,1)S(1)}, bf16[1024,1024]{1,0:T(8,128)(2,1)S(1)}, u32[]{:S(2)}, u32[]{:S(2)}) collective-permute-start(bf16[1024,1024]{1,0:T(8,128)(2,1)S(1)} %bitcast.11), channel_id=1, source_target_pairs={{0,8},{1,9},{2,10},{3,11},{4,12},{5,13},{6,14},{7,15},{8,0},{9,1},... | collective-permute-start | bytes 6291464 | tf_op jit(solution)/shard_map/ppermute | solution.py:36
  44.6 13.0 %collective-permute-start.12 = (bf16[512,1024]{1,0:T(8,128)(2,1)S(1)}, bf16[512,1024]{1,0:T(8,128)(2,1)S(1)}, u32[]{:S(2)}, u32[]{:S(2)}) collective-permute-start(bf16[512,1024]{1,0:T(8,128)(2,1)S(1)} %collective-permute-done.6.odd_ref), channel_id=1, source_target_pairs={{8,10},{9,11},{10,8},{11,9},{12,14},{13,15},{14,12},{15,13},{24,26... | collective-permute-start | bytes 3145736 | tf_op jit(solution)/shard_map/ppermute | solution.py:36
  45.3 8.2 %collective-permute-start.8 = (bf16[144,1152]{1,0:T(8,128)(2,1)S(1)}, bf16[144,1152]{1,0:T(8,128)(2,1)S(1)}, u32[]{:S(2)}, u32[]{:S(2)}) collective-permute-start(bf16[144,1152]{1,0:T(8,128)(2,1)S(1)} %collective-permute-done.5.rest_2_), channel_id=1, source_target_pairs={{0,1},{1,0},{2,3},{3,2},{4,5},{5,4},{6,7},{7,6},{8,9},{9,8},{10,11... | collective-permute-start | bytes 995336 | tf_op jit(solution)/shard_map/ppermute | solution.py:36
  47.5 9.7 %collective-permute-start.9 = (bf16[288,1152]{1,0:T(8,128)(2,1)S(1)}, bf16[288,1152]{1,0:T(8,128)(2,1)S(1)}, u32[]{:S(2)}, u32[]{:S(2)}) collective-permute-start(bf16[288,1152]{1,0:T(8,128)(2,1)S(1)} %collective-permute-done.3.rest_1_), channel_id=1, source_target_pairs={{0,8},{1,9},{2,10},{3,11},{4,12},{5,13},{6,14},{7,15},{8,0},{9,1},... | collective-permute-start | bytes 1990664 | tf_op jit(solution)/shard_map/ppermute | solution.py:36
  53.6 3.6 %collective-permute-start.10 = (bf16[144,1152]{1,0:T(8,128)(2,1)S(1)}, bf16[144,1152]{1,0:T(8,128)(2,1)S(1)}, u32[]{:S(2)}, u32[]{:S(2)}) collective-permute-start(bf16[144,1152]{1,0:T(8,128)(2,1)S(1)} %collective-permute-done.5.rest_2_), channel_id=1, source_target_pairs={{0,8},{1,9},{2,10},{3,11},{4,12},{5,13},{6,14},{7,15},{8,0},{9,1},... | collective-permute-start | bytes 995336 | tf_op jit(solution)/shard_map/ppermute | solution.py:36
  57.2 1.6 %collective-permute-start.13 = (bf16[144,1152]{1,0:T(8,128)(2,1)S(1)}, bf16[144,1152]{1,0:T(8,128)(2,1)S(1)}, u32[]{:S(2)}, u32[]{:S(2)}) collective-permute-start(bf16[144,1152]{1,0:T(8,128)(2,1)S(1)} %collective-permute-done.8.rest_3_), channel_id=1, source_target_pairs={{0,8},{1,9},{2,10},{3,11},{4,12},{5,13},{6,14},{7,15},{8,0},{9,1},... | collective-permute-start | bytes 995336 | tf_op jit(solution)/shard_map/ppermute | solution.py:36
  58.8 13.7 %collective-permute-start.15 = (bf16[512,1024]{1,0:T(8,128)(2,1)S(1)}, bf16[512,1024]{1,0:T(8,128)(2,1)S(1)}, u32[]{:S(2)}, u32[]{:S(2)}) collective-permute-start(bf16[512,1024]{1,0:T(8,128)(2,1)S(1)} %collective-permute-done.6.odd_ref), channel_id=1, source_target_pairs={{8,0},{9,1},{10,2},{11,3},{12,4},{13,5},{14,6},{15,7},{24,16},{25,... | collective-permute-start | bytes 3145736 | tf_op jit(solution)/shard_map/ppermute | solution.py:36
  60.1 12.4 %collective-permute-start.16 = (bf16[512,1024]{1,0:T(8,128)(2,1)S(1)}, bf16[512,1024]{1,0:T(8,128)(2,1)S(1)}, u32[]{:S(2)}, u32[]{:S(2)}) collective-permute-start(bf16[512,1024]{1,0:T(8,128)(2,1)S(1)} %collective-permute-done.12.odd_other_ref), channel_id=1, source_target_pairs={{8,0},{9,1},{10,2},{11,3},{12,4},{13,5},{14,6},{15,7},{24,16},{25,... | collective-permute-start | bytes 3145736 | tf_op jit(solution)/shard_map/ppermute | solution.py:36
  94.0 12.6 %all-to-all-start = ((f32[8,1,384]{2,1,0:T(1,128)}), f32[8,1,384]{2,1,0:T(1,128)S(1)}, u32[]{:S(2)}, u32[]{:S(2)}) async-start(f32[8,1,384]{2,1,0:T(1,128)} %shard_map.93), calls=%async_computation | async-start | bytes 24576 | tf_op jit(solution)/shard_map/all_to_all | solution.py:518
